TPU v7x, 32 devices: a whole 2x2x4 slice. The times are simulated.
32 devices in a mesh: pole: 4 (over y, x), sub: 8 (over z, core).
Axes of the slice: x: 2, y: 2, z: 4, core: 2. Of those that a mesh axis runs over, the one named last changes fastest.
Arguments:
- start_block: float32 [32768, 128], P('sub'), may hold values from -400 to 400
- inverses: float32 [4, 64, 512, 512], P('pole', 'sub'), may hold values from -1 to 3
- iface_rows: int32 [64, 2, 128], P('sub'), may hold values from 0 to 511, as said below
- neighbors: int32 [64, 2], P('sub'), may hold values from 0 to 63, as said below
- couplings: float32 [64, 2, 128], P('sub'), may hold values from 0.25 to 1
- pole_weights: float32 [4], P('pole'), may hold values from 0.25 to 1
Outputs:
- ortho_basis: float32 [32768, 128], P(('sub', 'pole'))
Inputs may be any that keep to these rules, and one draw needn't show every extreme that they name: `iface_rows`: in each subdomain the 256 listed rows are distinct. Subdomain j lies on index j // 8 of sub. neighbors[j, 0] lies on the previous index and neighbors[j, 1] on the next one, cyclically; over the subdomains of one index, the values in column 0 are the previous index's 8 subdomains, each once, and those in column 1 the next index's, each once.
All inputs are finite; a program needn't handle non-finite values.
Results may differ from a plain program's by a relative error of at most 0.0002.
Values sent between devices are 32-bit elements; how exact they have to be, the bound alone decides.
No kernel may reach another device: no remote copies, remote signals or barrier semaphores. Data moves between devices by JAX's collectives and lax.ppermute only.
A program may use at most 64 MiB of HBM per device.

v0:
```python
import math

import jax
import jax.numpy as jnp
from jax import lax
from jax.sharding import PartitionSpec as P

precise = lax.Precision.HIGHEST


def extended_2(cells, sides, width):
    for axis, dim in sides:
        count = lax.axis_size(axis)
        head = lax.slice_in_dim(cells, 0, width, axis=dim)
        tail = lax.slice_in_dim(cells, cells.shape[dim] - width, cells.shape[dim], axis=dim)
        cells = jnp.concatenate(
            [
                lax.ppermute(tail, axis, [(i, (i + 1) % count) for i in range(count)]),
                cells,
                lax.ppermute(head, axis, [((i + 1) % count, i) for i in range(count)]),
            ],
            axis=dim,
        )
    return cells


def apply_blocks(blocks, fields):
    return jnp.einsum(
        "sij,sjv->siv", blocks, fields, precision=precise, preferred_element_type=jnp.float32
    )


def add_coupled(fields, iface_rows, neighbor_vals, couplings):

    def one_sub(field_one, rows_one, terms_one):
        field_one = field_one.at[rows_one[0]].add(terms_one[0])
        return field_one.at[rows_one[1]].add(terms_one[1])

    return jax.vmap(one_sub)(fields, iface_rows, couplings[..., None] * neighbor_vals)


def per_device(start_block, inverses, iface_rows, neighbors, couplings, pole_weights):
    blocks = inverses[0]
    sub_count = blocks.shape[0]
    block_len = blocks.shape[1]
    vec_count = start_block.shape[1]
    iface_len = iface_rows.shape[2]
    fields = start_block.reshape(sub_count, block_len, vec_count)
    first_pass = apply_blocks(blocks, fields)
    offsets = (jnp.arange(sub_count, dtype=jnp.int32) * block_len)[:, None, None]
    flat_index = (iface_rows + offsets).transpose(1, 0, 2).reshape(-1)
    outgoing = jnp.take(first_pass.reshape(sub_count * block_len, vec_count), flat_index, axis=0)
    half_rows = sub_count * iface_len
    extended = extended_2(outgoing, (("sub", 0),), half_rows)
    from_prev = extended[:half_rows].reshape(sub_count, iface_len, vec_count)
    from_next = extended[3 * half_rows :].reshape(sub_count, iface_len, vec_count)
    columns = jnp.arange(sub_count, dtype=jnp.int32)[None, :]
    choose_prev = (neighbors[:, 0:1] % sub_count == columns).astype(jnp.float32)
    choose_next = (neighbors[:, 1:2] % sub_count == columns).astype(jnp.float32)
    low_terms = jnp.einsum(
        "jk,kiv->jiv", choose_prev, from_prev, precision=precise, preferred_element_type=jnp.float32
    )
    high_terms = jnp.einsum(
        "jk,kiv->jiv", choose_next, from_next, precision=precise, preferred_element_type=jnp.float32
    )
    corrected = add_coupled(fields, iface_rows, jnp.stack([low_terms, high_terms], 1), couplings)
    weight = pole_weights[0]
    own_rows = sub_count * block_len // lax.axis_size("pole")
    result = apply_blocks(blocks, corrected).reshape(lax.axis_size("pole") * own_rows, vec_count)
    filtered = lax.psum_scatter(weight * result, "pole", scatter_dimension=0, tiled=True)
    local_gram = jnp.dot(
        filtered.T, filtered, precision=precise, preferred_element_type=jnp.float32
    )
    gram_matrix = lax.psum(local_gram, ("pole", "sub"))
    lower_factor = jnp.linalg.cholesky(gram_matrix)
    total_rows = sub_count * block_len * lax.axis_size("sub")
    solved = lax.linalg.triangular_solve(
        lower_factor, filtered, left_side=False, lower=True, transpose_a=True
    )
    return math.sqrt(total_rows) * solved


def solution(mesh):
    placed = (
        P("sub", None),
        P("pole", "sub", None, None),
        P("sub", None, None),
        P("sub", None),
        P("sub", None, None),
        P("pole"),
    )
    return jax.shard_map(
        per_device, mesh=mesh, in_specs=placed, out_specs=P(("sub", "pole"), None), check_vma=False
    )
```

profile of v0, /device:TPU:0, one launch (start us, length us, event | category | flops | bytes accessed | tf_op | source)
XLA Modules:
  0.0 268.5 jit_solution(7039576573515902275)
XLA Ops:
  6.5 1.6 copy.36
  8.3 10.6 %fusion.2 = f32[8,512,128]{2,1,0:T(8,128)} fusion(f32[8,512,128]{2,1,0:T(8,128)S(1)} %bitcast.65, f32[1,8,512,512]{3,2,1,0:T(8,128)} %param.7), kind=kOutput, calls=%fused_computation.5 | convolution fusion | flops 3221225472 | bytes 12582912 | tf_op jit(solution)/shard_map/sij,sjv->siv/dot_general | solution.py:28
  18.8 7.0 %gather_fusion = f32[2048,128]{1,0:T(8,128)S(1)} fusion(f32[4096,128]{1,0:T(8,128)} %bitcast.67, s32[2048]{0:T(1024)S(1)} %broadcast_clamp_fusion), kind=kCustom, calls=%fused_computation | custom fusion | bytes 2105344 | tf_op jit(solution)/shard_map/jit(_take)/gather | solution.py:52
  25.9 0.3 broadcast_select_fusion
  26.3 1.0 fusion.22
  27.3 4.5 %collective-permute-start.1 = (f32[1024,128]{1,0:T(8,128)}, f32[1024,128]{1,0:T(8,128)S(1)}, u32[]{:S(2)}, u32[]{:S(2)}) collective-permute-start(f32[1024,128]{1,0:T(8,128)} %get-tuple-element.14), channel_id=1, source_target_pairs={{1,0},{2,1},{3,2},{4,3},{5,4},{6,5},{7,6},{0,7},{9,8},{10,9},{11,1... | collective-permute-start | bytes 1572872 | tf_op jit(solution)/shard_map/ppermute | solution.py:20
  32.8 9.6 %collective-permute-done.1 = f32[1024,128]{1,0:T(8,128)S(1)} collective-permute-done((f32[1024,128]{1,0:T(8,128)}, f32[1024,128]{1,0:T(8,128)S(1)}, u32[]{:S(2)}, u32[]{:S(2)}) %collective-permute-start.1) | collective-permute-done | bytes 524320 | tf_op jit(solution)/shard_map/ppermute | solution.py:20
  42.4 0.7 convolution_bitcast_fusion
  43.1 2.2 collective-permute-done
  45.3 0.7 convolution_bitcast_fusion.1
  46.7 6.8 %scatter_fusion = f32[4096,128]{1,0:T(8,128)S(1)} fusion(f32[4096,128]{1,0:T(8,128)S(1)} %copy.36, s32[1024]{0:T(1024)S(1)} %get-tuple-element.18, f32[1024,128]{1,0:T(8,128)S(1)} %bitcast.70), kind=kCustom, calls=%fused_computation.1 | custom fusion | flops 131072 | bytes 1576960
  53.5 7.0 %scatter_fusion.1 = f32[4096,128]{1,0:T(8,128)S(1)} fusion(f32[4096,128]{1,0:T(8,128)S(1)} %scatter_fusion, s32[1024]{0:T(1024)S(1)} %get-tuple-element.17, f32[1024,128]{1,0:T(8,128)S(1)} %bitcast.69), kind=kCustom, calls=%fused_computation.2 | custom fusion | flops 131072 | bytes 1576960
  60.4 12.6 %multiply_bitcast_fusion = f32[8,512,128]{1,2,0:T(8,128)} fusion(f32[8,512,128]{2,1,0:T(8,128)S(1)} %bitcast.66, f32[1,8,512,512]{3,2,1,0:T(8,128)} %param.7, f32[]{:T(128)} %bitcast.64), kind=kOutput, calls=%fused_computation.7 | convolution fusion | flops 3221749760 | bytes 12582916 | tf_op jit(solution)/shard_map/sij,sjv->siv/dot_general | solution.py:28
  73.1 2.9 %copy.20 = f32[8,512,128]{2,1,0:T(8,128)} copy(f32[8,512,128]{1,2,0:T(8,128)} %multiply_bitcast_fusion) | data formatting | bytes 4194304 | tf_op jit(solution)/shard_map/mul | solution.py:70
  76.0 34.5 %reduce-scatter.2.cloned.1.call-done = f32[1024,128]{1,0:T(8,128)} async-done(((f32[4096,128]{1,0:T(8,128)}), f32[1024,128]{1,0:T(8,128)}) %reduce-scatter.2.cloned.1.call-update) | async-done | bytes 524304 | tf_op jit(solution)/shard_map/reduce_scatter | solution.py:70
  110.5 2.8 %fusion.23 = f32[128,128]{0,1:T(8,128)} fusion(f32[1024,128]{1,0:T(8,128)} %reduce-scatter.2.cloned.1.call-done), kind=kOutput, calls=%fused_computation.59 | convolution fusion | flops 201326592 | bytes 589824 | tf_op jit(solution)/shard_map/dot_general | solution.py:71
  113.4 121.2 %all-reduce.2.cloned.1.call-done = f32[128,128]{0,1:T(8,128)} async-done(((f32[128,128]{0,1:T(8,128)}), f32[128,128]{0,1:T(8,128)}) %all-reduce.2.cloned.1.call-update) | async-done | bytes 65552 | tf_op jit(solution)/shard_map/psum | solution.py:74
  234.6 0.9 copy.22
  235.5 0.9 fusion.10
  236.4 11.7 %cholesky.16 = f32[128,128]{1,0:T(8,128)S(1)} custom-call(f32[128,128]{1,0:T(8,128)S(1)} %fusion.10), custom_call_target="Cholesky" | custom-call | tf_op jit(solution)/shard_map/jit(cholesky)/cholesky | solution.py:75
  248.1 0.6 compare_reduce_fusion
  248.7 0.7 fusion.8
  249.4 9.8 %custom-call.6 = f32[1,128,128]{1,2,0:T(8,128)S(1)} custom-call(f32[1,128,128]{2,1,0:T(8,128)S(1)} %fusion.8), custom_call_target="InvertDiagBlocksLowerTriangular" | custom-call | tf_op jit(solution)/shard_map/triangular_solve | solution.py:77
  259.2 2.4 convolution_multiply_fusion
  (35 shorter events, 1.2 us)
Async XLA Ops:
  6.5 1.6 copy-start
  6.5 104.0 %reduce-scatter.2.cloned.1.call-start = ((), (), s32[]{:S(2)}) async-start(), calls=%async_computation.1 | async-start | bytes 2621440 | tf_op jit(solution)/shard_map/reduce_scatter | solution.py:70
  25.9 5.9 %slice-start = ((s32[8,2,128]{2,1,0:T(2,128)}), s32[8,1,128]{2,1,0:T(1,128)S(1)}, s32[]{:S(2)}) async-start(s32[8,2,128]{2,1,0:T(2,128)} %param.8), calls=%async_computation.3 | async-start | bytes 8192 | tf_op jit(solution)/shard_map/vmap()/slice | solution.py:36
  25.9 5.9 %copy-start.2 = (s32[8,2]{0,1:T(2,128)S(1)}, s32[8,2]{0,1:T(2,128)}, u32[]{:S(2)}) copy-start(s32[8,2]{0,1:T(2,128)} %param.9) | copy-start | bytes 196
  25.9 6.0 %copy-start.3 = (s32[2]{0:T(128)S(1)}, s32[2]{0:T(128)}, u32[]{:S(2)}) copy-start(s32[2]{0:T(128)} %constant.83) | copy-start | bytes 28
  25.9 6.0 %copy-start.1 = (f32[8,2,128]{2,1,0:T(2,128)S(1)}, f32[8,2,128]{2,1,0:T(2,128)}, u32[]{:S(2)}) copy-start(f32[8,2,128]{2,1,0:T(2,128)} %param.10) | copy-start | bytes 24580
  25.9 6.8 %copy-start.4 = (s32[2]{0:T(128)S(1)}, s32[2]{0:T(128)}, u32[]{:S(2)}) copy-start(s32[2]{0:T(128)} %constant.86) | copy-start | bytes 28
  27.3 15.1 %collective-permute-start.1 = (f32[1024,128]{1,0:T(8,128)}, f32[1024,128]{1,0:T(8,128)S(1)}, u32[]{:S(2)}, u32[]{:S(2)}) collective-permute-start(f32[1024,128]{1,0:T(8,128)} %get-tuple-element.14), channel_id=1, source_target_pairs={{1,0},{2,1},{3,2},{4,3},{5,4},{6,5},{7,6},{0,7},{9,8},{10,9},{11,1... | collective-permute-start | bytes 1572872 | tf_op jit(solution)/shard_map/ppermute | solution.py:20
  31.8 13.5 %collective-permute-start = (f32[1024,128]{1,0:T(8,128)}, f32[1024,128]{1,0:T(8,128)S(1)}, u32[]{:S(2)}, u32[]{:S(2)}) collective-permute-start(f32[1024,128]{1,0:T(8,128)} %get-tuple-element.13), channel_id=1, source_target_pairs={{0,1},{1,2},{2,3},{3,4},{4,5},{5,6},{6,7},{7,0},{8,9},{9,10},{10,1... | collective-permute-start | bytes 1572872 | tf_op jit(solution)/shard_map/ppermute | solution.py:18
  76.0 158.6 %all-reduce.2.cloned.1.call-start = ((), (), s32[]{:S(2)}) async-start(), calls=%async_computation.2 | async-start | bytes 131072 | tf_op jit(solution)/shard_map/psum | solution.py:74
Sparse Core Ops, SparseCore 0:
  76.1 34.3 reduce-scatter.1
  117.0 117.4 all-reduce.1
where the time goes:
time: 270 us; the launch traced here: 268 us
  waiting for transfers between devices  168 us (62%)
  other arithmetic  38.4 us (14%)
  matrix products  29.8 us (11%)
  between operations  14.3 us (5%)
  local copies, waits for them, and re-layouts  13.9 us (5%)
  starting transfers between devices  4.53 us (2%)
    psum x1, waiting for transfers between devices, per_device(): gram_matrix = lax.psum(local_gram, ('pole', 'sub'))  121 us
    reduce_scatter x1, waiting for transfers between devices, per_device(): lax.psum_scatter(weight * result, 'pole', scatter_dimension=0, tiled=True)  34.5 us
    dot_general x2, matrix products, apply_blocks(): jnp.einsum('sij,sjv->siv', blocks, fields, precision=precise, preferred_e...  23.2 us
    unnamed x5, other arithmetic  13.9 us
    another operation x3, other arithmetic, per_device(): lower_factor = jnp.linalg.cholesky(gram_matrix)  12.4 us
    another operation x2, other arithmetic, per_device(): lax.linalg.triangular_solve(lower_factor, filtered, left_side=False, lowe...  10.5 us
    ppermute x1, waiting for transfers between devices, extended_2(): lax.ppermute(head, axis, [((i + 1) % count, i) for i in range(count)])  9.6 us
    gather x1, local copies, waits for them, and re-layouts, per_device(): jnp.take(first_pass.reshape(sub_count * block_len, vec_count), flat_index...  7.05 us
  transfers between devices with their start and end apart: 4, of which 4 were waited for; matrix products, arithmetic and copies ran while one was open for 0% of the time, Pallas kernels for 0%

commit v1 on v0

v1 whole, which is shorter than its diff:
```python
import functools
import math

import jax
import jax.numpy as jnp
from jax import lax
from jax.experimental import pallas as pl
from jax.experimental.pallas import tpu as pltpu
from jax.sharding import PartitionSpec as P

f32 = jnp.float32
bf16 = jnp.bfloat16


def split(x):
    high = x.astype(bf16)
    low = (x - high.astype(f32)).astype(bf16)
    return high, low


def mm(a, b):
    return jnp.dot(a, b, preferred_element_type=f32)


def split_dot(a, b):
    width = b.shape[1]
    both = jnp.concatenate(split(b), axis=1)
    both = mm(a[0], both) + mm(a[1], both)
    return both[:, :width] + both[:, width:]


def turn(x):
    return pltpu.roll(x, x.shape[1] // 2, 1)


def left_lanes(x):
    return lax.broadcasted_iota(jnp.int32, x.shape, 1) < x.shape[1] // 2


def pack(top, bottom, half):
    if half == 0:
        return jnp.where(left_lanes(top), top, turn(bottom))
    return jnp.where(left_lanes(top), turn(top), bottom)


def sub_parity():
    return lax.rem(lax.axis_index("sub"), 2)


def pack_side(side_ref, s, half):
    rows = side_ref.shape[1] // 2
    return pack(side_ref[s, :rows, :], side_ref[s, rows:, :], half)


def gather_side(s, side, pass_ref, rows, side_ref, out_ref):
    for k in range(rows.shape[2]):
        side_ref[s, k : k + 1, :] = pass_ref[s, pl.ds(rows[s, side, k], 1), :]
    out_ref[s] = pack_side(side_ref, s, 0)


def first_kernel(weight, inv_hbm, field_hbm, rows_hbm, pass_ref, side_ref, off_ref,
                 inv_buf, field_buf, rows, inv_sems, field_sems, rows_sem):
    count = field_buf.shape[0]
    rows_copy = pltpu.make_async_copy(rows_hbm, rows, rows_sem)
    rows_copy.start()

    def copies(s):
        return (
            pltpu.make_async_copy(field_hbm.at[s], field_buf.at[s], field_sems.at[s]),
            pltpu.make_async_copy(inv_hbm.at[s], inv_buf.at[s], inv_sems.at[s]),
        )

    for s in range(count):
        for copy in copies(s):
            copy.start()
    rows_copy.wait()
    parity = sub_parity()

    def one_sub(s, carry):
        for copy in copies(s):
            copy.wait()
        gather_side(jnp.maximum(s - 1, 0), parity, pass_ref, rows, side_ref, off_ref)
        pass_ref[s] = weight[0] * split_dot(split(inv_buf[s]), field_buf[s])
        return carry

    lax.fori_loop(0, count, one_sub, 0)
    gather_side(count - 1, parity, pass_ref, rows, side_ref, off_ref)


def columns_kernel(inv_hbm, rows_hbm, rows_ref, coup_ref, near_ref, pass_ref, off_side_ref,
                   high_cols_ref, low_cols_ref, pass0_ref, pass1_ref, off_ref, on0_ref, on1_ref, table_ref,
                   inv_buf, on_side_ref, rows, inv_sems, rows_sem):
    count, block_len = inv_buf.shape[:2]
    iface_len = rows_ref.shape[2]
    quarter = block_len // 4

    def copy(s):
        return pltpu.make_async_copy(inv_hbm.at[s], inv_buf.at[s], inv_sems.at[s])

    rows_copy = pltpu.make_async_copy(rows_hbm, rows, rows_sem)
    rows_copy.start()
    for s in range(count):
        copy(s).start()
    parity = sub_parity()
    for spot, side in enumerate((parity, 1 - parity)):
        near = lax.rem(near_ref[pl.ds(side, 1), :], count)
        for s in range(count):
            table_ref[spot, s] = jnp.broadcast_to(near[:, s : s + 1], table_ref.shape[2:])
    place = lax.broadcasted_iota(jnp.int32, (block_len, 2 * iface_len), 0)
    rows_copy.wait()

    def one_sub(s, carry):
        copy(s).wait()
        gather_side(s, 1 - parity, pass_ref, rows, on_side_ref, on0_ref)
        on1_ref[s] = pack_side(on_side_ref, s, 1)
        off_ref[s] = pack_side(off_side_ref, s, 1)
        for half, out_ref in enumerate((pass0_ref, pass1_ref)):
            for way in range(2):
                at = 2 * way * quarter
                out_ref[s, way] = pack(
                    pass_ref[s, at : at + quarter, :], pass_ref[s, at + quarter : at + 2 * quarter, :], half
                )
        at, coup = (
            jnp.concatenate([ref[s, pl.ds(side, 1), :] for side in (parity, 1 - parity)], axis=1)
            for ref in (rows_ref, coup_ref)
        )
        pick = (at == place).astype(f32).astype(bf16)
        inv_high, inv_low = split(inv_buf[s])
        high_cols_ref[s], low_cols_ref[s] = split((mm(inv_high, pick) + mm(inv_low, pick)) * coup)
        return carry

    lax.fori_loop(0, count, one_sub, 0)


def second_kernel(poles, sent, table_ref, high_ref, low_ref, pass_ref, off_ref, on_ref, out_ref):
    count, ways, quarter, _ = pass_ref.shape
    per_owner = count // poles
    steps = poles.bit_length() - 1
    me, parity = lax.axis_index("pole"), sub_parity()
    for r in range(sent, poles, 2):
        turned = sum(1 << (steps - 1 - step) for step in range(steps) if r >> step & 1)
        owner = me ^ jnp.where(parity == 0, r, turned)
        for c in range(per_owner):
            sub = owner * per_owner + c
            terms = []
            for spot, ref in enumerate((off_ref, on_ref)):
                near = jnp.concatenate([table_ref[spot, sub]] * (ref.shape[1] // 8), axis=0)
                side = ref[0]
                for at in range(1, count):
                    side = jnp.where(near == at, ref[at], side)
                turned_side = turn(side)
                terms += [
                    jnp.where(left_lanes(side), side, turned_side),
                    jnp.where(left_lanes(side), turned_side, side),
                ]
            terms = jnp.concatenate(terms, axis=0)
            high = terms.astype(bf16).astype(f32)
            both = jnp.where(left_lanes(terms), high, terms - high).astype(bf16)
            out = mm(high_ref[sub], both) + mm(low_ref[sub], both)
            out = out + turn(out)
            for way in range(ways):
                at = 2 * way * quarter
                top, bottom = out[at : at + quarter], out[at + quarter : at + 2 * quarter]
                to = (c * ways + way) * quarter
                out_ref[r // 2, to : to + quarter, :] = (
                    jnp.where(left_lanes(top), top, bottom) + pass_ref[sub, way]
                )


def gram_kernel(groups, per_owner, *refs):
    count = sum(groups)
    ins, (halves_ref, gram_ref, out_ref) = refs[:count], refs[count:]
    parts = []
    at = 0
    for size in groups:
        parts.append(functools.reduce(jnp.add, [ref[0] for ref in ins[at : at + size]]))
        at += size
    quarter = out_ref.shape[0] // (4 * per_owner)
    for way in range(2):
        for c in range(per_owner):
            first, second = (part[(2 * c + way) * quarter : (2 * c + way + 1) * quarter] for part in parts)
            at = (4 * c + 2 * way) * quarter
            out_ref[at : at + quarter, :] = jnp.where(left_lanes(first), first, turn(second))
            out_ref[at + quarter : at + 2 * quarter, :] = jnp.where(left_lanes(first), turn(first), second)
    high, low = split(out_ref[...])
    width = out_ref.shape[1]
    halves = jnp.concatenate([high, low], axis=1)
    halves_ref[...] = halves
    both = lax.dot_general(high, halves, (((0,), (0,)), ((), ())), preferred_element_type=f32)
    cross = both[:, width:]
    gram = both[:, :width] + (cross + cross.T)
    half = width // 2
    row = lax.broadcasted_iota(jnp.int32, (half, width), 0)
    col = lax.broadcasted_iota(jnp.int32, (half, width), 1)
    gram_ref[:half, :] = jnp.where(row > col - half, jnp.where(col < half, gram[half:], turn(gram[:half])), gram[half:])
    diag = jnp.sum(jnp.where(row == col, gram[:half], 0.0), axis=0, keepdims=True)
    gram_ref[half:, :] = jnp.broadcast_to(diag, (gram_ref.shape[0] - half, width))


def unpacked(gram):
    width = gram.shape[1]
    half = width // 2
    row = lax.broadcasted_iota(jnp.int32, (half, width), 0)
    col = lax.broadcasted_iota(jnp.int32, (half, width), 1)
    top = gram[:half]
    diag = jnp.broadcast_to(gram[half : half + 1], top.shape)
    first = jnp.where(row > col, turn(top), jnp.where(row == col, 0.5 * diag, 0.0))
    last = jnp.where(col < half, top, jnp.where(col - half > row, top, jnp.where(col - half == row, 0.5 * top, 0.0)))
    lower = jnp.concatenate([first, last], axis=0)
    return lower + lower.T


def four_pivots(a):
    det = a[0][0] * a[1][1] - a[1][0] * a[1][0]
    inv = 1.0 / det
    p00, p01, p11 = a[1][1] * inv, -a[1][0] * inv, a[0][0] * inv
    g20, g21 = a[2][0] * p00 + a[2][1] * p01, a[2][0] * p01 + a[2][1] * p11
    g30, g31 = a[3][0] * p00 + a[3][1] * p01, a[3][0] * p01 + a[3][1] * p11
    s22 = a[2][2] - (g20 * a[2][0] + g21 * a[2][1])
    s32 = a[3][2] - (g30 * a[2][0] + g31 * a[2][1])
    s33 = a[3][3] - (g30 * a[3][0] + g31 * a[3][1])
    inv = 1.0 / (s22 * s33 - s32 * s32)
    q00, q01, q11 = s33 * inv, -s32 * inv, s22 * inv

    def solve(r):
        z2 = r[2] - (g20 * r[0] + g21 * r[1])
        z3 = r[3] - (g30 * r[0] + g31 * r[1])
        w2, w3 = q00 * z2 + q01 * z3, q01 * z2 + q11 * z3
        w0 = p00 * r[0] + p01 * r[1] - (g20 * w2 + g30 * w3)
        w1 = p01 * r[0] + p11 * r[1] - (g21 * w2 + g31 * w3)
        return [w0, w1, w2, w3]

    def normalized(r):
        z2 = r[2] - (g20 * r[0] + g21 * r[1])
        z3 = r[3] - (g30 * r[0] + g31 * r[1])
        root0, root2 = lax.rsqrt(a[0][0]), lax.rsqrt(s22)
        l10, l32 = a[1][0] * (root0 * root0), s32 * (root2 * root2)
        return [
            r[0] * root0,
            (r[1] - l10 * r[0]) * lax.rsqrt(a[1][1] - l10 * a[1][0]),
            z2 * root2,
            (z3 - l32 * z2) * lax.rsqrt(s33 - l32 * s32),
        ]

    return solve, normalized


def combined(weights, rows):
    return (weights[0] * rows[0] + weights[1] * rows[1]) + (weights[2] * rows[2] + weights[3] * rows[3])


def inverse_rows(gram, tile_refs):
    vecs = gram.shape[0]
    tile, block = 8, 4
    tiles = vecs // tile
    sub_id = lax.broadcasted_iota(jnp.int32, (tile, vecs), 0)
    lane_id = lax.broadcasted_iota(jnp.int32, (tile, vecs), 1)
    diag = [jnp.where(lane_id == sub_id + t * tile, gram[t * tile : (t + 1) * tile], 0.0) for t in range(tiles)]
    scale = lax.rsqrt(jnp.sum(functools.reduce(jnp.add, diag), axis=0, keepdims=True))
    left, right = [], []
    for t in range(tiles):
        own = lax.rsqrt(jnp.sum(diag[t], axis=1, keepdims=True))
        left.append(gram[t * tile : (t + 1) * tile] * scale * own)
        right.append(jnp.where(lane_id == sub_id + t * tile, jnp.broadcast_to(scale, (tile, vecs)), 0.0))

    def lane(x, k):
        return jnp.broadcast_to(x[:, k : k + 1], (tile, vecs))

    def rows_of(tiles_now):
        for ref, x in zip(tile_refs, tiles_now):
            ref[...] = x
        return [[ref[pl.ds(i, tile, stride=0), :] for i in range(tile)] for ref in tile_refs]

    done = []
    for at in range(tiles):
        k = at * tile
        both_rows = rows_of((left[at], right[at]))
        a = [[lane(both_rows[0][i], k + j) for i in range(j + 1)] for j in range(tile)]
        solve, normalized = four_pivots(a)
        inner = [solve(a[j][:block]) for j in range(block, tile)]
        after = [
            [a[block + j][block + i] - combined(a[block + j], inner[i]) for i in range(j + 1)] for j in range(block)
        ]
        solve_after, normalized_after = four_pivots(after)
        weights = []
        for rows in both_rows:
            first = solve(rows[:block])
            later = [rows[block + j] - combined(a[block + j], first) for j in range(block)]
            second = solve_after(later)
            first = [w - combined([inner[j][i] for j in range(block)], second) for i, w in enumerate(first)]
            weights.append(first + second)
        done += [x[:1] for x in normalized(rows[:block]) + normalized_after(later)]
        for t in range(at + 1, tiles):
            cols = [lane(left[t], k + i) for i in range(tile)]
            for part, w in zip((left, right), weights):
                part[t] = part[t] - (combined(cols[:block], w[:block]) + combined(cols[block:], w[block:]))
    return jnp.concatenate(done, axis=0)


def ortho_kernel(scale, *refs):
    *gram_refs, halves_ref, out_ref, left_ref, right_ref = refs
    gram = functools.reduce(jnp.add, [ref[...] for ref in gram_refs])
    width = gram.shape[1]
    inverse = jnp.concatenate(split(inverse_rows(unpacked(gram), (left_ref, right_ref)) * scale), axis=0)
    both = lax.dot_general(
        halves_ref[...],
        jnp.concatenate([inverse, inverse], axis=1),
        (((1,), (1,)), ((), ())),
        preferred_element_type=f32,
    )
    out_ref[...] = both[:, :width] + both[:, width:]


def call(body, out_shape, flops=0, moved=0, limit=24, **kw):
    return pl.pallas_call(
        body,
        out_shape=out_shape,
        compiler_params=pltpu.CompilerParams(vmem_limit_bytes=limit * 1024 * 1024),
        cost_estimate=pl.CostEstimate(flops=flops, bytes_accessed=moved, transcendentals=0),
        **kw,
    )


def swap(value, even, odd):
    poles, groups = lax.axis_size("pole"), lax.axis_size("sub")
    pairs = []
    for p in range(poles):
        for s in range(groups):
            pole_mask, sub_mask = odd if s % 2 else even
            pairs.append((p * groups + s, (p ^ pole_mask) * groups + (s ^ sub_mask)))
    return lax.ppermute(value, ("pole", "sub"), pairs)


def per_device(start_block, inverses, iface_rows, neighbors, couplings, pole_weights):
    blocks = inverses[0]
    sub_count, block_len = blocks.shape[:2]
    vecs = start_block.shape[1]
    iface_len = iface_rows.shape[2]
    poles, groups = lax.axis_size("pole"), lax.axis_size("sub")
    fields = start_block.reshape(sub_count, block_len, vecs)
    shape = jax.ShapeDtypeStruct
    smem = pl.BlockSpec(memory_space=pltpu.SMEM)
    hbm = pl.BlockSpec(memory_space=pltpu.HBM)
    vmem = pl.BlockSpec(memory_space=pltpu.VMEM)
    block_bytes = sub_count * block_len * block_len * 4
    field_bytes = sub_count * block_len * vecs * 4
    packed = shape((sub_count, iface_len // 2, vecs), f32)
    in_hbm = functools.partial(pltpu.with_memory_space_constraint, memory_space=pltpu.HBM)
    in_vmem = functools.partial(pltpu.with_memory_space_constraint, memory_space=pltpu.VMEM)
    sides = shape((sub_count, iface_len, vecs), f32)
    first, off_side, off0 = call(
        first_kernel,
        (shape(fields.shape, f32), sides, packed),
        flops=8 * sub_count * block_len * block_len * vecs,
        moved=block_bytes + 3 * field_bytes,
        in_specs=[smem, hbm, hbm, hbm],
        out_specs=[vmem] * 3,
        scratch_shapes=[
            pltpu.VMEM(blocks.shape, f32),
            pltpu.VMEM(fields.shape, f32),
            pltpu.SMEM(iface_rows.shape, jnp.int32),
            pltpu.SemaphoreType.DMA((sub_count,)),
            pltpu.SemaphoreType.DMA((sub_count,)),
            pltpu.SemaphoreType.DMA,
        ],
        name="first_pass",
    )(pole_weights, in_hbm(blocks), in_hbm(fields), in_hbm(iface_rows))
    first, off_side = in_vmem(first), in_vmem(off_side)
    across = [(s, (s + (1 if s % 2 else -1)) % groups) for s in range(groups)]
    inside = [(s, s ^ 1) for s in range(groups)]
    off_in0 = lax.ppermute(off0, "sub", across)
    cols = shape((sub_count, block_len, 2 * iface_len), bf16)
    pass_half = shape((sub_count, 2, block_len // 4, vecs), f32)
    cols_high, cols_low, pass0, pass1, off1, on0, on1, table = call(
        columns_kernel,
        (cols, cols, pass_half, pass_half, packed, packed, packed, shape((2, sub_count, 8, vecs), jnp.int32)),
        flops=8 * sub_count * block_len * block_len * iface_len,
        moved=2 * block_bytes,
        in_specs=[hbm] * 2 + [vmem] * 5,
        out_specs=[vmem] * 8,
        scratch_shapes=[
            pltpu.VMEM(blocks.shape, f32),
            pltpu.VMEM(sides.shape, f32),
            pltpu.SMEM(iface_rows.shape, jnp.int32),
            pltpu.SemaphoreType.DMA((sub_count,)),
            pltpu.SemaphoreType.DMA,
        ],
        name="interface_columns",
    )(in_hbm(blocks), in_hbm(iface_rows), iface_rows, couplings, neighbors.T, first, off_side)
    on_in0 = lax.ppermute(on0, "sub", inside)
    halves = [(off_in0, on_in0), (lax.ppermute(off1, "sub", across), lax.ppermute(on1, "sub", inside))]
    cols_high, cols_low, pass0, pass1 = (in_vmem(v) for v in (cols_high, cols_low, pass0, pass1))

    per_owner = sub_count // poles
    steps = poles.bit_length() - 1
    parts = shape((poles // 2, per_owner * block_len // 2, vecs), f32)
    pending = []
    for own_pass, (off_in, on_in) in zip((pass0, pass1), halves):
        send, keep = (
            call(
                functools.partial(second_kernel, poles, sent),
                parts,
                flops=4 * sub_count * block_len * 2 * iface_len * vecs,
                moved=2 * sub_count * block_len * vecs * 4,
                in_specs=[vmem] * 6,
                out_specs=vmem,
                name="second_pass",
            )(table, cols_high, cols_low, own_pass, off_in, on_in)
            for sent in (1, 0)
        )
        pending.append((send, [keep]))

    for step in range(steps):
        masks = (1 << step, 0), (1 << (steps - 1 - step), 0)
        for half, (send, kept) in enumerate(pending):
            kept = kept + [swap(send, *masks)]
            if kept[0].shape[0] > 1:
                send = functools.reduce(jnp.add, [v[1::2] for v in kept])
                kept = [v[0::2] for v in kept]
            pending[half] = (send, kept)

    summands = [kept for _, kept in pending]
    sizes = tuple(len(kept) for kept in summands)
    own_rows = per_owner * block_len
    basis_halves, gram = call(
        functools.partial(gram_kernel, sizes, per_owner),
        (shape((own_rows, 2 * vecs), bf16), shape((vecs // 2 + 8, vecs), f32)),
        flops=4 * own_rows * vecs * vecs,
        moved=5 * own_rows * vecs * 4,
        in_specs=[vmem] * sum(sizes),
        out_specs=[vmem] * 2,
        scratch_shapes=[pltpu.VMEM((own_rows, vecs), f32)],
        name="gram",
    )(*[v for kept in summands for v in kept])

    stages = [[(0, 1)], [(r, 0) for r in range(1, poles)]]
    base = 2
    while base < groups:
        radix = min(4, groups // base)
        stages.append([(0, base * r) for r in range(1, radix)])
        base *= radix
    grams = [gram]
    for masks in stages:
        total = functools.reduce(jnp.add, grams)
        grams = [total] + [swap(total, m, m) for m in masks]

    total_rows = sub_count * block_len * groups
    return call(
        functools.partial(ortho_kernel, math.sqrt(total_rows)),
        shape((own_rows, vecs), f32),
        flops=6 * own_rows * vecs * vecs,
        moved=2 * own_rows * vecs * 4,
        in_specs=[vmem] * (len(grams) + 1),
        out_specs=vmem,
        scratch_shapes=[pltpu.VMEM((8, vecs), f32)] * 2,
        name="ortho",
    )(*grams, basis_halves)


def solution(mesh):
    placed = (
        P("sub", None),
        P("pole", "sub", None, None),
        P("sub", None, None),
        P("sub", None),
        P("sub", None, None),
        P("pole"),
    )
    return jax.shard_map(
        per_device, mesh=mesh, in_specs=placed, out_specs=P(("sub", "pole"), None), check_vma=False
    )
```

time: 270 us -> 68.4 us (0.25)
  waiting for transfers between devices: 168 us -> 26.3 us
  other arithmetic: 38.4 us -> 0.15 us
  matrix products: 29.8 us -> 0 us
  Pallas kernels: 0 us -> 21.5 us
  starting transfers between devices: 4.53 us -> 19.5 us
  local copies, waits for them, and re-layouts: 13.9 us -> 0.01 us
  between operations: 14.3 us -> 0.79 us
    psum x1 -> x0, waiting for transfers between devices: 121 us -> none  [per_device(): gram_matrix = lax.psum(local_gram, ('pole', 'sub'))]
    reduce_scatter x1 -> x0, waiting for transfers between devices: 34.5 us -> none  [per_device(): lax.psum_scatter(weight * result, 'pole', scatter_dimension=0, tiled=True)]
    dot_general x5 -> x0, matrix products: 27.4 us -> none  [the longest x2 23.2 us: apply_blocks(): jnp.einsum('sij,sjv->siv', blocks, fields, precision=precise, preferred_e...]
    another operation x5 -> x0, other arithmetic: 22.9 us -> none  [the longest x3 12.4 us: per_device(): lower_factor = jnp.linalg.cholesky(gram_matrix)]
    pallas_call x0 -> x8, Pallas kernels: none -> 21.5 us  [the longest x1 6.36 us: per_device(): call(columns_kernel, (cols, cols, pass_half, pass_half, packed, packed, p...]
    ppermute x2 -> x15, starting transfers between devices: 4.49 us -> 19.5 us  [the longest x11 14.2 us: swap(): return lax.ppermute(value, ('pole', 'sub'), pairs)]
    ppermute x2 -> x15, waiting for transfers between devices: 11.8 us -> 26.3 us  [the longest x11 20 us: swap(): return lax.ppermute(value, ('pole', 'sub'), pairs)]
    unnamed x5 -> x0, other arithmetic: 13.9 us -> none
  transfers between devices with their start and end apart: 4 -> 15, of which waited for: 4 -> 10; matrix products, arithmetic and copies ran while one was open for 0% -> 0% of each run, Pallas kernels for 0% -> 15%
where the time goes in v1:
time: 68.4 us; the launch traced here: 68.2 us
  waiting for transfers between devices  26.3 us (38%)
  Pallas kernels  21.5 us (31%)
  starting transfers between devices  19.5 us (29%)
  between operations  0.79 us (1%)
    ppermute x11, waiting for transfers between devices, swap(): return lax.ppermute(value, ('pole', 'sub'), pairs)  20 us
    ppermute x11, starting transfers between devices, swap(): return lax.ppermute(value, ('pole', 'sub'), pairs)  14.2 us
    pallas_call x1, Pallas kernels, per_device(): call(columns_kernel, (cols, cols, pass_half, pass_half, packed, packed, p...  6.36 us
    pallas_call x1, Pallas kernels, per_device(): call(first_kernel, (shape(fields.shape, f32), sides, packed), flops=8 * s...  6.1 us
    ppermute x1, waiting for transfers between devices, per_device(): lax.ppermute(off1, 'sub', across)  5.52 us
    pallas_call x1, Pallas kernels, per_device(): call(functools.partial(ortho_kernel, math.sqrt(total_rows)), shape((own_r...  4.9 us
    ppermute x1, starting transfers between devices, per_device(): off_in0 = lax.ppermute(off0, 'sub', across)  4.55 us
    pallas_call x4, Pallas kernels, per_device(): call(functools.partial(second_kernel, poles, sent), parts, flops=4 * sub_...  3.59 us
  transfers between devices with their start and end apart: 15, of which 10 were waited for; matrix products, arithmetic and copies ran while one was open for 0% of the time, Pallas kernels for 15%

profile of v1, /device:TPU:0, one launch (start us, length us, event | category | flops | bytes accessed | tf_op | source)
XLA Modules:
  0.0 68.2 jit_solution(15855040005009345008)
XLA Ops:
  0.7 6.1 %first_pass.1 = (f32[8,512,128]{2,1,0:T(8,128)S(1)}, f32[8,128,128]{2,1,0:T(8,128)S(1)}, f32[8,64,128]{2,1,0:T(8,128)S(1)}) custom-call(f32[1]{0:T(128)S(6)} %copy.7.weight, f32[8,512,512]{2,1,0:T(8,128)} %bitcast.4, f32[8,512,128]{2,1,0:T(8,128)} %bitcast.6, s32[8,2,128]{2,1,0:T(2,128)} %rows_ref.1), custom_call_target="tpu_custom_call" | custom-call | flops 2147483648 | bytes 14680064 | tf_op jit(solution)/shard_map/first_pass/pallas_call | solution.py:351
  6.8 4.6 %collective-permute-start = (f32[8,64,128]{2,1,0:T(8,128)S(1)}, f32[8,64,128]{2,1,0:T(8,128)S(1)}, u32[]{:S(2)}, u32[]{:S(2)}) collective-permute-start(f32[8,64,128]{2,1,0:T(8,128)S(1)} %get-tuple-element.24), channel_id=1, source_target_pairs={{0,7},{1,2},{2,1},{3,4},{4,3},{5,6},{6,5},{7,0},{8,15},{9,10},{10,... | collective-permute-start | bytes 786440 | tf_op jit(solution)/shard_map/ppermute | solution.py:371
  11.3 6.4 %interface_columns.1 = (bf16[8,512,256]{2,1,0:T(8,128)(2,1)S(1)}, bf16[8,512,256]{2,1,0:T(8,128)(2,1)S(1)}, f32[8,2,128,128]{3,2,1,0:T(8,128)S(1)}, f32[8,2,128,...) custom-call(f32[8,512,512]{2,1,0:T(8,128)} %bitcast.5, ...), custom_call_target="tpu_custom_call" | custom-call | flops 2147483648 | bytes 16777216 | tf_op jit(solution)/shard_map/interface_columns/pallas_call | solution.py:374
  18.5 0.8 %collective-permute-done.1.on_ref = f32[8,64,128]{2,1,0:T(8,128)S(1)} collective-permute-done((f32[8,64,128]{2,1,0:T(8,128)S(1)}, f32[8,64,128]{2,1,0:T(8,128)S(1)}, u32[]{:S(2)}, u32[]{:S(2)}) %collective-permute-start.1) | collective-permute-done | bytes 262176 | tf_op jit(solution)/shard_map/ppermute | solution.py:390
  19.3 0.9 %second_pass.5 = f32[2,512,128]{2,1,0:T(8,128)S(1)} custom-call(s32[2,8,8,128]{3,2,1,0:T(8,128)S(1)} %get-tuple-element.20.table_ref, bf16[8,512,256]{2,1,0:T(8,128)(2,1)S(1)} %get-tuple-element.21.high_ref, bf16[8,512,256]{2,1,0:T(8,128)(2,1)S(1)} %get-tuple-element.22.low_ref, f32[8,2,128,128]{3,2,1,0:T(8,128)S(1)} %get-tuple-element.23.pass_ref, ...), custom_call_target="tpu_custom_call" | custom-call | flops 536870912 | bytes 4194304 | tf_op jit(solution)/shard_map/second_pass/pallas_call | solution.py:400
  20.2 1.6 %collective-permute-start.2 = (f32[2,512,128]{2,1,0:T(8,128)S(1)}, f32[2,512,128]{2,1,0:T(8,128)S(1)}, u32[]{:S(2)}, u32[]{:S(2)}) collective-permute-start(f32[2,512,128]{2,1,0:T(8,128)S(1)} %second_pass.5), channel_id=1, source_target_pairs={{0,8},{1,17},{2,10},{3,19},{4,12},{5,21},{6,14},{7,23},{8,0},{9,25... | collective-permute-start | bytes 1572872 | tf_op jit(solution)/shard_map/ppermute | solution.py:331
  21.8 5.5 %collective-permute-done.4.off_ref = f32[8,64,128]{2,1,0:T(8,128)S(1)} collective-permute-done((f32[8,64,128]{2,1,0:T(8,128)S(1)}, f32[8,64,128]{2,1,0:T(8,128)S(1)}, u32[]{:S(2)}, u32[]{:S(2)}) %collective-permute-start.4) | collective-permute-done | bytes 262176 | tf_op jit(solution)/shard_map/ppermute | solution.py:391
  27.3 0.9 %second_pass.7 = f32[2,512,128]{2,1,0:T(8,128)S(1)} custom-call(s32[2,8,8,128]{3,2,1,0:T(8,128)S(1)} %get-tuple-element.20.table_ref, bf16[8,512,256]{2,1,0:T(8,128)(2,1)S(1)} %get-tuple-element.21.high_ref, bf16[8,512,256]{2,1,0:T(8,128)(2,1)S(1)} %get-tuple-element.22.low_ref, f32[8,2,128,128]{3,2,1,0:T(8,128)S(1)} %get-tuple-element.26.pass_ref, ...), custom_call_target="tpu_custom_call" | custom-call | flops 536870912 | bytes 4194304 | tf_op jit(solution)/shard_map/second_pass/pallas_call | solution.py:400
  28.2 1.6 %collective-permute-start.6 = (f32[2,512,128]{2,1,0:T(8,128)S(1)}, f32[2,512,128]{2,1,0:T(8,128)S(1)}, u32[]{:S(2)}, u32[]{:S(2)}) collective-permute-start(f32[2,512,128]{2,1,0:T(8,128)S(1)} %second_pass.7), channel_id=1, source_target_pairs={{0,8},{1,17},{2,10},{3,19},{4,12},{5,21},{6,14},{7,23},{8,0},{9,25... | collective-permute-start | bytes 1572872 | tf_op jit(solution)/shard_map/ppermute | solution.py:331
  29.8 0.9 %second_pass.6 = f32[2,512,128]{2,1,0:T(8,128)S(1)} custom-call(s32[2,8,8,128]{3,2,1,0:T(8,128)S(1)} %get-tuple-element.20.table_ref, bf16[8,512,256]{2,1,0:T(8,128)(2,1)S(1)} %get-tuple-element.21.high_ref, bf16[8,512,256]{2,1,0:T(8,128)(2,1)S(1)} %get-tuple-element.22.low_ref, f32[8,2,128,128]{3,2,1,0:T(8,128)S(1)} %get-tuple-element.26.pass_ref, ...), custom_call_target="tpu_custom_call" | custom-call | flops 536870912 | bytes 4194304 | tf_op jit(solution)/shard_map/second_pass/pallas_call | solution.py:400
  30.7 0.9 %second_pass.4 = f32[2,512,128]{2,1,0:T(8,128)S(1)} custom-call(s32[2,8,8,128]{3,2,1,0:T(8,128)S(1)} %get-tuple-element.20.table_ref, bf16[8,512,256]{2,1,0:T(8,128)(2,1)S(1)} %get-tuple-element.21.high_ref, bf16[8,512,256]{2,1,0:T(8,128)(2,1)S(1)} %get-tuple-element.22.low_ref, f32[8,2,128,128]{3,2,1,0:T(8,128)S(1)} %get-tuple-element.23.pass_ref, ...), custom_call_target="tpu_custom_call" | custom-call | flops 536870912 | bytes 4194304 | tf_op jit(solution)/shard_map/second_pass/pallas_call | solution.py:400
  31.7 1.6 %collective-permute-start.3 = (f32[1,512,128]{2,1,0:T(8,128)S(1)}, f32[1,512,128]{2,1,0:T(8,128)S(1)}, u32[]{:S(2)}, u32[]{:S(2)}) collective-permute-start(f32[1,512,128]{2,1,0:T(8,128)S(1)} %get-tuple-element.34), channel_id=1, source_target_pairs={{0,16},{1,9},{2,18},{3,11},{4,20},{5,13},{6,22},{7,15},{8,24},{9,1... | collective-permute-start | bytes 786440 | tf_op jit(solution)/shard_map/ppermute | solution.py:331
  33.3 8.6 %collective-permute-done.6 = f32[2,512,128]{2,1,0:T(8,128)S(1)} collective-permute-done((f32[2,512,128]{2,1,0:T(8,128)S(1)}, f32[2,512,128]{2,1,0:T(8,128)S(1)}, u32[]{:S(2)}, u32[]{:S(2)}) %collective-permute-start.6) | collective-permute-done | bytes 524320 | tf_op jit(solution)/shard_map/ppermute | solution.py:331
  41.9 1.4 %collective-permute-start.7 = (f32[1,512,128]{2,1,0:T(8,128)S(1)}, f32[1,512,128]{2,1,0:T(8,128)S(1)}, u32[]{:S(2)}, u32[]{:S(2)}) collective-permute-start(f32[1,512,128]{2,1,0:T(8,128)S(1)} %get-tuple-element.31), channel_id=1, source_target_pairs={{0,16},{1,9},{2,18},{3,11},{4,20},{5,13},{6,22},{7,15},{8,24},{9,1... | collective-permute-start | bytes 786440 | tf_op jit(solution)/shard_map/ppermute | solution.py:331
  43.4 5.0 %collective-permute-done.7.refs_5_ = f32[1,512,128]{2,1,0:T(8,128)S(1)} collective-permute-done((f32[1,512,128]{2,1,0:T(8,128)S(1)}, f32[1,512,128]{2,1,0:T(8,128)S(1)}, u32[]{:S(2)}, u32[]{:S(2)}) %collective-permute-start.7) | collective-permute-done | bytes 262176 | tf_op jit(solution)/shard_map/ppermute | solution.py:331
  49.0 1.2 %collective-permute-done.8 = f32[72,128]{1,0:T(8,128)S(1)} collective-permute-done((f32[72,128]{1,0:T(8,128)S(1)}, f32[72,128]{1,0:T(8,128)S(1)}, u32[]{:S(2)}, u32[]{:S(2)}) %collective-permute-start.8) | collective-permute-done | bytes 36896 | tf_op jit(solution)/shard_map/ppermute | solution.py:331
  50.2 2.1 %collective-permute-start.11 = (f32[72,128]{1,0:T(8,128)S(1)}, f32[72,128]{1,0:T(8,128)S(1)}, u32[]{:S(2)}, u32[]{:S(2)}) collective-permute-start(f32[72,128]{1,0:T(8,128)S(1)} %add.20), channel_id=1, source_target_pairs={{0,24},{1,25},{2,26},{3,27},{4,28},{5,29},{6,30},{7,31},{8,16},{9,... | collective-permute-start | bytes 110600 | tf_op jit(solution)/shard_map/ppermute | solution.py:331
  52.3 0.7 %collective-permute-start.10 = (f32[72,128]{1,0:T(8,128)S(1)}, f32[72,128]{1,0:T(8,128)S(1)}, u32[]{:S(2)}, u32[]{:S(2)}) collective-permute-start(f32[72,128]{1,0:T(8,128)S(1)} %add.20), channel_id=1, source_target_pairs={{0,16},{1,17},{2,18},{3,19},{4,20},{5,21},{6,22},{7,23},{8,24},{9,... | collective-permute-start | bytes 110600 | tf_op jit(solution)/shard_map/ppermute | solution.py:331
  53.0 0.7 %collective-permute-start.9 = (f32[72,128]{1,0:T(8,128)S(1)}, f32[72,128]{1,0:T(8,128)S(1)}, u32[]{:S(2)}, u32[]{:S(2)}) collective-permute-start(f32[72,128]{1,0:T(8,128)S(1)} %add.20), channel_id=1, source_target_pairs={{0,8},{1,9},{2,10},{3,11},{4,12},{5,13},{6,14},{7,15},{8,0},{9,1},... | collective-permute-start | bytes 110600 | tf_op jit(solution)/shard_map/ppermute | solution.py:331
  53.7 1.4 %collective-permute-done.11 = f32[72,128]{1,0:T(8,128)S(1)} collective-permute-done((f32[72,128]{1,0:T(8,128)S(1)}, f32[72,128]{1,0:T(8,128)S(1)}, u32[]{:S(2)}, u32[]{:S(2)}) %collective-permute-start.11) | collective-permute-done | bytes 36896 | tf_op jit(solution)/shard_map/ppermute | solution.py:331
  55.1 1.1 %collective-permute-done.10 = f32[72,128]{1,0:T(8,128)S(1)} collective-permute-done((f32[72,128]{1,0:T(8,128)S(1)}, f32[72,128]{1,0:T(8,128)S(1)}, u32[]{:S(2)}, u32[]{:S(2)}) %collective-permute-start.10) | collective-permute-done | bytes 36896 | tf_op jit(solution)/shard_map/ppermute | solution.py:331
  57.1 4.3 %collective-permute-start.12 = (f32[72,128]{1,0:T(8,128)S(1)}, f32[72,128]{1,0:T(8,128)S(1)}, u32[]{:S(2)}, u32[]{:S(2)}) collective-permute-start(f32[72,128]{1,0:T(8,128)S(1)} %add_add_fusion.refs_0_), channel_id=1, source_target_pairs={{0,2},{1,3},{2,0},{3,1},{4,6},{5,7},{6,4},{7,5},{8,10},{9,11},{10,... | collective-permute-start | bytes 110600 | tf_op jit(solution)/shard_map/ppermute | solution.py:331
  61.4 1.4 %collective-permute-done.14.refs_3_ = f32[72,128]{1,0:T(8,128)S(1)} collective-permute-done((f32[72,128]{1,0:T(8,128)S(1)}, f32[72,128]{1,0:T(8,128)S(1)}, u32[]{:S(2)}, u32[]{:S(2)}) %collective-permute-start.14) | collective-permute-done | bytes 36896 | tf_op jit(solution)/shard_map/ppermute | solution.py:331
  63.3 4.9 %ortho.1 = f32[1024,128]{1,0:T(8,128)} custom-call(f32[72,128]{1,0:T(8,128)S(1)} %add_add_fusion.refs_0_, f32[72,128]{1,0:T(8,128)S(1)} %collective-permute-done.12.refs_1_, f32[72,128]{1,0:T(8,128)S(1)} %collective-permute-done.13.refs_2_, f32[72,128]{1,0:T(8,128)S(1)} %collective-permute-done.14.refs_3_, bf16[1024,256]{1,0:T(8,128)(2,1)S(1)} %get-tuple-element.30.refs_4_), custom_call_target="tpu_custom_call" | custom-call | flops 100663296 | bytes 1048576 | tf_op jit(solution)/shard_map/ortho/pallas_call | solution.py:448
  (22 shorter events, 3.0 us)
Async XLA Ops:
  0.7 10.7 %copy-start = (f32[8,2,128]{2,1,0:T(2,128)S(1)}, f32[8,2,128]{2,1,0:T(2,128)}, u32[]{:S(2)}) copy-start(f32[8,2,128]{2,1,0:T(2,128)} %coup_ref.1) | copy-start | bytes 24580
  0.7 10.7 %copy-start.1 = (s32[8,2]{0,1:T(2,128)S(1)}, s32[8,2]{0,1:T(2,128)}, u32[]{:S(2)}) copy-start(s32[8,2]{0,1:T(2,128)} %param.9) | copy-start | bytes 196
  6.8 11.7 %collective-permute-start = (f32[8,64,128]{2,1,0:T(8,128)S(1)}, f32[8,64,128]{2,1,0:T(8,128)S(1)}, u32[]{:S(2)}, u32[]{:S(2)}) collective-permute-start(f32[8,64,128]{2,1,0:T(8,128)S(1)} %get-tuple-element.24), channel_id=1, source_target_pairs={{0,7},{1,2},{2,1},{3,4},{4,3},{5,6},{6,5},{7,0},{8,15},{9,10},{10,... | collective-permute-start | bytes 786440 | tf_op jit(solution)/shard_map/ppermute | solution.py:371
  17.7 1.6 %collective-permute-start.1 = (f32[8,64,128]{2,1,0:T(8,128)S(1)}, f32[8,64,128]{2,1,0:T(8,128)S(1)}, u32[]{:S(2)}, u32[]{:S(2)}) collective-permute-start(f32[8,64,128]{2,1,0:T(8,128)S(1)} %get-tuple-element.25), channel_id=1, source_target_pairs={{0,1},{1,0},{2,3},{3,2},{4,5},{5,4},{6,7},{7,6},{8,9},{9,8},{10,11... | collective-permute-start | bytes 786440 | tf_op jit(solution)/shard_map/ppermute | solution.py:390
  17.8 9.5 %collective-permute-start.4 = (f32[8,64,128]{2,1,0:T(8,128)S(1)}, f32[8,64,128]{2,1,0:T(8,128)S(1)}, u32[]{:S(2)}, u32[]{:S(2)}) collective-permute-start(f32[8,64,128]{2,1,0:T(8,128)S(1)} %get-tuple-element.27), channel_id=1, source_target_pairs={{0,7},{1,2},{2,1},{3,4},{4,3},{5,6},{6,5},{7,0},{8,15},{9,10},{10,... | collective-permute-start | bytes 786440 | tf_op jit(solution)/shard_map/ppermute | solution.py:391
  18.5 8.8 %collective-permute-start.5 = (f32[8,64,128]{2,1,0:T(8,128)S(1)}, f32[8,64,128]{2,1,0:T(8,128)S(1)}, u32[]{:S(2)}, u32[]{:S(2)}) collective-permute-start(f32[8,64,128]{2,1,0:T(8,128)S(1)} %get-tuple-element.28), channel_id=1, source_target_pairs={{0,1},{1,0},{2,3},{3,2},{4,5},{5,4},{6,7},{7,6},{8,9},{9,8},{10,11... | collective-permute-start | bytes 786440 | tf_op jit(solution)/shard_map/ppermute | solution.py:391
  20.2 11.4 %collective-permute-start.2 = (f32[2,512,128]{2,1,0:T(8,128)S(1)}, f32[2,512,128]{2,1,0:T(8,128)S(1)}, u32[]{:S(2)}, u32[]{:S(2)}) collective-permute-start(f32[2,512,128]{2,1,0:T(8,128)S(1)} %second_pass.5), channel_id=1, source_target_pairs={{0,8},{1,17},{2,10},{3,19},{4,12},{5,21},{6,14},{7,23},{8,0},{9,25... | collective-permute-start | bytes 1572872 | tf_op jit(solution)/shard_map/ppermute | solution.py:331
  28.2 13.6 %collective-permute-start.6 = (f32[2,512,128]{2,1,0:T(8,128)S(1)}, f32[2,512,128]{2,1,0:T(8,128)S(1)}, u32[]{:S(2)}, u32[]{:S(2)}) collective-permute-start(f32[2,512,128]{2,1,0:T(8,128)S(1)} %second_pass.7), channel_id=1, source_target_pairs={{0,8},{1,17},{2,10},{3,19},{4,12},{5,21},{6,14},{7,23},{8,0},{9,25... | collective-permute-start | bytes 1572872 | tf_op jit(solution)/shard_map/ppermute | solution.py:331
  31.7 11.7 %collective-permute-start.3 = (f32[1,512,128]{2,1,0:T(8,128)S(1)}, f32[1,512,128]{2,1,0:T(8,128)S(1)}, u32[]{:S(2)}, u32[]{:S(2)}) collective-permute-start(f32[1,512,128]{2,1,0:T(8,128)S(1)} %get-tuple-element.34), channel_id=1, source_target_pairs={{0,16},{1,9},{2,18},{3,11},{4,20},{5,13},{6,22},{7,15},{8,24},{9,1... | collective-permute-start | bytes 786440 | tf_op jit(solution)/shard_map/ppermute | solution.py:331
  41.9 6.4 %collective-permute-start.7 = (f32[1,512,128]{2,1,0:T(8,128)S(1)}, f32[1,512,128]{2,1,0:T(8,128)S(1)}, u32[]{:S(2)}, u32[]{:S(2)}) collective-permute-start(f32[1,512,128]{2,1,0:T(8,128)S(1)} %get-tuple-element.31), channel_id=1, source_target_pairs={{0,16},{1,9},{2,18},{3,11},{4,20},{5,13},{6,22},{7,15},{8,24},{9,1... | collective-permute-start | bytes 786440 | tf_op jit(solution)/shard_map/ppermute | solution.py:331
  48.9 1.3 %collective-permute-start.8 = (f32[72,128]{1,0:T(8,128)S(1)}, f32[72,128]{1,0:T(8,128)S(1)}, u32[]{:S(2)}, u32[]{:S(2)}) collective-permute-start(f32[72,128]{1,0:T(8,128)S(1)} %get-tuple-element.29), channel_id=1, source_target_pairs={{0,1},{1,0},{2,3},{3,2},{4,5},{5,4},{6,7},{7,6},{8,9},{9,8},{10,11... | collective-permute-start | bytes 110600 | tf_op jit(solution)/shard_map/ppermute | solution.py:331
  50.2 4.9 %collective-permute-start.11 = (f32[72,128]{1,0:T(8,128)S(1)}, f32[72,128]{1,0:T(8,128)S(1)}, u32[]{:S(2)}, u32[]{:S(2)}) collective-permute-start(f32[72,128]{1,0:T(8,128)S(1)} %add.20), channel_id=1, source_target_pairs={{0,24},{1,25},{2,26},{3,27},{4,28},{5,29},{6,30},{7,31},{8,16},{9,... | collective-permute-start | bytes 110600 | tf_op jit(solution)/shard_map/ppermute | solution.py:331
  52.3 4.0 %collective-permute-start.10 = (f32[72,128]{1,0:T(8,128)S(1)}, f32[72,128]{1,0:T(8,128)S(1)}, u32[]{:S(2)}, u32[]{:S(2)}) collective-permute-start(f32[72,128]{1,0:T(8,128)S(1)} %add.20), channel_id=1, source_target_pairs={{0,16},{1,17},{2,18},{3,19},{4,20},{5,21},{6,22},{7,23},{8,24},{9,... | collective-permute-start | bytes 110600 | tf_op jit(solution)/shard_map/ppermute | solution.py:331
  53.0 4.0 %collective-permute-start.9 = (f32[72,128]{1,0:T(8,128)S(1)}, f32[72,128]{1,0:T(8,128)S(1)}, u32[]{:S(2)}, u32[]{:S(2)}) collective-permute-start(f32[72,128]{1,0:T(8,128)S(1)} %add.20), channel_id=1, source_target_pairs={{0,8},{1,9},{2,10},{3,11},{4,12},{5,13},{6,14},{7,15},{8,0},{9,1},... | collective-permute-start | bytes 110600 | tf_op jit(solution)/shard_map/ppermute | solution.py:331
  57.0 5.8 %collective-permute-start.14 = (f32[72,128]{1,0:T(8,128)S(1)}, f32[72,128]{1,0:T(8,128)S(1)}, u32[]{:S(2)}, u32[]{:S(2)}) collective-permute-start(f32[72,128]{1,0:T(8,128)S(1)} %add_add_fusion.refs_0_), channel_id=1, source_target_pairs={{0,6},{1,7},{2,4},{3,5},{4,2},{5,3},{6,0},{7,1},{8,14},{9,15},{10,... | collective-permute-start | bytes 110600 | tf_op jit(solution)/shard_map/ppermute | solution.py:331
  57.0 5.7 %collective-permute-start.13 = (f32[72,128]{1,0:T(8,128)S(1)}, f32[72,128]{1,0:T(8,128)S(1)}, u32[]{:S(2)}, u32[]{:S(2)}) collective-permute-start(f32[72,128]{1,0:T(8,128)S(1)} %add_add_fusion.refs_0_), channel_id=1, source_target_pairs={{0,4},{1,5},{2,6},{3,7},{4,0},{5,1},{6,2},{7,3},{8,12},{9,13},{10,... | collective-permute-start | bytes 110600 | tf_op jit(solution)/shard_map/ppermute | solution.py:331
  57.1 6.2 %collective-permute-start.12 = (f32[72,128]{1,0:T(8,128)S(1)}, f32[72,128]{1,0:T(8,128)S(1)}, u32[]{:S(2)}, u32[]{:S(2)}) collective-permute-start(f32[72,128]{1,0:T(8,128)S(1)} %add_add_fusion.refs_0_), channel_id=1, source_target_pairs={{0,2},{1,3},{2,0},{3,1},{4,6},{5,7},{6,4},{7,5},{8,10},{9,11},{10,... | collective-permute-start | bytes 110600 | tf_op jit(solution)/shard_map/ppermute | solution.py:331

commit v2 on v1

--- a/solution.py
+++ b/solution.py
@@ -58,8 +58,8 @@
     out_ref[s] = pack_side(side_ref, s, 0)
 
 
-def first_kernel(weight, inv_hbm, field_hbm, rows_hbm, pass_ref, side_ref, off_ref,
-                 inv_buf, field_buf, rows, inv_sems, field_sems, rows_sem):
+def first_kernel(weight, inv_hbm, field_hbm, rows_hbm, pass_ref, side_ref, off_ref, inv_buf,
+                 field_buf, rows, inv_sems, field_sems, rows_sem):
     count = field_buf.shape[0]
     rows_copy = pltpu.make_async_copy(rows_hbm, rows, rows_sem)
     rows_copy.start()
@@ -87,20 +87,15 @@
     gather_side(count - 1, parity, pass_ref, rows, side_ref, off_ref)
 
 
-def columns_kernel(inv_hbm, rows_hbm, rows_ref, coup_ref, near_ref, pass_ref, off_side_ref,
+def columns_kernel(rows_hbm, inv_ref, rows_ref, coup_ref, near_ref, pass_ref, off_side_ref,
                    high_cols_ref, low_cols_ref, pass0_ref, pass1_ref, off_ref, on0_ref, on1_ref, table_ref,
-                   inv_buf, on_side_ref, rows, inv_sems, rows_sem):
-    count, block_len = inv_buf.shape[:2]
+                   on_side_ref, rows, rows_sem):
+    count, block_len = inv_ref.shape[:2]
     iface_len = rows_ref.shape[2]
     quarter = block_len // 4
 
-    def copy(s):
-        return pltpu.make_async_copy(inv_hbm.at[s], inv_buf.at[s], inv_sems.at[s])
-
     rows_copy = pltpu.make_async_copy(rows_hbm, rows, rows_sem)
     rows_copy.start()
-    for s in range(count):
-        copy(s).start()
     parity = sub_parity()
     for spot, side in enumerate((parity, 1 - parity)):
         near = lax.rem(near_ref[pl.ds(side, 1), :], count)
@@ -110,7 +105,6 @@
     rows_copy.wait()
 
     def one_sub(s, carry):
-        copy(s).wait()
         gather_side(s, 1 - parity, pass_ref, rows, on_side_ref, on0_ref)
         on1_ref[s] = pack_side(on_side_ref, s, 1)
         off_ref[s] = pack_side(off_side_ref, s, 1)
@@ -125,7 +119,7 @@
             for ref in (rows_ref, coup_ref)
         )
         pick = (at == place).astype(f32).astype(bf16)
-        inv_high, inv_low = split(inv_buf[s])
+        inv_high, inv_low = split(inv_ref[s])
         high_cols_ref[s], low_cols_ref[s] = split((mm(inv_high, pick) + mm(inv_low, pick)) * coup)
         return carry
 
@@ -210,16 +204,21 @@
     return lower + lower.T
 
 
+def reciprocal(x):
+    guess = pl.reciprocal(x, approx=True)
+    return guess * (2.0 - x * guess)
+
+
 def four_pivots(a):
     det = a[0][0] * a[1][1] - a[1][0] * a[1][0]
-    inv = 1.0 / det
+    inv = reciprocal(det)
     p00, p01, p11 = a[1][1] * inv, -a[1][0] * inv, a[0][0] * inv
     g20, g21 = a[2][0] * p00 + a[2][1] * p01, a[2][0] * p01 + a[2][1] * p11
     g30, g31 = a[3][0] * p00 + a[3][1] * p01, a[3][0] * p01 + a[3][1] * p11
     s22 = a[2][2] - (g20 * a[2][0] + g21 * a[2][1])
     s32 = a[3][2] - (g30 * a[2][0] + g31 * a[2][1])
     s33 = a[3][3] - (g30 * a[3][0] + g31 * a[3][1])
-    inv = 1.0 / (s22 * s33 - s32 * s32)
+    inv = reciprocal(s22 * s33 - s32 * s32)
     q00, q01, q11 = s33 * inv, -s32 * inv, s22 * inv
 
     def solve(r):
@@ -348,15 +347,14 @@
     in_hbm = functools.partial(pltpu.with_memory_space_constraint, memory_space=pltpu.HBM)
     in_vmem = functools.partial(pltpu.with_memory_space_constraint, memory_space=pltpu.VMEM)
     sides = shape((sub_count, iface_len, vecs), f32)
-    first, off_side, off0 = call(
+    first, off_side, off0, inv_here = call(
         first_kernel,
-        (shape(fields.shape, f32), sides, packed),
+        (shape(fields.shape, f32), sides, packed, shape(blocks.shape, f32)),
         flops=8 * sub_count * block_len * block_len * vecs,
         moved=block_bytes + 3 * field_bytes,
-        in_specs=[smem, hbm, hbm, hbm],
-        out_specs=[vmem] * 3,
+        in_specs=[smem] + [hbm] * 3,
+        out_specs=[vmem] * 4,
         scratch_shapes=[
-            pltpu.VMEM(blocks.shape, f32),
             pltpu.VMEM(fields.shape, f32),
             pltpu.SMEM(iface_rows.shape, jnp.int32),
             pltpu.SemaphoreType.DMA((sub_count,)),
@@ -364,8 +362,8 @@
             pltpu.SemaphoreType.DMA,
         ],
         name="first_pass",
-    )(pole_weights, in_hbm(blocks), in_hbm(fields), in_hbm(iface_rows))
-    first, off_side = in_vmem(first), in_vmem(off_side)
+    )(pole_weights, *[in_hbm(v) for v in (blocks, fields, iface_rows)])
+    first, off_side, inv_here = (in_vmem(v) for v in (first, off_side, inv_here))
     across = [(s, (s + (1 if s % 2 else -1)) % groups) for s in range(groups)]
     inside = [(s, s ^ 1) for s in range(groups)]
     off_in0 = lax.ppermute(off0, "sub", across)
@@ -376,18 +374,17 @@
         (cols, cols, pass_half, pass_half, packed, packed, packed, shape((2, sub_count, 8, vecs), jnp.int32)),
         flops=8 * sub_count * block_len * block_len * iface_len,
         moved=2 * block_bytes,
-        in_specs=[hbm] * 2 + [vmem] * 5,
+        in_specs=[hbm] + [vmem] * 6,
         out_specs=[vmem] * 8,
         scratch_shapes=[
-            pltpu.VMEM(blocks.shape, f32),
             pltpu.VMEM(sides.shape, f32),
             pltpu.SMEM(iface_rows.shape, jnp.int32),
-            pltpu.SemaphoreType.DMA((sub_count,)),
             pltpu.SemaphoreType.DMA,
         ],
         name="interface_columns",
-    )(in_hbm(blocks), in_hbm(iface_rows), iface_rows, couplings, neighbors.T, first, off_side)
+    )(in_hbm(iface_rows), inv_here, iface_rows, couplings, neighbors.T, first, off_side)
     on_in0 = lax.ppermute(on0, "sub", inside)
+    off1, on1, off_in0 = lax.optimization_barrier((off1, on1, off_in0))
     halves = [(off_in0, on_in0), (lax.ppermute(off1, "sub", across), lax.ppermute(on1, "sub", inside))]
     cols_high, cols_low, pass0, pass1 = (in_vmem(v) for v in (cols_high, cols_low, pass0, pass1))
 

time: 68.4 us -> 70 us (1.023)
  starting transfers between devices: 19.5 us -> 21.3 us
    ppermute x1, starting transfers between devices: 0.69 us -> 2.56 us  [per_device(): lax.ppermute(off1, 'sub', across)]
    ppermute x1, waiting for transfers between devices: 0.83 us -> 0.01 us  [per_device(): on_in0 = lax.ppermute(on0, 'sub', inside)]
  transfers between devices with their start and end apart: 15 -> 15, of which waited for: 10 -> 10; matrix products, arithmetic and copies ran while one was open for 0% -> 0% of each run, Pallas kernels for 15% -> 14%
where the time goes in v2:
time: 70 us; the launch traced here: 69.7 us
  waiting for transfers between devices  26.1 us (37%)
  Pallas kernels  21.4 us (31%)
  starting transfers between devices  21.3 us (30%)
  between operations  0.77 us (1%)
    ppermute x11, waiting for transfers between devices, swap(): return lax.ppermute(value, ('pole', 'sub'), pairs)  20.6 us
    ppermute x11, starting transfers between devices, swap(): return lax.ppermute(value, ('pole', 'sub'), pairs)  14.2 us
    pallas_call x1, Pallas kernels, per_device(): call(first_kernel, (shape(fields.shape, f32), sides, packed, shape(blocks...  6.08 us
    pallas_call x1, Pallas kernels, per_device(): call(columns_kernel, (cols, cols, pass_half, pass_half, packed, packed, p...  5.81 us
    ppermute x1, waiting for transfers between devices, per_device(): lax.ppermute(off1, 'sub', across)  5.35 us
    pallas_call x1, Pallas kernels, per_device(): call(functools.partial(ortho_kernel, math.sqrt(total_rows)), shape((own_r...  5.3 us
    ppermute x1, starting transfers between devices, per_device(): off_in0 = lax.ppermute(off0, 'sub', across)  4.51 us
    pallas_call x4, Pallas kernels, per_device(): call(functools.partial(second_kernel, poles, sent), parts, flops=4 * sub_...  3.62 us
  transfers between devices with their start and end apart: 15, of which 10 were waited for; matrix products, arithmetic and copies ran while one was open for 0% of the time, Pallas kernels for 14%

profile of v2, /device:TPU:0, one launch (start us, length us, event | category | flops | bytes accessed | tf_op | source)
XLA Modules:
  0.0 69.7 jit_solution(1662049085345696769)
XLA Ops:
  0.7 6.1 %first_pass.1 = (f32[8,512,128]{2,1,0:T(8,128)S(1)}, f32[8,128,128]{2,1,0:T(8,128)S(1)}, f32[8,64,128]{2,1,0:T(8,128)S(1)}, f32[8,512,512]{2,1,0:T(8,128)S(1)}) custom-call(f32[1]{0:T(128)S(6)} %copy.7.weight, f32[8,512,512]{2,1,0:T(8,128)} %bitcast.4, f32[8,512,128]{2,1,0:T(8,128)} %bitcast.5, s32[8,2,128]{2,1,0:T(2,128)} %rows_ref.1), custom_call_target="tpu_custom_call" | custom-call | flops 2147483648 | bytes 14680064 | tf_op jit(solution)/shard_map/first_pass/pallas_call | solution.py:350
  6.8 4.5 %collective-permute-start = (f32[8,64,128]{2,1,0:T(8,128)S(1)}, f32[8,64,128]{2,1,0:T(8,128)S(1)}, u32[]{:S(2)}, u32[]{:S(2)}) collective-permute-start(f32[8,64,128]{2,1,0:T(8,128)S(1)} %get-tuple-element.31), channel_id=1, source_target_pairs={{0,7},{1,2},{2,1},{3,4},{4,3},{5,6},{6,5},{7,0},{8,15},{9,10},{10,... | collective-permute-start | bytes 786440 | tf_op jit(solution)/shard_map/ppermute | solution.py:369
  11.3 5.8 %interface_columns.1 = (bf16[8,512,256]{2,1,0:T(8,128)(2,1)S(1)}, bf16[8,512,256]{2,1,0:T(8,128)(2,1)S(1)}, f32[8,2,128,128]{3,2,1,0:T(8,128)S(1)}, f32[8,2,128,...) custom-call(s32[8,2,128]{2,1,0:T(2,128)} %rows_ref.1, ...), custom_call_target="tpu_custom_call" | custom-call | flops 2147483648 | bytes 16777216 | tf_op jit(solution)/shard_map/interface_columns/pallas_call | solution.py:372
  17.3 2.6 %collective-permute-start.4 = (f32[8,64,128]{2,1,0:T(8,128)S(1)}, f32[8,64,128]{2,1,0:T(8,128)S(1)}, u32[]{:S(2)}, u32[]{:S(2)}) collective-permute-start(f32[8,64,128]{2,1,0:T(8,128)S(1)} %get-tuple-element.35), channel_id=1, source_target_pairs={{0,7},{1,2},{2,1},{3,4},{4,3},{5,6},{6,5},{7,0},{8,15},{9,10},{10,... | collective-permute-start | bytes 786440 | tf_op jit(solution)/shard_map/ppermute | solution.py:388
  19.8 0.9 %second_pass.5 = f32[2,512,128]{2,1,0:T(8,128)S(1)} custom-call(s32[2,8,8,128]{3,2,1,0:T(8,128)S(1)} %get-tuple-element.25.table_ref, bf16[8,512,256]{2,1,0:T(8,128)(2,1)S(1)} %get-tuple-element.26.high_ref, bf16[8,512,256]{2,1,0:T(8,128)(2,1)S(1)} %get-tuple-element.27.low_ref, f32[8,2,128,128]{3,2,1,0:T(8,128)S(1)} %get-tuple-element.28.pass_ref, ...), custom_call_target="tpu_custom_call" | custom-call | flops 536870912 | bytes 4194304 | tf_op jit(solution)/shard_map/second_pass/pallas_call | solution.py:397
  20.7 1.5 %collective-permute-start.2 = (f32[2,512,128]{2,1,0:T(8,128)S(1)}, f32[2,512,128]{2,1,0:T(8,128)S(1)}, u32[]{:S(2)}, u32[]{:S(2)}) collective-permute-start(f32[2,512,128]{2,1,0:T(8,128)S(1)} %second_pass.5), channel_id=1, source_target_pairs={{0,8},{1,17},{2,10},{3,19},{4,12},{5,21},{6,14},{7,23},{8,0},{9,25... | collective-permute-start | bytes 1572872 | tf_op jit(solution)/shard_map/ppermute | solution.py:330
  22.3 5.4 %collective-permute-done.4.off_ref = f32[8,64,128]{2,1,0:T(8,128)S(1)} collective-permute-done((f32[8,64,128]{2,1,0:T(8,128)S(1)}, f32[8,64,128]{2,1,0:T(8,128)S(1)}, u32[]{:S(2)}, u32[]{:S(2)}) %collective-permute-start.4) | collective-permute-done | bytes 262176 | tf_op jit(solution)/shard_map/ppermute | solution.py:388
  27.6 0.9 %second_pass.7 = f32[2,512,128]{2,1,0:T(8,128)S(1)} custom-call(s32[2,8,8,128]{3,2,1,0:T(8,128)S(1)} %get-tuple-element.25.table_ref, bf16[8,512,256]{2,1,0:T(8,128)(2,1)S(1)} %get-tuple-element.26.high_ref, bf16[8,512,256]{2,1,0:T(8,128)(2,1)S(1)} %get-tuple-element.27.low_ref, f32[8,2,128,128]{3,2,1,0:T(8,128)S(1)} %get-tuple-element.34.pass_ref, ...), custom_call_target="tpu_custom_call" | custom-call | flops 536870912 | bytes 4194304 | tf_op jit(solution)/shard_map/second_pass/pallas_call | solution.py:397
  28.5 1.5 %collective-permute-start.6 = (f32[2,512,128]{2,1,0:T(8,128)S(1)}, f32[2,512,128]{2,1,0:T(8,128)S(1)}, u32[]{:S(2)}, u32[]{:S(2)}) collective-permute-start(f32[2,512,128]{2,1,0:T(8,128)S(1)} %second_pass.7), channel_id=1, source_target_pairs={{0,8},{1,17},{2,10},{3,19},{4,12},{5,21},{6,14},{7,23},{8,0},{9,25... | collective-permute-start | bytes 1572872 | tf_op jit(solution)/shard_map/ppermute | solution.py:330
  30.1 0.9 %second_pass.4 = f32[2,512,128]{2,1,0:T(8,128)S(1)} custom-call(s32[2,8,8,128]{3,2,1,0:T(8,128)S(1)} %get-tuple-element.25.table_ref, bf16[8,512,256]{2,1,0:T(8,128)(2,1)S(1)} %get-tuple-element.26.high_ref, bf16[8,512,256]{2,1,0:T(8,128)(2,1)S(1)} %get-tuple-element.27.low_ref, f32[8,2,128,128]{3,2,1,0:T(8,128)S(1)} %get-tuple-element.28.pass_ref, ...), custom_call_target="tpu_custom_call" | custom-call | flops 536870912 | bytes 4194304 | tf_op jit(solution)/shard_map/second_pass/pallas_call | solution.py:397
  31.0 0.9 %second_pass.6 = f32[2,512,128]{2,1,0:T(8,128)S(1)} custom-call(s32[2,8,8,128]{3,2,1,0:T(8,128)S(1)} %get-tuple-element.25.table_ref, bf16[8,512,256]{2,1,0:T(8,128)(2,1)S(1)} %get-tuple-element.26.high_ref, bf16[8,512,256]{2,1,0:T(8,128)(2,1)S(1)} %get-tuple-element.27.low_ref, f32[8,2,128,128]{3,2,1,0:T(8,128)S(1)} %get-tuple-element.34.pass_ref, ...), custom_call_target="tpu_custom_call" | custom-call | flops 536870912 | bytes 4194304 | tf_op jit(solution)/shard_map/second_pass/pallas_call | solution.py:397
  32.0 1.6 %collective-permute-start.3 = (f32[1,512,128]{2,1,0:T(8,128)S(1)}, f32[1,512,128]{2,1,0:T(8,128)S(1)}, u32[]{:S(2)}, u32[]{:S(2)}) collective-permute-start(f32[1,512,128]{2,1,0:T(8,128)S(1)} %get-tuple-element.42), channel_id=1, source_target_pairs={{0,16},{1,9},{2,18},{3,11},{4,20},{5,13},{6,22},{7,15},{8,24},{9,1... | collective-permute-start | bytes 786440 | tf_op jit(solution)/shard_map/ppermute | solution.py:330
  33.6 9.4 %collective-permute-done.6 = f32[2,512,128]{2,1,0:T(8,128)S(1)} collective-permute-done((f32[2,512,128]{2,1,0:T(8,128)S(1)}, f32[2,512,128]{2,1,0:T(8,128)S(1)}, u32[]{:S(2)}, u32[]{:S(2)}) %collective-permute-start.6) | collective-permute-done | bytes 524320 | tf_op jit(solution)/shard_map/ppermute | solution.py:330
  43.1 1.5 %collective-permute-start.7 = (f32[1,512,128]{2,1,0:T(8,128)S(1)}, f32[1,512,128]{2,1,0:T(8,128)S(1)}, u32[]{:S(2)}, u32[]{:S(2)}) collective-permute-start(f32[1,512,128]{2,1,0:T(8,128)S(1)} %get-tuple-element.39), channel_id=1, source_target_pairs={{0,16},{1,9},{2,18},{3,11},{4,20},{5,13},{6,22},{7,15},{8,24},{9,1... | collective-permute-start | bytes 786440 | tf_op jit(solution)/shard_map/ppermute | solution.py:330
  44.6 4.9 %collective-permute-done.7.refs_5_ = f32[1,512,128]{2,1,0:T(8,128)S(1)} collective-permute-done((f32[1,512,128]{2,1,0:T(8,128)S(1)}, f32[1,512,128]{2,1,0:T(8,128)S(1)}, u32[]{:S(2)}, u32[]{:S(2)}) %collective-permute-start.7) | collective-permute-done | bytes 262176 | tf_op jit(solution)/shard_map/ppermute | solution.py:330
  50.2 1.2 %collective-permute-done.8 = f32[72,128]{1,0:T(8,128)S(1)} collective-permute-done((f32[72,128]{1,0:T(8,128)S(1)}, f32[72,128]{1,0:T(8,128)S(1)}, u32[]{:S(2)}, u32[]{:S(2)}) %collective-permute-start.8) | collective-permute-done | bytes 36896 | tf_op jit(solution)/shard_map/ppermute | solution.py:330
  51.4 2.1 %collective-permute-start.11 = (f32[72,128]{1,0:T(8,128)S(1)}, f32[72,128]{1,0:T(8,128)S(1)}, u32[]{:S(2)}, u32[]{:S(2)}) collective-permute-start(f32[72,128]{1,0:T(8,128)S(1)} %add.20), channel_id=1, source_target_pairs={{0,24},{1,25},{2,26},{3,27},{4,28},{5,29},{6,30},{7,31},{8,16},{9,... | collective-permute-start | bytes 110600 | tf_op jit(solution)/shard_map/ppermute | solution.py:330
  54.0 0.8 %collective-permute-start.9 = (f32[72,128]{1,0:T(8,128)S(1)}, f32[72,128]{1,0:T(8,128)S(1)}, u32[]{:S(2)}, u32[]{:S(2)}) collective-permute-start(f32[72,128]{1,0:T(8,128)S(1)} %add.20), channel_id=1, source_target_pairs={{0,8},{1,9},{2,10},{3,11},{4,12},{5,13},{6,14},{7,15},{8,0},{9,1},... | collective-permute-start | bytes 110600 | tf_op jit(solution)/shard_map/ppermute | solution.py:330
  54.9 1.4 %collective-permute-done.11 = f32[72,128]{1,0:T(8,128)S(1)} collective-permute-done((f32[72,128]{1,0:T(8,128)S(1)}, f32[72,128]{1,0:T(8,128)S(1)}, u32[]{:S(2)}, u32[]{:S(2)}) %collective-permute-start.11) | collective-permute-done | bytes 36896 | tf_op jit(solution)/shard_map/ppermute | solution.py:330
  56.3 1.2 %collective-permute-done.10 = f32[72,128]{1,0:T(8,128)S(1)} collective-permute-done((f32[72,128]{1,0:T(8,128)S(1)}, f32[72,128]{1,0:T(8,128)S(1)}, u32[]{:S(2)}, u32[]{:S(2)}) %collective-permute-start.10) | collective-permute-done | bytes 36896 | tf_op jit(solution)/shard_map/ppermute | solution.py:330
  58.5 4.0 %collective-permute-start.12 = (f32[72,128]{1,0:T(8,128)S(1)}, f32[72,128]{1,0:T(8,128)S(1)}, u32[]{:S(2)}, u32[]{:S(2)}) collective-permute-start(f32[72,128]{1,0:T(8,128)S(1)} %add_add_fusion.refs_0_), channel_id=1, source_target_pairs={{0,2},{1,3},{2,0},{3,1},{4,6},{5,7},{6,4},{7,5},{8,10},{9,11},{10,... | collective-permute-start | bytes 110600 | tf_op jit(solution)/shard_map/ppermute | solution.py:330
  62.5 1.4 %collective-permute-done.14.refs_3_ = f32[72,128]{1,0:T(8,128)S(1)} collective-permute-done((f32[72,128]{1,0:T(8,128)S(1)}, f32[72,128]{1,0:T(8,128)S(1)}, u32[]{:S(2)}, u32[]{:S(2)}) %collective-permute-start.14) | collective-permute-done | bytes 36896 | tf_op jit(solution)/shard_map/ppermute | solution.py:330
  63.8 0.6 collective-permute-done.12.refs_1_
  64.4 5.3 %ortho.1 = f32[1024,128]{1,0:T(8,128)} custom-call(f32[72,128]{1,0:T(8,128)S(1)} %add_add_fusion.refs_0_, f32[72,128]{1,0:T(8,128)S(1)} %collective-permute-done.12.refs_1_, f32[72,128]{1,0:T(8,128)S(1)} %collective-permute-done.13.refs_2_, f32[72,128]{1,0:T(8,128)S(1)} %collective-permute-done.14.refs_3_, bf16[1024,256]{1,0:T(8,128)(2,1)S(1)} %get-tuple-element.38.refs_4_), custom_call_target="tpu_custom_call" | custom-call | flops 100663296 | bytes 1048576 | tf_op jit(solution)/shard_map/ortho/pallas_call | solution.py:445
  (22 shorter events, 2.5 us)
Async XLA Ops:
  0.7 10.6 %copy-start = (f32[8,2,128]{2,1,0:T(2,128)S(1)}, f32[8,2,128]{2,1,0:T(2,128)}, u32[]{:S(2)}) copy-start(f32[8,2,128]{2,1,0:T(2,128)} %coup_ref.1) | copy-start | bytes 24580
  0.7 10.6 %copy-start.1 = (s32[8,2]{0,1:T(2,128)S(1)}, s32[8,2]{0,1:T(2,128)}, u32[]{:S(2)}) copy-start(s32[8,2]{0,1:T(2,128)} %param.9) | copy-start | bytes 196
  6.8 10.5 %collective-permute-start = (f32[8,64,128]{2,1,0:T(8,128)S(1)}, f32[8,64,128]{2,1,0:T(8,128)S(1)}, u32[]{:S(2)}, u32[]{:S(2)}) collective-permute-start(f32[8,64,128]{2,1,0:T(8,128)S(1)} %get-tuple-element.31), channel_id=1, source_target_pairs={{0,7},{1,2},{2,1},{3,4},{4,3},{5,6},{6,5},{7,0},{8,15},{9,10},{10,... | collective-permute-start | bytes 786440 | tf_op jit(solution)/shard_map/ppermute | solution.py:369
  17.1 2.7 %collective-permute-start.1 = (f32[8,64,128]{2,1,0:T(8,128)S(1)}, f32[8,64,128]{2,1,0:T(8,128)S(1)}, u32[]{:S(2)}, u32[]{:S(2)}) collective-permute-start(f32[8,64,128]{2,1,0:T(8,128)S(1)} %get-tuple-element.33), channel_id=1, source_target_pairs={{0,1},{1,0},{2,3},{3,2},{4,5},{5,4},{6,7},{7,6},{8,9},{9,8},{10,11... | collective-permute-start | bytes 786440 | tf_op jit(solution)/shard_map/ppermute | solution.py:386
  17.3 10.4 %collective-permute-start.4 = (f32[8,64,128]{2,1,0:T(8,128)S(1)}, f32[8,64,128]{2,1,0:T(8,128)S(1)}, u32[]{:S(2)}, u32[]{:S(2)}) collective-permute-start(f32[8,64,128]{2,1,0:T(8,128)S(1)} %get-tuple-element.35), channel_id=1, source_target_pairs={{0,7},{1,2},{2,1},{3,4},{4,3},{5,6},{6,5},{7,0},{8,15},{9,10},{10,... | collective-permute-start | bytes 786440 | tf_op jit(solution)/shard_map/ppermute | solution.py:388
  19.8 7.8 %collective-permute-start.5 = (f32[8,64,128]{2,1,0:T(8,128)S(1)}, f32[8,64,128]{2,1,0:T(8,128)S(1)}, u32[]{:S(2)}, u32[]{:S(2)}) collective-permute-start(f32[8,64,128]{2,1,0:T(8,128)S(1)} %get-tuple-element.36), channel_id=1, source_target_pairs={{0,1},{1,0},{2,3},{3,2},{4,5},{5,4},{6,7},{7,6},{8,9},{9,8},{10,11... | collective-permute-start | bytes 786440 | tf_op jit(solution)/shard_map/ppermute | solution.py:388
  20.7 11.2 %collective-permute-start.2 = (f32[2,512,128]{2,1,0:T(8,128)S(1)}, f32[2,512,128]{2,1,0:T(8,128)S(1)}, u32[]{:S(2)}, u32[]{:S(2)}) collective-permute-start(f32[2,512,128]{2,1,0:T(8,128)S(1)} %second_pass.5), channel_id=1, source_target_pairs={{0,8},{1,17},{2,10},{3,19},{4,12},{5,21},{6,14},{7,23},{8,0},{9,25... | collective-permute-start | bytes 1572872 | tf_op jit(solution)/shard_map/ppermute | solution.py:330
  28.5 14.5 %collective-permute-start.6 = (f32[2,512,128]{2,1,0:T(8,128)S(1)}, f32[2,512,128]{2,1,0:T(8,128)S(1)}, u32[]{:S(2)}, u32[]{:S(2)}) collective-permute-start(f32[2,512,128]{2,1,0:T(8,128)S(1)} %second_pass.7), channel_id=1, source_target_pairs={{0,8},{1,17},{2,10},{3,19},{4,12},{5,21},{6,14},{7,23},{8,0},{9,25... | collective-permute-start | bytes 1572872 | tf_op jit(solution)/shard_map/ppermute | solution.py:330
  32.0 12.6 %collective-permute-start.3 = (f32[1,512,128]{2,1,0:T(8,128)S(1)}, f32[1,512,128]{2,1,0:T(8,128)S(1)}, u32[]{:S(2)}, u32[]{:S(2)}) collective-permute-start(f32[1,512,128]{2,1,0:T(8,128)S(1)} %get-tuple-element.42), channel_id=1, source_target_pairs={{0,16},{1,9},{2,18},{3,11},{4,20},{5,13},{6,22},{7,15},{8,24},{9,1... | collective-permute-start | bytes 786440 | tf_op jit(solution)/shard_map/ppermute | solution.py:330
  43.1 6.4 %collective-permute-start.7 = (f32[1,512,128]{2,1,0:T(8,128)S(1)}, f32[1,512,128]{2,1,0:T(8,128)S(1)}, u32[]{:S(2)}, u32[]{:S(2)}) collective-permute-start(f32[1,512,128]{2,1,0:T(8,128)S(1)} %get-tuple-element.39), channel_id=1, source_target_pairs={{0,16},{1,9},{2,18},{3,11},{4,20},{5,13},{6,22},{7,15},{8,24},{9,1... | collective-permute-start | bytes 786440 | tf_op jit(solution)/shard_map/ppermute | solution.py:330
  50.1 1.3 %collective-permute-start.8 = (f32[72,128]{1,0:T(8,128)S(1)}, f32[72,128]{1,0:T(8,128)S(1)}, u32[]{:S(2)}, u32[]{:S(2)}) collective-permute-start(f32[72,128]{1,0:T(8,128)S(1)} %get-tuple-element.37), channel_id=1, source_target_pairs={{0,1},{1,0},{2,3},{3,2},{4,5},{5,4},{6,7},{7,6},{8,9},{9,8},{10,11... | collective-permute-start | bytes 110600 | tf_op jit(solution)/shard_map/ppermute | solution.py:330
  51.4 4.9 %collective-permute-start.11 = (f32[72,128]{1,0:T(8,128)S(1)}, f32[72,128]{1,0:T(8,128)S(1)}, u32[]{:S(2)}, u32[]{:S(2)}) collective-permute-start(f32[72,128]{1,0:T(8,128)S(1)} %add.20), channel_id=1, source_target_pairs={{0,24},{1,25},{2,26},{3,27},{4,28},{5,29},{6,30},{7,31},{8,16},{9,... | collective-permute-start | bytes 110600 | tf_op jit(solution)/shard_map/ppermute | solution.py:330
  53.5 4.0 %collective-permute-start.10 = (f32[72,128]{1,0:T(8,128)S(1)}, f32[72,128]{1,0:T(8,128)S(1)}, u32[]{:S(2)}, u32[]{:S(2)}) collective-permute-start(f32[72,128]{1,0:T(8,128)S(1)} %add.20), channel_id=1, source_target_pairs={{0,16},{1,17},{2,18},{3,19},{4,20},{5,21},{6,22},{7,23},{8,24},{9,... | collective-permute-start | bytes 110600 | tf_op jit(solution)/shard_map/ppermute | solution.py:330
  54.0 4.0 %collective-permute-start.9 = (f32[72,128]{1,0:T(8,128)S(1)}, f32[72,128]{1,0:T(8,128)S(1)}, u32[]{:S(2)}, u32[]{:S(2)}) collective-permute-start(f32[72,128]{1,0:T(8,128)S(1)} %add.20), channel_id=1, source_target_pairs={{0,8},{1,9},{2,10},{3,11},{4,12},{5,13},{6,14},{7,15},{8,0},{9,1},... | collective-permute-start | bytes 110600 | tf_op jit(solution)/shard_map/ppermute | solution.py:330
  58.0 5.8 %collective-permute-start.14 = (f32[72,128]{1,0:T(8,128)S(1)}, f32[72,128]{1,0:T(8,128)S(1)}, u32[]{:S(2)}, u32[]{:S(2)}) collective-permute-start(f32[72,128]{1,0:T(8,128)S(1)} %add_add_fusion.refs_0_), channel_id=1, source_target_pairs={{0,6},{1,7},{2,4},{3,5},{4,2},{5,3},{6,0},{7,1},{8,14},{9,15},{10,... | collective-permute-start | bytes 110600 | tf_op jit(solution)/shard_map/ppermute | solution.py:330
  58.5 5.4 %collective-permute-start.13 = (f32[72,128]{1,0:T(8,128)S(1)}, f32[72,128]{1,0:T(8,128)S(1)}, u32[]{:S(2)}, u32[]{:S(2)}) collective-permute-start(f32[72,128]{1,0:T(8,128)S(1)} %add_add_fusion.refs_0_), channel_id=1, source_target_pairs={{0,4},{1,5},{2,6},{3,7},{4,0},{5,1},{6,2},{7,3},{8,12},{9,13},{10,... | collective-permute-start | bytes 110600 | tf_op jit(solution)/shard_map/ppermute | solution.py:330
  58.5 5.9 %collective-permute-start.12 = (f32[72,128]{1,0:T(8,128)S(1)}, f32[72,128]{1,0:T(8,128)S(1)}, u32[]{:S(2)}, u32[]{:S(2)}) collective-permute-start(f32[72,128]{1,0:T(8,128)S(1)} %add_add_fusion.refs_0_), channel_id=1, source_target_pairs={{0,2},{1,3},{2,0},{3,1},{4,6},{5,7},{6,4},{7,5},{8,10},{9,11},{10,... | collective-permute-start | bytes 110600 | tf_op jit(solution)/shard_map/ppermute | solution.py:330

commit v3 on v2

--- a/solution.py
+++ b/solution.py
@@ -1,4 +1,5 @@
 import functools
+import itertools
 import math
 
 import jax
@@ -58,8 +59,8 @@
     out_ref[s] = pack_side(side_ref, s, 0)
 
 
-def first_kernel(weight, inv_hbm, field_hbm, rows_hbm, pass_ref, side_ref, off_ref, inv_buf,
-                 field_buf, rows, inv_sems, field_sems, rows_sem):
+def first_kernel(weight, inv_hbm, field_hbm, rows_hbm, pass_ref, side_ref, off_ref, inv_high_ref, inv_low_ref,
+                 inv_buf, field_buf, rows, inv_sems, field_sems, rows_sem):
     count = field_buf.shape[0]
     rows_copy = pltpu.make_async_copy(rows_hbm, rows, rows_sem)
     rows_copy.start()
@@ -80,17 +81,18 @@
         for copy in copies(s):
             copy.wait()
         gather_side(jnp.maximum(s - 1, 0), parity, pass_ref, rows, side_ref, off_ref)
-        pass_ref[s] = weight[0] * split_dot(split(inv_buf[s]), field_buf[s])
+        inv_high_ref[s], inv_low_ref[s] = parts = split(inv_buf[s])
+        pass_ref[s] = weight[0] * split_dot(parts, field_buf[s])
         return carry
 
     lax.fori_loop(0, count, one_sub, 0)
     gather_side(count - 1, parity, pass_ref, rows, side_ref, off_ref)
 
 
-def columns_kernel(rows_hbm, inv_ref, rows_ref, coup_ref, near_ref, pass_ref, off_side_ref,
+def columns_kernel(rows_hbm, inv_high_ref, inv_low_ref, rows_ref, coup_ref, near_ref, pass_ref, off_side_ref,
                    high_cols_ref, low_cols_ref, pass0_ref, pass1_ref, off_ref, on0_ref, on1_ref, table_ref,
                    on_side_ref, rows, rows_sem):
-    count, block_len = inv_ref.shape[:2]
+    count, block_len = inv_high_ref.shape[:2]
     iface_len = rows_ref.shape[2]
     quarter = block_len // 4
 
@@ -119,60 +121,72 @@
             for ref in (rows_ref, coup_ref)
         )
         pick = (at == place).astype(f32).astype(bf16)
-        inv_high, inv_low = split(inv_ref[s])
-        high_cols_ref[s], low_cols_ref[s] = split((mm(inv_high, pick) + mm(inv_low, pick)) * coup)
+        high_cols_ref[s], low_cols_ref[s] = split((mm(inv_high_ref[s], pick) + mm(inv_low_ref[s], pick)) * coup)
         return carry
 
     lax.fori_loop(0, count, one_sub, 0)
 
 
-def second_kernel(poles, sent, table_ref, high_ref, low_ref, pass_ref, off_ref, on_ref, out_ref):
+def second_kernel(poles, sent, table_ref, high_ref, low_ref, pass_ref, off_ref, on_ref, *out_refs):
     count, ways, quarter, _ = pass_ref.shape
     per_owner = count // poles
     steps = poles.bit_length() - 1
     me, parity = lax.axis_index("pole"), sub_parity()
+    split_ways = len(out_refs) == ways
     for r in range(sent, poles, 2):
         turned = sum(1 << (steps - 1 - step) for step in range(steps) if r >> step & 1)
-        owner = me ^ jnp.where(parity == 0, r, turned)
+        if split_ways:
+            owners = [(me ^ r, [0]), (me ^ turned, [1])]
+        else:
+            owners = [(me ^ jnp.where(parity == 0, r, turned), [0, 1])]
         for c in range(per_owner):
-            sub = owner * per_owner + c
-            terms = []
-            for spot, ref in enumerate((off_ref, on_ref)):
-                near = jnp.concatenate([table_ref[spot, sub]] * (ref.shape[1] // 8), axis=0)
-                side = ref[0]
-                for at in range(1, count):
-                    side = jnp.where(near == at, ref[at], side)
-                turned_side = turn(side)
-                terms += [
-                    jnp.where(left_lanes(side), side, turned_side),
-                    jnp.where(left_lanes(side), turned_side, side),
-                ]
-            terms = jnp.concatenate(terms, axis=0)
-            high = terms.astype(bf16).astype(f32)
-            both = jnp.where(left_lanes(terms), high, terms - high).astype(bf16)
-            out = mm(high_ref[sub], both) + mm(low_ref[sub], both)
-            out = out + turn(out)
-            for way in range(ways):
-                at = 2 * way * quarter
-                top, bottom = out[at : at + quarter], out[at + quarter : at + 2 * quarter]
-                to = (c * ways + way) * quarter
-                out_ref[r // 2, to : to + quarter, :] = (
-                    jnp.where(left_lanes(top), top, bottom) + pass_ref[sub, way]
-                )
-
-
-def gram_kernel(groups, per_owner, *refs):
-    count = sum(groups)
+            for owner, own_ways in owners:
+                sub = owner * per_owner + c
+                terms = []
+                for spot, ref in enumerate((off_ref, on_ref)):
+                    near = jnp.concatenate([table_ref[spot, sub]] * (ref.shape[1] // 8), axis=0)
+                    side = ref[0]
+                    for at in range(1, count):
+                        side = jnp.where(near == at, ref[at], side)
+                    turned_side = turn(side)
+                    terms += [
+                        jnp.where(left_lanes(side), side, turned_side),
+                        jnp.where(left_lanes(side), turned_side, side),
+                    ]
+                terms = jnp.concatenate(terms, axis=0)
+                high = terms.astype(bf16).astype(f32)
+                both = jnp.where(left_lanes(terms), high, terms - high).astype(bf16)
+                start, stop = 2 * own_ways[0] * quarter, 2 * (own_ways[-1] + 1) * quarter
+                out = mm(high_ref[sub, start:stop, :], both) + mm(low_ref[sub, start:stop, :], both)
+                out = out + turn(out)
+                for spot, way in enumerate(own_ways):
+                    at = 2 * spot * quarter
+                    top, bottom = out[at : at + quarter], out[at + quarter : at + 2 * quarter]
+                    to = (c * len(own_ways) + spot) * quarter
+                    out_refs[way if split_ways else 0][r // 2, to : to + quarter, :] = (
+                        jnp.where(left_lanes(top), top, bottom) + pass_ref[sub, way]
+                    )
+
+
+def gram_kernel(halves, per_owner, *refs):
+    count = sum(size for sizes in halves for size in sizes)
     ins, (halves_ref, gram_ref, out_ref) = refs[:count], refs[count:]
     parts = []
     at = 0
-    for size in groups:
-        parts.append(functools.reduce(jnp.add, [ref[0] for ref in ins[at : at + size]]))
-        at += size
+    for sizes in halves:
+        parts.append([])
+        for size in sizes:
+            parts[-1].append(functools.reduce(jnp.add, [ref[0] for ref in ins[at : at + size]]))
+            at += size
     quarter = out_ref.shape[0] // (4 * per_owner)
+
+    def piece(arrays, c, way):
+        spot = c if len(arrays) == 2 else 2 * c + way
+        return arrays[way % len(arrays)][spot * quarter : (spot + 1) * quarter]
+
     for way in range(2):
         for c in range(per_owner):
-            first, second = (part[(2 * c + way) * quarter : (2 * c + way + 1) * quarter] for part in parts)
+            first, second = (piece(arrays, c, way) for arrays in parts)
             at = (4 * c + 2 * way) * quarter
             out_ref[at : at + quarter, :] = jnp.where(left_lanes(first), first, turn(second))
             out_ref[at + quarter : at + 2 * quarter, :] = jnp.where(left_lanes(first), turn(first), second)
@@ -191,6 +205,12 @@
     gram_ref[half:, :] = jnp.broadcast_to(diag, (gram_ref.shape[0] - half, width))
 
 
+def share_kernel(total_ref, *refs):
+    *got_refs, out_ref = refs
+    own = jnp.where(sub_parity() == 0, total_ref[...], 0.0)
+    out_ref[...] = functools.reduce(jnp.add, [ref[...] for ref in got_refs], own)
+
+
 def unpacked(gram):
     width = gram.shape[1]
     half = width // 2
@@ -204,21 +224,16 @@
     return lower + lower.T
 
 
-def reciprocal(x):
-    guess = pl.reciprocal(x, approx=True)
-    return guess * (2.0 - x * guess)
-
-
 def four_pivots(a):
     det = a[0][0] * a[1][1] - a[1][0] * a[1][0]
-    inv = reciprocal(det)
+    inv = 1.0 / det
     p00, p01, p11 = a[1][1] * inv, -a[1][0] * inv, a[0][0] * inv
     g20, g21 = a[2][0] * p00 + a[2][1] * p01, a[2][0] * p01 + a[2][1] * p11
     g30, g31 = a[3][0] * p00 + a[3][1] * p01, a[3][0] * p01 + a[3][1] * p11
     s22 = a[2][2] - (g20 * a[2][0] + g21 * a[2][1])
     s32 = a[3][2] - (g30 * a[2][0] + g31 * a[2][1])
     s33 = a[3][3] - (g30 * a[3][0] + g31 * a[3][1])
-    inv = reciprocal(s22 * s33 - s32 * s32)
+    inv = 1.0 / (s22 * s33 - s32 * s32)
     q00, q01, q11 = s33 * inv, -s32 * inv, s22 * inv
 
     def solve(r):
@@ -325,8 +340,9 @@
     pairs = []
     for p in range(poles):
         for s in range(groups):
-            pole_mask, sub_mask = odd if s % 2 else even
-            pairs.append((p * groups + s, (p ^ pole_mask) * groups + (s ^ sub_mask)))
+            masks = odd if s % 2 else even
+            if masks:
+                pairs.append((p * groups + s, (p ^ masks[0]) * groups + (s ^ masks[1])))
     return lax.ppermute(value, ("pole", "sub"), pairs)
 
 
@@ -347,14 +363,16 @@
     in_hbm = functools.partial(pltpu.with_memory_space_constraint, memory_space=pltpu.HBM)
     in_vmem = functools.partial(pltpu.with_memory_space_constraint, memory_space=pltpu.VMEM)
     sides = shape((sub_count, iface_len, vecs), f32)
-    first, off_side, off0, inv_here = call(
+    halves = shape(blocks.shape, bf16)
+    first, off_side, off0, inv_high, inv_low = call(
         first_kernel,
-        (shape(fields.shape, f32), sides, packed, shape(blocks.shape, f32)),
+        (shape(fields.shape, f32), sides, packed, halves, halves),
         flops=8 * sub_count * block_len * block_len * vecs,
         moved=block_bytes + 3 * field_bytes,
         in_specs=[smem] + [hbm] * 3,
-        out_specs=[vmem] * 4,
+        out_specs=[vmem] * 5,
         scratch_shapes=[
+            pltpu.VMEM(blocks.shape, f32),
             pltpu.VMEM(fields.shape, f32),
             pltpu.SMEM(iface_rows.shape, jnp.int32),
             pltpu.SemaphoreType.DMA((sub_count,)),
@@ -363,7 +381,7 @@
         ],
         name="first_pass",
     )(pole_weights, *[in_hbm(v) for v in (blocks, fields, iface_rows)])
-    first, off_side, inv_here = (in_vmem(v) for v in (first, off_side, inv_here))
+    first, off_side, inv_high, inv_low = (in_vmem(v) for v in (first, off_side, inv_high, inv_low))
     across = [(s, (s + (1 if s % 2 else -1)) % groups) for s in range(groups)]
     inside = [(s, s ^ 1) for s in range(groups)]
     off_in0 = lax.ppermute(off0, "sub", across)
@@ -374,7 +392,7 @@
         (cols, cols, pass_half, pass_half, packed, packed, packed, shape((2, sub_count, 8, vecs), jnp.int32)),
         flops=8 * sub_count * block_len * block_len * iface_len,
         moved=2 * block_bytes,
-        in_specs=[hbm] + [vmem] * 6,
+        in_specs=[hbm] + [vmem] * 7,
         out_specs=[vmem] * 8,
         scratch_shapes=[
             pltpu.VMEM(sides.shape, f32),
@@ -382,64 +400,70 @@
             pltpu.SemaphoreType.DMA,
         ],
         name="interface_columns",
-    )(in_hbm(iface_rows), inv_here, iface_rows, couplings, neighbors.T, first, off_side)
+    )(in_hbm(iface_rows), inv_high, inv_low, iface_rows, couplings, neighbors.T, first, off_side)
     on_in0 = lax.ppermute(on0, "sub", inside)
-    off1, on1, off_in0 = lax.optimization_barrier((off1, on1, off_in0))
+    on1, off_in0 = lax.optimization_barrier((on1, off_in0))
     halves = [(off_in0, on_in0), (lax.ppermute(off1, "sub", across), lax.ppermute(on1, "sub", inside))]
     cols_high, cols_low, pass0, pass1 = (in_vmem(v) for v in (cols_high, cols_low, pass0, pass1))
 
     per_owner = sub_count // poles
     steps = poles.bit_length() - 1
-    parts = shape((poles // 2, per_owner * block_len // 2, vecs), f32)
     pending = []
-    for own_pass, (off_in, on_in) in zip((pass0, pass1), halves):
+    for arrays, own_pass, (off_in, on_in) in zip((1, 2), (pass0, pass1), halves):
         send, keep = (
             call(
                 functools.partial(second_kernel, poles, sent),
-                parts,
+                (shape((poles // 2, per_owner * block_len // (2 * arrays), vecs), f32),) * arrays,
                 flops=4 * sub_count * block_len * 2 * iface_len * vecs,
                 moved=2 * sub_count * block_len * vecs * 4,
                 in_specs=[vmem] * 6,
-                out_specs=vmem,
+                out_specs=[vmem] * arrays,
                 name="second_pass",
             )(table, cols_high, cols_low, own_pass, off_in, on_in)
             for sent in (1, 0)
         )
-        pending.append((send, [keep]))
+        pending.append([(a, [b]) for a, b in zip(send, keep)])
 
     for step in range(steps):
-        masks = (1 << step, 0), (1 << (steps - 1 - step), 0)
-        for half, (send, kept) in enumerate(pending):
-            kept = kept + [swap(send, *masks)]
-            if kept[0].shape[0] > 1:
-                send = functools.reduce(jnp.add, [v[1::2] for v in kept])
-                kept = [v[0::2] for v in kept]
-            pending[half] = (send, kept)
-
-    summands = [kept for _, kept in pending]
-    sizes = tuple(len(kept) for kept in summands)
+        in_order, turned = (1 << step, 0), (1 << (steps - 1 - step), 0)
+        for arrays in pending:
+            for way, (send, kept) in enumerate(arrays):
+                masks = (in_order, turned) if len(arrays) == 1 else ((in_order, turned)[way],) * 2
+                kept = kept + [swap(send, *masks)]
+                if kept[0].shape[0] > 1:
+                    send = functools.reduce(jnp.add, [v[1::2] for v in kept])
+                    kept = [v[0::2] for v in kept]
+                arrays[way] = (send, kept)
+
+    summands = [[kept for _, kept in arrays] for arrays in pending]
+    sizes = tuple(tuple(len(kept) for kept in arrays) for arrays in summands)
     own_rows = per_owner * block_len
     basis_halves, gram = call(
         functools.partial(gram_kernel, sizes, per_owner),
         (shape((own_rows, 2 * vecs), bf16), shape((vecs // 2 + 8, vecs), f32)),
         flops=4 * own_rows * vecs * vecs,
         moved=5 * own_rows * vecs * 4,
-        in_specs=[vmem] * sum(sizes),
+        in_specs=[vmem] * sum(map(sum, sizes)),
         out_specs=[vmem] * 2,
         scratch_shapes=[pltpu.VMEM((own_rows, vecs), f32)],
         name="gram",
-    )(*[v for kept in summands for v in kept])
-
-    stages = [[(0, 1)], [(r, 0) for r in range(1, poles)]]
+    )(*[v for arrays in summands for kept in arrays for v in kept])
+
+    stages = [[(r, 0) for r in range(poles - 1, 0, -1)]]
     base = 2
     while base < groups:
         radix = min(4, groups // base)
-        stages.append([(0, base * r) for r in range(1, radix)])
+        stages.append([(0, base * r) for r in range(radix - 1, 0, -1)])
         base *= radix
-    grams = [gram]
+    inside_chip = ((0, 1), (0, 1))
+    grams = [gram, swap(gram, *inside_chip)]
     for masks in stages:
         total = functools.reduce(jnp.add, grams)
-        grams = [total] + [swap(total, m, m) for m in masks]
+        got = [
+            swap(total, even, odd) for even, odd in itertools.zip_longest(masks[0::2], masks[1::2])
+        ]
+        share = call(share_kernel, shape(gram.shape, f32), name="gram_share")(total, *got)
+        grams = [share, swap(share, *inside_chip)]
 
     total_rows = sub_count * block_len * groups
     return call(

time: 70 us -> 69.1 us (0.987)
  waiting for transfers between devices: 26.1 us -> 24.1 us
  starting transfers between devices: 21.3 us -> 22.9 us
    ppermute x11 -> x13, starting transfers between devices: 14.2 us -> 17.6 us  [swap(): return lax.ppermute(value, ('pole', 'sub'), pairs)]
    ppermute x11 -> x13, waiting for transfers between devices: 20.6 us -> 17.7 us  [swap(): return lax.ppermute(value, ('pole', 'sub'), pairs)]
    ppermute x1, starting transfers between devices: 2.56 us -> 0.67 us  [per_device(): lax.ppermute(off1, 'sub', across)]
    ppermute x1, waiting for transfers between devices: 0.01 us -> 0.84 us  [per_device(): on_in0 = lax.ppermute(on0, 'sub', inside)]
    pallas_call x5 -> x7, Pallas kernels: 9.7 us -> 9.81 us  [the longest x1 6.06 us: per_device(): call(first_kernel, (shape(fields.shape, f32), sides, packed, halves, halv...]
  transfers between devices with their start and end apart: 15 -> 17, of which waited for: 10 -> 13; matrix products, arithmetic and copies ran while one was open for 0% -> 0% of each run, Pallas kernels for 14% -> 14%
where the time goes in v3:
time: 69.1 us; the launch traced here: 68.8 us
  waiting for transfers between devices  24.1 us (35%)
  starting transfers between devices  22.9 us (33%)
  Pallas kernels  21 us (30%)
  between operations  0.8 us (1%)
    ppermute x13, waiting for transfers between devices, swap(): return lax.ppermute(value, ('pole', 'sub'), pairs)  17.7 us
    ppermute x13, starting transfers between devices, swap(): return lax.ppermute(value, ('pole', 'sub'), pairs)  17.6 us
    pallas_call x1, Pallas kernels, per_device(): call(first_kernel, (shape(fields.shape, f32), sides, packed, halves, halv...  6.06 us
    pallas_call x1, Pallas kernels, per_device(): call(columns_kernel, (cols, cols, pass_half, pass_half, packed, packed, p...  5.68 us
    ppermute x1, waiting for transfers between devices, per_device(): lax.ppermute(off1, 'sub', across)  5.51 us
    pallas_call x1, Pallas kernels, per_device(): call(functools.partial(ortho_kernel, math.sqrt(total_rows)), shape((own_r...  4.9 us
    ppermute x1, starting transfers between devices, per_device(): off_in0 = lax.ppermute(off0, 'sub', across)  4.56 us
    pallas_call x4, Pallas kernels, per_device(): call(functools.partial(second_kernel, poles, sent), (shape((poles // 2, p...  3.72 us
  transfers between devices with their start and end apart: 17, of which 13 were waited for; matrix products, arithmetic and copies ran while one was open for 0% of the time, Pallas kernels for 14%

profile of v3, /device:TPU:0, one launch (start us, length us, event | category | flops | bytes accessed | tf_op | source)
XLA Modules:
  0.0 68.8 jit_solution(14965704769968804199)
XLA Ops:
  0.7 6.1 %first_pass.1 = (f32[8,512,128]{2,1,0:T(8,128)S(1)}, f32[8,128,128]{2,1,0:T(8,128)S(1)}, f32[8,64,128]{2,1,0:T(8,128)S(1)}, bf16[8,512,512]{2,1,0:T(8,128)(2,1)S(1)}, bf16[8,512,512]{2,1,0:T(8,128)(2,1)S(1)}) custom-call(f32[1]{0:T(128)S(6)} %copy.7.weight, f32[8,512,512]{2,1,0:T(8,128)} %bitcast.4, f32[8,512,128]{2,1,0:T(8,128)} %bitcast.5, ...), custom_call_target="tpu_custom_call" | custom-call | flops 2147483648 | bytes 14680064 | tf_op jit(solution)/shard_map/first_pass/pallas_call | solution.py:367
  6.7 4.6 %collective-permute-start = (f32[8,64,128]{2,1,0:T(8,128)S(1)}, f32[8,64,128]{2,1,0:T(8,128)S(1)}, u32[]{:S(2)}, u32[]{:S(2)}) collective-permute-start(f32[8,64,128]{2,1,0:T(8,128)S(1)} %get-tuple-element.35), channel_id=1, source_target_pairs={{0,7},{1,2},{2,1},{3,4},{4,3},{5,6},{6,5},{7,0},{8,15},{9,10},{10,... | collective-permute-start | bytes 786440 | tf_op jit(solution)/shard_map/ppermute | solution.py:387
  11.3 5.7 %interface_columns.1 = (bf16[8,512,256]{2,1,0:T(8,128)(2,1)S(1)}, bf16[8,512,256]{2,1,0:T(8,128)(2,1)S(1)}, f32[8,2,128,128]{3,2,1,0:T(8,128)S(1)}, f32[8,2,128,...) custom-call(s32[8,2,128]{2,1,0:T(2,128)} %rows_ref.1, ...), custom_call_target="tpu_custom_call" | custom-call | flops 2147483648 | bytes 16777216 | tf_op jit(solution)/shard_map/interface_columns/pallas_call | solution.py:390
  19.5 1.6 %collective-permute-start.2 = (f32[2,512,128]{2,1,0:T(8,128)S(1)}, f32[2,512,128]{2,1,0:T(8,128)S(1)}, u32[]{:S(2)}, u32[]{:S(2)}) collective-permute-start(f32[2,512,128]{2,1,0:T(8,128)S(1)} %second_pass.5), channel_id=1, source_target_pairs={{0,8},{1,17},{2,10},{3,19},{4,12},{5,21},{6,14},{7,23},{8,0},{9,25... | collective-permute-start | bytes 1572872 | tf_op jit(solution)/shard_map/ppermute | solution.py:346
  21.1 5.5 %collective-permute-done.4.off_ref = f32[8,64,128]{2,1,0:T(8,128)S(1)} collective-permute-done((f32[8,64,128]{2,1,0:T(8,128)S(1)}, f32[8,64,128]{2,1,0:T(8,128)S(1)}, u32[]{:S(2)}, u32[]{:S(2)}) %collective-permute-start.4) | collective-permute-done | bytes 262176 | tf_op jit(solution)/shard_map/ppermute | solution.py:406
  26.6 1.0 %second_pass.7 = (f32[2,256,128]{2,1,0:T(8,128)S(1)}, f32[2,256,128]{2,1,0:T(8,128)S(1)}) custom-call(s32[2,8,8,128]{3,2,1,0:T(8,128)S(1)} %get-tuple-element.30.table_ref, bf16[8,512,256]{2,1,0:T(8,128)(2,1)S(1)} %get-tuple-element.31.high_ref, bf16[8,512,256]{2,1,0:T(8,128)(2,1)S(1)} %get-tuple-element.32.low_ref, ...), custom_call_target="tpu_custom_call" | custom-call | flops 536870912 | bytes 4194304 | tf_op jit(solution)/shard_map/second_pass/pallas_call | solution.py:414
  27.5 1.6 %collective-permute-start.6 = (f32[2,256,128]{2,1,0:T(8,128)S(1)}, f32[2,256,128]{2,1,0:T(8,128)S(1)}, u32[]{:S(2)}, u32[]{:S(2)}) collective-permute-start(f32[2,256,128]{2,1,0:T(8,128)S(1)} %get-tuple-element.42), channel_id=1, source_target_pairs={{0,8},{1,9},{2,10},{3,11},{4,12},{5,13},{6,14},{7,15},{8,0},{9,1},... | collective-permute-start | bytes 786440 | tf_op jit(solution)/shard_map/ppermute | solution.py:346
  30.0 1.6 %collective-permute-start.8 = (f32[2,256,128]{2,1,0:T(8,128)S(1)}, f32[2,256,128]{2,1,0:T(8,128)S(1)}, u32[]{:S(2)}, u32[]{:S(2)}) collective-permute-start(f32[2,256,128]{2,1,0:T(8,128)S(1)} %get-tuple-element.44), channel_id=1, source_target_pairs={{0,16},{1,17},{2,18},{3,19},{4,20},{5,21},{6,22},{7,23},{8,24},{9,... | collective-permute-start | bytes 786440 | tf_op jit(solution)/shard_map/ppermute | solution.py:346
  31.6 1.0 %second_pass.6 = (f32[2,256,128]{2,1,0:T(8,128)S(1)}, f32[2,256,128]{2,1,0:T(8,128)S(1)}) custom-call(s32[2,8,8,128]{3,2,1,0:T(8,128)S(1)} %get-tuple-element.30.table_ref, bf16[8,512,256]{2,1,0:T(8,128)(2,1)S(1)} %get-tuple-element.31.high_ref, bf16[8,512,256]{2,1,0:T(8,128)(2,1)S(1)} %get-tuple-element.32.low_ref, ...), custom_call_target="tpu_custom_call" | custom-call | flops 536870912 | bytes 4194304 | tf_op jit(solution)/shard_map/second_pass/pallas_call | solution.py:414
  32.6 2.0 %collective-permute-done.6 = f32[2,256,128]{2,1,0:T(8,128)S(1)} collective-permute-done((f32[2,256,128]{2,1,0:T(8,128)S(1)}, f32[2,256,128]{2,1,0:T(8,128)S(1)}, u32[]{:S(2)}, u32[]{:S(2)}) %collective-permute-start.6) | collective-permute-done | bytes 262176 | tf_op jit(solution)/shard_map/ppermute | solution.py:346
  34.6 1.6 %collective-permute-start.7 = (f32[1,256,128]{2,1,0:T(8,128)S(1)}, f32[1,256,128]{2,1,0:T(8,128)S(1)}, u32[]{:S(2)}, u32[]{:S(2)}) collective-permute-start(f32[1,256,128]{2,1,0:T(8,128)S(1)} %get-tuple-element.53), channel_id=1, source_target_pairs={{0,16},{1,17},{2,18},{3,19},{4,20},{5,21},{6,22},{7,23},{8,24},{9,... | collective-permute-start | bytes 393224 | tf_op jit(solution)/shard_map/ppermute | solution.py:346
  36.8 1.3 %collective-permute-done.8 = f32[2,256,128]{2,1,0:T(8,128)S(1)} collective-permute-done((f32[2,256,128]{2,1,0:T(8,128)S(1)}, f32[2,256,128]{2,1,0:T(8,128)S(1)}, u32[]{:S(2)}, u32[]{:S(2)}) %collective-permute-start.8) | collective-permute-done | bytes 262176 | tf_op jit(solution)/shard_map/ppermute | solution.py:346
  38.4 1.2 %collective-permute-done.7.refs_5_ = f32[1,256,128]{2,1,0:T(8,128)S(1)} collective-permute-done((f32[1,256,128]{2,1,0:T(8,128)S(1)}, f32[1,256,128]{2,1,0:T(8,128)S(1)}, u32[]{:S(2)}, u32[]{:S(2)}) %collective-permute-start.7) | collective-permute-done | bytes 131104 | tf_op jit(solution)/shard_map/ppermute | solution.py:346
  39.6 3.6 %collective-permute-done.9.refs_8_ = f32[1,256,128]{2,1,0:T(8,128)S(1)} collective-permute-done((f32[1,256,128]{2,1,0:T(8,128)S(1)}, f32[1,256,128]{2,1,0:T(8,128)S(1)}, u32[]{:S(2)}, u32[]{:S(2)}) %collective-permute-start.9) | collective-permute-done | bytes 131104 | tf_op jit(solution)/shard_map/ppermute | solution.py:346
  43.9 1.2 %collective-permute-done.10 = f32[72,128]{1,0:T(8,128)S(1)} collective-permute-done((f32[72,128]{1,0:T(8,128)S(1)}, f32[72,128]{1,0:T(8,128)S(1)}, u32[]{:S(2)}, u32[]{:S(2)}) %collective-permute-start.10) | collective-permute-done | bytes 36896 | tf_op jit(solution)/shard_map/ppermute | solution.py:346
  45.1 2.9 %collective-permute-start.12 = (f32[72,128]{1,0:T(8,128)S(1)}, f32[72,128]{1,0:T(8,128)S(1)}, u32[]{:S(2)}, u32[]{:S(2)}) collective-permute-start(f32[72,128]{1,0:T(8,128)S(1)} %add.18.total_ref), channel_id=1, source_target_pairs={{0,8},{2,10},{4,12},{6,14},{8,0},{10,2},{12,4},{14,6},{16,24},{18,... | collective-permute-start | bytes 110600 | tf_op jit(solution)/shard_map/ppermute | solution.py:346
  47.9 2.1 %collective-permute-start.11 = (f32[72,128]{1,0:T(8,128)S(1)}, f32[72,128]{1,0:T(8,128)S(1)}, u32[]{:S(2)}, u32[]{:S(2)}) collective-permute-start(f32[72,128]{1,0:T(8,128)S(1)} %add.18.total_ref), channel_id=1, source_target_pairs={{0,24},{1,17},{2,26},{3,19},{4,28},{5,21},{6,30},{7,23},{8,16},{9,... | collective-permute-start | bytes 110600 | tf_op jit(solution)/shard_map/ppermute | solution.py:346
  50.9 1.9 %collective-permute-done.11.refs_0_ = f32[72,128]{1,0:T(8,128)S(1)} collective-permute-done((f32[72,128]{1,0:T(8,128)S(1)}, f32[72,128]{1,0:T(8,128)S(1)}, u32[]{:S(2)}, u32[]{:S(2)}) %collective-permute-start.11) | collective-permute-done | bytes 36896 | tf_op jit(solution)/shard_map/ppermute | solution.py:346
  52.9 1.2 %collective-permute-done.13 = f32[72,128]{1,0:T(8,128)S(1)} collective-permute-done((f32[72,128]{1,0:T(8,128)S(1)}, f32[72,128]{1,0:T(8,128)S(1)}, u32[]{:S(2)}, u32[]{:S(2)}) %collective-permute-start.13) | collective-permute-done | bytes 36896 | tf_op jit(solution)/shard_map/ppermute | solution.py:346
  54.1 2.7 %collective-permute-start.15 = (f32[72,128]{1,0:T(8,128)S(1)}, f32[72,128]{1,0:T(8,128)S(1)}, u32[]{:S(2)}, u32[]{:S(2)}) collective-permute-start(f32[72,128]{1,0:T(8,128)S(1)} %add.19.total_ref), channel_id=1, source_target_pairs={{0,2},{2,0},{4,6},{6,4},{8,10},{10,8},{12,14},{14,12},{16,18},{18,... | collective-permute-start | bytes 110600 | tf_op jit(solution)/shard_map/ppermute | solution.py:346
  56.8 2.6 %collective-permute-start.14 = (f32[72,128]{1,0:T(8,128)S(1)}, f32[72,128]{1,0:T(8,128)S(1)}, u32[]{:S(2)}, u32[]{:S(2)}) collective-permute-start(f32[72,128]{1,0:T(8,128)S(1)} %add.19.total_ref), channel_id=1, source_target_pairs={{0,6},{1,5},{2,4},{3,7},{4,2},{5,1},{6,0},{7,3},{8,14},{9,13},{10,... | collective-permute-start | bytes 110600 | tf_op jit(solution)/shard_map/ppermute | solution.py:346
  60.0 2.7 %collective-permute-done.14.refs_0_ = f32[72,128]{1,0:T(8,128)S(1)} collective-permute-done((f32[72,128]{1,0:T(8,128)S(1)}, f32[72,128]{1,0:T(8,128)S(1)}, u32[]{:S(2)}, u32[]{:S(2)}) %collective-permute-start.14) | collective-permute-done | bytes 36896 | tf_op jit(solution)/shard_map/ppermute | solution.py:346
  62.7 1.2 %collective-permute-done.16.refs_1_ = f32[72,128]{1,0:T(8,128)S(1)} collective-permute-done((f32[72,128]{1,0:T(8,128)S(1)}, f32[72,128]{1,0:T(8,128)S(1)}, u32[]{:S(2)}, u32[]{:S(2)}) %collective-permute-start.16) | collective-permute-done | bytes 36896 | tf_op jit(solution)/shard_map/ppermute | solution.py:346
  63.9 4.9 %ortho.1 = f32[1024,128]{1,0:T(8,128)} custom-call(f32[72,128]{1,0:T(8,128)S(1)} %gram_share.3.refs_0_, f32[72,128]{1,0:T(8,128)S(1)} %collective-permute-done.16.refs_1_, bf16[1024,256]{1,0:T(8,128)(2,1)S(1)} %get-tuple-element.46.refs_2_), custom_call_target="tpu_custom_call" | custom-call | flops 100663296 | bytes 1048576 | tf_op jit(solution)/shard_map/ortho/pallas_call | solution.py:469
  (29 shorter events, 6.6 us)
Async XLA Ops:
  0.7 10.7 %copy-start = (f32[8,2,128]{2,1,0:T(2,128)S(1)}, f32[8,2,128]{2,1,0:T(2,128)}, u32[]{:S(2)}) copy-start(f32[8,2,128]{2,1,0:T(2,128)} %coup_ref.1) | copy-start | bytes 24580
  0.7 10.6 %copy-start.1 = (s32[8,2]{0,1:T(2,128)S(1)}, s32[8,2]{0,1:T(2,128)}, u32[]{:S(2)}) copy-start(s32[8,2]{0,1:T(2,128)} %param.9) | copy-start | bytes 196
  6.7 11.0 %collective-permute-start = (f32[8,64,128]{2,1,0:T(8,128)S(1)}, f32[8,64,128]{2,1,0:T(8,128)S(1)}, u32[]{:S(2)}, u32[]{:S(2)}) collective-permute-start(f32[8,64,128]{2,1,0:T(8,128)S(1)} %get-tuple-element.35), channel_id=1, source_target_pairs={{0,7},{1,2},{2,1},{3,4},{4,3},{5,6},{6,5},{7,0},{8,15},{9,10},{10,... | collective-permute-start | bytes 786440 | tf_op jit(solution)/shard_map/ppermute | solution.py:387
  17.0 1.6 %collective-permute-start.1 = (f32[8,64,128]{2,1,0:T(8,128)S(1)}, f32[8,64,128]{2,1,0:T(8,128)S(1)}, u32[]{:S(2)}, u32[]{:S(2)}) collective-permute-start(f32[8,64,128]{2,1,0:T(8,128)S(1)} %get-tuple-element.37), channel_id=1, source_target_pairs={{0,1},{1,0},{2,3},{3,2},{4,5},{5,4},{6,7},{7,6},{8,9},{9,8},{10,11... | collective-permute-start | bytes 786440 | tf_op jit(solution)/shard_map/ppermute | solution.py:404
  17.1 9.5 %collective-permute-start.4 = (f32[8,64,128]{2,1,0:T(8,128)S(1)}, f32[8,64,128]{2,1,0:T(8,128)S(1)}, u32[]{:S(2)}, u32[]{:S(2)}) collective-permute-start(f32[8,64,128]{2,1,0:T(8,128)S(1)} %get-tuple-element.39), channel_id=1, source_target_pairs={{0,7},{1,2},{2,1},{3,4},{4,3},{5,6},{6,5},{7,0},{8,15},{9,10},{10,... | collective-permute-start | bytes 786440 | tf_op jit(solution)/shard_map/ppermute | solution.py:406
  17.7 8.8 %collective-permute-start.5 = (f32[8,64,128]{2,1,0:T(8,128)S(1)}, f32[8,64,128]{2,1,0:T(8,128)S(1)}, u32[]{:S(2)}, u32[]{:S(2)}) collective-permute-start(f32[8,64,128]{2,1,0:T(8,128)S(1)} %get-tuple-element.40), channel_id=1, source_target_pairs={{0,1},{1,0},{2,3},{3,2},{4,5},{5,4},{6,7},{7,6},{8,9},{9,8},{10,11... | collective-permute-start | bytes 786440 | tf_op jit(solution)/shard_map/ppermute | solution.py:406
  19.5 16.7 %collective-permute-start.2 = (f32[2,512,128]{2,1,0:T(8,128)S(1)}, f32[2,512,128]{2,1,0:T(8,128)S(1)}, u32[]{:S(2)}, u32[]{:S(2)}) collective-permute-start(f32[2,512,128]{2,1,0:T(8,128)S(1)} %second_pass.5), channel_id=1, source_target_pairs={{0,8},{1,17},{2,10},{3,19},{4,12},{5,21},{6,14},{7,23},{8,0},{9,25... | collective-permute-start | bytes 1572872 | tf_op jit(solution)/shard_map/ppermute | solution.py:346
  27.5 7.0 %collective-permute-start.6 = (f32[2,256,128]{2,1,0:T(8,128)S(1)}, f32[2,256,128]{2,1,0:T(8,128)S(1)}, u32[]{:S(2)}, u32[]{:S(2)}) collective-permute-start(f32[2,256,128]{2,1,0:T(8,128)S(1)} %get-tuple-element.42), channel_id=1, source_target_pairs={{0,8},{1,9},{2,10},{3,11},{4,12},{5,13},{6,14},{7,15},{8,0},{9,1},... | collective-permute-start | bytes 786440 | tf_op jit(solution)/shard_map/ppermute | solution.py:346
  30.0 8.1 %collective-permute-start.8 = (f32[2,256,128]{2,1,0:T(8,128)S(1)}, f32[2,256,128]{2,1,0:T(8,128)S(1)}, u32[]{:S(2)}, u32[]{:S(2)}) collective-permute-start(f32[2,256,128]{2,1,0:T(8,128)S(1)} %get-tuple-element.44), channel_id=1, source_target_pairs={{0,16},{1,17},{2,18},{3,19},{4,20},{5,21},{6,22},{7,23},{8,24},{9,... | collective-permute-start | bytes 786440 | tf_op jit(solution)/shard_map/ppermute | solution.py:346
  34.6 5.0 %collective-permute-start.7 = (f32[1,256,128]{2,1,0:T(8,128)S(1)}, f32[1,256,128]{2,1,0:T(8,128)S(1)}, u32[]{:S(2)}, u32[]{:S(2)}) collective-permute-start(f32[1,256,128]{2,1,0:T(8,128)S(1)} %get-tuple-element.53), channel_id=1, source_target_pairs={{0,16},{1,17},{2,18},{3,19},{4,20},{5,21},{6,22},{7,23},{8,24},{9,... | collective-permute-start | bytes 393224 | tf_op jit(solution)/shard_map/ppermute | solution.py:346
  36.2 7.0 %collective-permute-start.3 = (f32[1,512,128]{2,1,0:T(8,128)S(1)}, f32[1,512,128]{2,1,0:T(8,128)S(1)}, u32[]{:S(2)}, u32[]{:S(2)}) collective-permute-start(f32[1,512,128]{2,1,0:T(8,128)S(1)} %get-tuple-element.47), channel_id=1, source_target_pairs={{0,16},{1,9},{2,18},{3,11},{4,20},{5,13},{6,22},{7,15},{8,24},{9,1... | collective-permute-start | bytes 786440 | tf_op jit(solution)/shard_map/ppermute | solution.py:346
  38.2 5.0 %collective-permute-start.9 = (f32[1,256,128]{2,1,0:T(8,128)S(1)}, f32[1,256,128]{2,1,0:T(8,128)S(1)}, u32[]{:S(2)}, u32[]{:S(2)}) collective-permute-start(f32[1,256,128]{2,1,0:T(8,128)S(1)} %get-tuple-element.50), channel_id=1, source_target_pairs={{0,8},{1,9},{2,10},{3,11},{4,12},{5,13},{6,14},{7,15},{8,0},{9,1},... | collective-permute-start | bytes 393224 | tf_op jit(solution)/shard_map/ppermute | solution.py:346
  43.8 1.3 %collective-permute-start.10 = (f32[72,128]{1,0:T(8,128)S(1)}, f32[72,128]{1,0:T(8,128)S(1)}, u32[]{:S(2)}, u32[]{:S(2)}) collective-permute-start(f32[72,128]{1,0:T(8,128)S(1)} %get-tuple-element.45), channel_id=1, source_target_pairs={{0,1},{1,0},{2,3},{3,2},{4,5},{5,4},{6,7},{7,6},{8,9},{9,8},{10,11... | collective-permute-start | bytes 110600 | tf_op jit(solution)/shard_map/ppermute | solution.py:346
  45.1 5.8 %collective-permute-start.12 = (f32[72,128]{1,0:T(8,128)S(1)}, f32[72,128]{1,0:T(8,128)S(1)}, u32[]{:S(2)}, u32[]{:S(2)}) collective-permute-start(f32[72,128]{1,0:T(8,128)S(1)} %add.18.total_ref), channel_id=1, source_target_pairs={{0,8},{2,10},{4,12},{6,14},{8,0},{10,2},{12,4},{14,6},{16,24},{18,... | collective-permute-start | bytes 110600 | tf_op jit(solution)/shard_map/ppermute | solution.py:346
  47.9 4.9 %collective-permute-start.11 = (f32[72,128]{1,0:T(8,128)S(1)}, f32[72,128]{1,0:T(8,128)S(1)}, u32[]{:S(2)}, u32[]{:S(2)}) collective-permute-start(f32[72,128]{1,0:T(8,128)S(1)} %add.18.total_ref), channel_id=1, source_target_pairs={{0,24},{1,17},{2,26},{3,19},{4,28},{5,21},{6,30},{7,23},{8,16},{9,... | collective-permute-start | bytes 110600 | tf_op jit(solution)/shard_map/ppermute | solution.py:346
  52.9 1.3 %collective-permute-start.13 = (f32[72,128]{1,0:T(8,128)S(1)}, f32[72,128]{1,0:T(8,128)S(1)}, u32[]{:S(2)}, u32[]{:S(2)}) collective-permute-start(f32[72,128]{1,0:T(8,128)S(1)} %gram_share.2), channel_id=1, source_target_pairs={{0,1},{1,0},{2,3},{3,2},{4,5},{5,4},{6,7},{7,6},{8,9},{9,8},{10,11... | collective-permute-start | bytes 110600 | tf_op jit(solution)/shard_map/ppermute | solution.py:346
  54.1 5.8 %collective-permute-start.15 = (f32[72,128]{1,0:T(8,128)S(1)}, f32[72,128]{1,0:T(8,128)S(1)}, u32[]{:S(2)}, u32[]{:S(2)}) collective-permute-start(f32[72,128]{1,0:T(8,128)S(1)} %add.19.total_ref), channel_id=1, source_target_pairs={{0,2},{2,0},{4,6},{6,4},{8,10},{10,8},{12,14},{14,12},{16,18},{18,... | collective-permute-start | bytes 110600 | tf_op jit(solution)/shard_map/ppermute | solution.py:346
  56.8 5.8 %collective-permute-start.14 = (f32[72,128]{1,0:T(8,128)S(1)}, f32[72,128]{1,0:T(8,128)S(1)}, u32[]{:S(2)}, u32[]{:S(2)}) collective-permute-start(f32[72,128]{1,0:T(8,128)S(1)} %add.19.total_ref), channel_id=1, source_target_pairs={{0,6},{1,5},{2,4},{3,7},{4,2},{5,1},{6,0},{7,3},{8,14},{9,13},{10,... | collective-permute-start | bytes 110600 | tf_op jit(solution)/shard_map/ppermute | solution.py:346
  62.7 1.3 %collective-permute-start.16 = (f32[72,128]{1,0:T(8,128)S(1)}, f32[72,128]{1,0:T(8,128)S(1)}, u32[]{:S(2)}, u32[]{:S(2)}) collective-permute-start(f32[72,128]{1,0:T(8,128)S(1)} %gram_share.3.refs_0_), channel_id=1, source_target_pairs={{0,1},{1,0},{2,3},{3,2},{4,5},{5,4},{6,7},{7,6},{8,9},{9,8},{10,11... | collective-permute-start | bytes 110600 | tf_op jit(solution)/shard_map/ppermute | solution.py:346

commit v4 on v3

--- a/solution.py
+++ b/solution.py
@@ -1,5 +1,4 @@
 import functools
-import itertools
 import math
 
 import jax
@@ -205,12 +204,6 @@
     gram_ref[half:, :] = jnp.broadcast_to(diag, (gram_ref.shape[0] - half, width))
 
 
-def share_kernel(total_ref, *refs):
-    *got_refs, out_ref = refs
-    own = jnp.where(sub_parity() == 0, total_ref[...], 0.0)
-    out_ref[...] = functools.reduce(jnp.add, [ref[...] for ref in got_refs], own)
-
-
 def unpacked(gram):
     width = gram.shape[1]
     half = width // 2
@@ -340,9 +333,8 @@
     pairs = []
     for p in range(poles):
         for s in range(groups):
-            masks = odd if s % 2 else even
-            if masks:
-                pairs.append((p * groups + s, (p ^ masks[0]) * groups + (s ^ masks[1])))
+            pole_mask, sub_mask = odd if s % 2 else even
+            pairs.append((p * groups + s, (p ^ pole_mask) * groups + (s ^ sub_mask)))
     return lax.ppermute(value, ("pole", "sub"), pairs)
 
 
@@ -409,7 +401,7 @@
     per_owner = sub_count // poles
     steps = poles.bit_length() - 1
     pending = []
-    for arrays, own_pass, (off_in, on_in) in zip((1, 2), (pass0, pass1), halves):
+    for arrays, own_pass, (off_in, on_in) in zip((2, 2), (pass0, pass1), halves):
         send, keep = (
             call(
                 functools.partial(second_kernel, poles, sent),
@@ -449,21 +441,12 @@
         name="gram",
     )(*[v for arrays in summands for kept in arrays for v in kept])
 
-    stages = [[(r, 0) for r in range(poles - 1, 0, -1)]]
-    base = 2
-    while base < groups:
-        radix = min(4, groups // base)
-        stages.append([(0, base * r) for r in range(radix - 1, 0, -1)])
-        base *= radix
-    inside_chip = ((0, 1), (0, 1))
-    grams = [gram, swap(gram, *inside_chip)]
+    stages = [[(0, 1)], [(r, 0) for r in range(1, poles)]]
+    stages += [[(0, 1 << bit)] for bit in range(1, groups.bit_length() - 1)]
+    grams = [gram]
     for masks in stages:
         total = functools.reduce(jnp.add, grams)
-        got = [
-            swap(total, even, odd) for even, odd in itertools.zip_longest(masks[0::2], masks[1::2])
-        ]
-        share = call(share_kernel, shape(gram.shape, f32), name="gram_share")(total, *got)
-        grams = [share, swap(share, *inside_chip)]
+        grams = [total] + [swap(total, m, m) for m in masks]
 
     total_rows = sub_count * block_len * groups
     return call(

time: 69.1 us -> 66 us (0.955)
  starting transfers between devices: 22.9 us -> 19.2 us
    ppermute x13 -> x14, starting transfers between devices: 17.6 us -> 13.8 us  [swap(): return lax.ppermute(value, ('pole', 'sub'), pairs)]
    ppermute x13 -> x14, waiting for transfers between devices: 17.7 us -> 20.8 us  [swap(): return lax.ppermute(value, ('pole', 'sub'), pairs)]
    ppermute x1, waiting for transfers between devices: 5.51 us -> 2.87 us  [per_device(): lax.ppermute(off1, 'sub', across)]
  transfers between devices with their start and end apart: 17 -> 18, of which waited for: 13 -> 13; matrix products, arithmetic and copies ran while one was open for 0% -> 0% of each run, Pallas kernels for 14% -> 15%
where the time goes in v4:
time: 66 us; the launch traced here: 65.7 us
  waiting for transfers between devices  24.4 us (37%)
  Pallas kernels  21.1 us (32%)
  starting transfers between devices  19.2 us (29%)
  between operations  0.78 us (1%)
    ppermute x14, waiting for transfers between devices, swap(): return lax.ppermute(value, ('pole', 'sub'), pairs)  20.8 us
    ppermute x14, starting transfers between devices, swap(): return lax.ppermute(value, ('pole', 'sub'), pairs)  13.8 us
    pallas_call x1, Pallas kernels, per_device(): call(first_kernel, (shape(fields.shape, f32), sides, packed, halves, halv...  6.05 us
    pallas_call x1, Pallas kernels, per_device(): call(columns_kernel, (cols, cols, pass_half, pass_half, packed, packed, p...  5.67 us
    pallas_call x1, Pallas kernels, per_device(): call(functools.partial(ortho_kernel, math.sqrt(total_rows)), shape((own_r...  4.9 us
    ppermute x1, starting transfers between devices, per_device(): off_in0 = lax.ppermute(off0, 'sub', across)  4.57 us
    pallas_call x4, Pallas kernels, per_device(): call(functools.partial(second_kernel, poles, sent), (shape((poles // 2, p...  3.97 us
    ppermute x1, waiting for transfers between devices, per_device(): lax.ppermute(off1, 'sub', across)  2.87 us
  transfers between devices with their start and end apart: 18, of which 13 were waited for; matrix products, arithmetic and copies ran while one was open for 0% of the time, Pallas kernels for 15%

profile of v4, /device:TPU:0, one launch (start us, length us, event | category | flops | bytes accessed | tf_op | source)
XLA Modules:
  0.0 65.7 jit_solution(10445046632108903116)
XLA Ops:
  0.7 6.0 %first_pass.1 = (f32[8,512,128]{2,1,0:T(8,128)S(1)}, f32[8,128,128]{2,1,0:T(8,128)S(1)}, f32[8,64,128]{2,1,0:T(8,128)S(1)}, bf16[8,512,512]{2,1,0:T(8,128)(2,1)S(1)}, bf16[8,512,512]{2,1,0:T(8,128)(2,1)S(1)}) custom-call(f32[1]{0:T(128)S(6)} %copy.7.weight, f32[8,512,512]{2,1,0:T(8,128)} %bitcast.4, f32[8,512,128]{2,1,0:T(8,128)} %bitcast.5, ...), custom_call_target="tpu_custom_call" | custom-call | flops 2147483648 | bytes 14680064 | tf_op jit(solution)/shard_map/first_pass/pallas_call | solution.py:359
  6.7 4.6 %collective-permute-start = (f32[8,64,128]{2,1,0:T(8,128)S(1)}, f32[8,64,128]{2,1,0:T(8,128)S(1)}, u32[]{:S(2)}, u32[]{:S(2)}) collective-permute-start(f32[8,64,128]{2,1,0:T(8,128)S(1)} %get-tuple-element.39), channel_id=1, source_target_pairs={{0,7},{1,2},{2,1},{3,4},{4,3},{5,6},{6,5},{7,0},{8,15},{9,10},{10,... | collective-permute-start | bytes 786440 | tf_op jit(solution)/shard_map/ppermute | solution.py:379
  11.3 5.7 %interface_columns.1 = (bf16[8,512,256]{2,1,0:T(8,128)(2,1)S(1)}, bf16[8,512,256]{2,1,0:T(8,128)(2,1)S(1)}, f32[8,2,128,128]{3,2,1,0:T(8,128)S(1)}, f32[8,2,128,...) custom-call(s32[8,2,128]{2,1,0:T(2,128)} %rows_ref.1, ...), custom_call_target="tpu_custom_call" | custom-call | flops 2147483648 | bytes 16777216 | tf_op jit(solution)/shard_map/interface_columns/pallas_call | solution.py:382
  18.6 1.0 %second_pass.5 = (f32[2,256,128]{2,1,0:T(8,128)S(1)}, f32[2,256,128]{2,1,0:T(8,128)S(1)}) custom-call(s32[2,8,8,128]{3,2,1,0:T(8,128)S(1)} %get-tuple-element.34.table_ref, bf16[8,512,256]{2,1,0:T(8,128)(2,1)S(1)} %get-tuple-element.35.high_ref, bf16[8,512,256]{2,1,0:T(8,128)(2,1)S(1)} %get-tuple-element.36.low_ref, ...), custom_call_target="tpu_custom_call" | custom-call | flops 536870912 | bytes 4194304 | tf_op jit(solution)/shard_map/second_pass/pallas_call | solution.py:406
  19.6 1.6 %collective-permute-start.2 = (f32[2,256,128]{2,1,0:T(8,128)S(1)}, f32[2,256,128]{2,1,0:T(8,128)S(1)}, u32[]{:S(2)}, u32[]{:S(2)}) collective-permute-start(f32[2,256,128]{2,1,0:T(8,128)S(1)} %get-tuple-element.43), channel_id=1, source_target_pairs={{0,8},{1,9},{2,10},{3,11},{4,12},{5,13},{6,14},{7,15},{8,0},{9,1},... | collective-permute-start | bytes 786440 | tf_op jit(solution)/shard_map/ppermute | solution.py:338
  21.2 1.5 %collective-permute-start.4 = (f32[2,256,128]{2,1,0:T(8,128)S(1)}, f32[2,256,128]{2,1,0:T(8,128)S(1)}, u32[]{:S(2)}, u32[]{:S(2)}) collective-permute-start(f32[2,256,128]{2,1,0:T(8,128)S(1)} %get-tuple-element.45), channel_id=1, source_target_pairs={{0,16},{1,17},{2,18},{3,19},{4,20},{5,21},{6,22},{7,23},{8,24},{9,... | collective-permute-start | bytes 786440 | tf_op jit(solution)/shard_map/ppermute | solution.py:338
  22.7 1.0 %second_pass.4 = (f32[2,256,128]{2,1,0:T(8,128)S(1)}, f32[2,256,128]{2,1,0:T(8,128)S(1)}) custom-call(s32[2,8,8,128]{3,2,1,0:T(8,128)S(1)} %get-tuple-element.34.table_ref, bf16[8,512,256]{2,1,0:T(8,128)(2,1)S(1)} %get-tuple-element.35.high_ref, bf16[8,512,256]{2,1,0:T(8,128)(2,1)S(1)} %get-tuple-element.36.low_ref, ...), custom_call_target="tpu_custom_call" | custom-call | flops 536870912 | bytes 4194304 | tf_op jit(solution)/shard_map/second_pass/pallas_call | solution.py:406
  23.7 2.9 %collective-permute-done.6.off_ref = f32[8,64,128]{2,1,0:T(8,128)S(1)} collective-permute-done((f32[8,64,128]{2,1,0:T(8,128)S(1)}, f32[8,64,128]{2,1,0:T(8,128)S(1)}, u32[]{:S(2)}, u32[]{:S(2)}) %collective-permute-start.6) | collective-permute-done | bytes 262176 | tf_op jit(solution)/shard_map/ppermute | solution.py:398
  26.6 1.0 %second_pass.7 = (f32[2,256,128]{2,1,0:T(8,128)S(1)}, f32[2,256,128]{2,1,0:T(8,128)S(1)}) custom-call(s32[2,8,8,128]{3,2,1,0:T(8,128)S(1)} %get-tuple-element.34.table_ref, bf16[8,512,256]{2,1,0:T(8,128)(2,1)S(1)} %get-tuple-element.35.high_ref, bf16[8,512,256]{2,1,0:T(8,128)(2,1)S(1)} %get-tuple-element.36.low_ref, ...), custom_call_target="tpu_custom_call" | custom-call | flops 536870912 | bytes 4194304 | tf_op jit(solution)/shard_map/second_pass/pallas_call | solution.py:406
  27.6 1.5 %collective-permute-start.8 = (f32[2,256,128]{2,1,0:T(8,128)S(1)}, f32[2,256,128]{2,1,0:T(8,128)S(1)}, u32[]{:S(2)}, u32[]{:S(2)}) collective-permute-start(f32[2,256,128]{2,1,0:T(8,128)S(1)} %get-tuple-element.50), channel_id=1, source_target_pairs={{0,8},{1,9},{2,10},{3,11},{4,12},{5,13},{6,14},{7,15},{8,0},{9,1},... | collective-permute-start | bytes 786440 | tf_op jit(solution)/shard_map/ppermute | solution.py:338
  29.1 1.5 %collective-permute-start.10 = (f32[2,256,128]{2,1,0:T(8,128)S(1)}, f32[2,256,128]{2,1,0:T(8,128)S(1)}, u32[]{:S(2)}, u32[]{:S(2)}) collective-permute-start(f32[2,256,128]{2,1,0:T(8,128)S(1)} %get-tuple-element.52), channel_id=1, source_target_pairs={{0,16},{1,17},{2,18},{3,19},{4,20},{5,21},{6,22},{7,23},{8,24},{9,... | collective-permute-start | bytes 786440 | tf_op jit(solution)/shard_map/ppermute | solution.py:338
  32.9 3.1 %collective-permute-done.8 = f32[2,256,128]{2,1,0:T(8,128)S(1)} collective-permute-done((f32[2,256,128]{2,1,0:T(8,128)S(1)}, f32[2,256,128]{2,1,0:T(8,128)S(1)}, u32[]{:S(2)}, u32[]{:S(2)}) %collective-permute-start.8) | collective-permute-done | bytes 262176 | tf_op jit(solution)/shard_map/ppermute | solution.py:338
  36.0 1.6 %collective-permute-start.9 = (f32[1,256,128]{2,1,0:T(8,128)S(1)}, f32[1,256,128]{2,1,0:T(8,128)S(1)}, u32[]{:S(2)}, u32[]{:S(2)}) collective-permute-start(f32[1,256,128]{2,1,0:T(8,128)S(1)} %get-tuple-element.58), channel_id=1, source_target_pairs={{0,16},{1,17},{2,18},{3,19},{4,20},{5,21},{6,22},{7,23},{8,24},{9,... | collective-permute-start | bytes 393224 | tf_op jit(solution)/shard_map/ppermute | solution.py:338
  38.4 1.3 %collective-permute-start.11 = (f32[1,256,128]{2,1,0:T(8,128)S(1)}, f32[1,256,128]{2,1,0:T(8,128)S(1)}, u32[]{:S(2)}, u32[]{:S(2)}) collective-permute-start(f32[1,256,128]{2,1,0:T(8,128)S(1)} %get-tuple-element.55), channel_id=1, source_target_pairs={{0,8},{1,9},{2,10},{3,11},{4,12},{5,13},{6,14},{7,15},{8,0},{9,1},... | collective-permute-start | bytes 393224 | tf_op jit(solution)/shard_map/ppermute | solution.py:338
  40.0 1.4 %collective-permute-done.9.refs_8_ = f32[1,256,128]{2,1,0:T(8,128)S(1)} collective-permute-done((f32[1,256,128]{2,1,0:T(8,128)S(1)}, f32[1,256,128]{2,1,0:T(8,128)S(1)}, u32[]{:S(2)}, u32[]{:S(2)}) %collective-permute-start.9) | collective-permute-done | bytes 131104 | tf_op jit(solution)/shard_map/ppermute | solution.py:338
  41.4 2.1 %collective-permute-done.11.refs_11_ = f32[1,256,128]{2,1,0:T(8,128)S(1)} collective-permute-done((f32[1,256,128]{2,1,0:T(8,128)S(1)}, f32[1,256,128]{2,1,0:T(8,128)S(1)}, u32[]{:S(2)}, u32[]{:S(2)}) %collective-permute-start.11) | collective-permute-done | bytes 131104 | tf_op jit(solution)/shard_map/ppermute | solution.py:338
  44.1 1.2 %collective-permute-done.12 = f32[72,128]{1,0:T(8,128)S(1)} collective-permute-done((f32[72,128]{1,0:T(8,128)S(1)}, f32[72,128]{1,0:T(8,128)S(1)}, u32[]{:S(2)}, u32[]{:S(2)}) %collective-permute-start.12) | collective-permute-done | bytes 36896 | tf_op jit(solution)/shard_map/ppermute | solution.py:338
  45.3 1.4 %collective-permute-start.15 = (f32[72,128]{1,0:T(8,128)S(1)}, f32[72,128]{1,0:T(8,128)S(1)}, u32[]{:S(2)}, u32[]{:S(2)}) collective-permute-start(f32[72,128]{1,0:T(8,128)S(1)} %add.31), channel_id=1, source_target_pairs={{0,24},{1,25},{2,26},{3,27},{4,28},{5,29},{6,30},{7,31},{8,16},{9,... | collective-permute-start | bytes 110600 | tf_op jit(solution)/shard_map/ppermute | solution.py:338
  46.7 1.3 %collective-permute-start.14 = (f32[72,128]{1,0:T(8,128)S(1)}, f32[72,128]{1,0:T(8,128)S(1)}, u32[]{:S(2)}, u32[]{:S(2)}) collective-permute-start(f32[72,128]{1,0:T(8,128)S(1)} %add.31), channel_id=1, source_target_pairs={{0,16},{1,17},{2,18},{3,19},{4,20},{5,21},{6,22},{7,23},{8,24},{9,... | collective-permute-start | bytes 110600 | tf_op jit(solution)/shard_map/ppermute | solution.py:338
  48.8 1.4 %collective-permute-done.15 = f32[72,128]{1,0:T(8,128)S(1)} collective-permute-done((f32[72,128]{1,0:T(8,128)S(1)}, f32[72,128]{1,0:T(8,128)S(1)}, u32[]{:S(2)}, u32[]{:S(2)}) %collective-permute-start.15) | collective-permute-done | bytes 36896 | tf_op jit(solution)/shard_map/ppermute | solution.py:338
  50.6 1.3 %collective-permute-done.13 = f32[72,128]{1,0:T(8,128)S(1)} collective-permute-done((f32[72,128]{1,0:T(8,128)S(1)}, f32[72,128]{1,0:T(8,128)S(1)}, u32[]{:S(2)}, u32[]{:S(2)}) %collective-permute-start.13) | collective-permute-done | bytes 36896 | tf_op jit(solution)/shard_map/ppermute | solution.py:338
  52.0 3.9 %collective-permute-done.16 = f32[72,128]{1,0:T(8,128)S(1)} collective-permute-done((f32[72,128]{1,0:T(8,128)S(1)}, f32[72,128]{1,0:T(8,128)S(1)}, u32[]{:S(2)}, u32[]{:S(2)}) %collective-permute-start.16) | collective-permute-done | bytes 36896 | tf_op jit(solution)/shard_map/ppermute | solution.py:338
  56.0 4.8 %collective-permute-done.17.refs_1_ = f32[72,128]{1,0:T(8,128)S(1)} collective-permute-done((f32[72,128]{1,0:T(8,128)S(1)}, f32[72,128]{1,0:T(8,128)S(1)}, u32[]{:S(2)}, u32[]{:S(2)}) %collective-permute-start.17) | collective-permute-done | bytes 36896 | tf_op jit(solution)/shard_map/ppermute | solution.py:338
  60.8 4.9 %ortho.1 = f32[1024,128]{1,0:T(8,128)} custom-call(f32[72,128]{1,0:T(8,128)S(1)} %add.35.refs_0_, f32[72,128]{1,0:T(8,128)S(1)} %collective-permute-done.17.refs_1_, bf16[1024,256]{1,0:T(8,128)(2,1)S(1)} %get-tuple-element.54.refs_2_), custom_call_target="tpu_custom_call" | custom-call | flops 100663296 | bytes 1048576 | tf_op jit(solution)/shard_map/ortho/pallas_call | solution.py:452
  (31 shorter events, 7.0 us)
Async XLA Ops:
  0.7 10.6 %copy-start = (f32[8,2,128]{2,1,0:T(2,128)S(1)}, f32[8,2,128]{2,1,0:T(2,128)}, u32[]{:S(2)}) copy-start(f32[8,2,128]{2,1,0:T(2,128)} %coup_ref.1) | copy-start | bytes 24580
  0.7 10.6 %copy-start.1 = (s32[8,2]{0,1:T(2,128)S(1)}, s32[8,2]{0,1:T(2,128)}, u32[]{:S(2)}) copy-start(s32[8,2]{0,1:T(2,128)} %param.9) | copy-start | bytes 196
  6.7 11.0 %collective-permute-start = (f32[8,64,128]{2,1,0:T(8,128)S(1)}, f32[8,64,128]{2,1,0:T(8,128)S(1)}, u32[]{:S(2)}, u32[]{:S(2)}) collective-permute-start(f32[8,64,128]{2,1,0:T(8,128)S(1)} %get-tuple-element.39), channel_id=1, source_target_pairs={{0,7},{1,2},{2,1},{3,4},{4,3},{5,6},{6,5},{7,0},{8,15},{9,10},{10,... | collective-permute-start | bytes 786440 | tf_op jit(solution)/shard_map/ppermute | solution.py:379
  17.0 1.6 %collective-permute-start.1 = (f32[8,64,128]{2,1,0:T(8,128)S(1)}, f32[8,64,128]{2,1,0:T(8,128)S(1)}, u32[]{:S(2)}, u32[]{:S(2)}) collective-permute-start(f32[8,64,128]{2,1,0:T(8,128)S(1)} %get-tuple-element.41), channel_id=1, source_target_pairs={{0,1},{1,0},{2,3},{3,2},{4,5},{5,4},{6,7},{7,6},{8,9},{9,8},{10,11... | collective-permute-start | bytes 786440 | tf_op jit(solution)/shard_map/ppermute | solution.py:396
  17.1 9.5 %collective-permute-start.6 = (f32[8,64,128]{2,1,0:T(8,128)S(1)}, f32[8,64,128]{2,1,0:T(8,128)S(1)}, u32[]{:S(2)}, u32[]{:S(2)}) collective-permute-start(f32[8,64,128]{2,1,0:T(8,128)S(1)} %get-tuple-element.47), channel_id=1, source_target_pairs={{0,7},{1,2},{2,1},{3,4},{4,3},{5,6},{6,5},{7,0},{8,15},{9,10},{10,... | collective-permute-start | bytes 786440 | tf_op jit(solution)/shard_map/ppermute | solution.py:398
  17.8 8.8 %collective-permute-start.7 = (f32[8,64,128]{2,1,0:T(8,128)S(1)}, f32[8,64,128]{2,1,0:T(8,128)S(1)}, u32[]{:S(2)}, u32[]{:S(2)}) collective-permute-start(f32[8,64,128]{2,1,0:T(8,128)S(1)} %get-tuple-element.48), channel_id=1, source_target_pairs={{0,1},{1,0},{2,3},{3,2},{4,5},{5,4},{6,7},{7,6},{8,9},{9,8},{10,11... | collective-permute-start | bytes 786440 | tf_op jit(solution)/shard_map/ppermute | solution.py:398
  19.6 11.0 %collective-permute-start.2 = (f32[2,256,128]{2,1,0:T(8,128)S(1)}, f32[2,256,128]{2,1,0:T(8,128)S(1)}, u32[]{:S(2)}, u32[]{:S(2)}) collective-permute-start(f32[2,256,128]{2,1,0:T(8,128)S(1)} %get-tuple-element.43), channel_id=1, source_target_pairs={{0,8},{1,9},{2,10},{3,11},{4,12},{5,13},{6,14},{7,15},{8,0},{9,1},... | collective-permute-start | bytes 786440 | tf_op jit(solution)/shard_map/ppermute | solution.py:338
  21.2 10.1 %collective-permute-start.4 = (f32[2,256,128]{2,1,0:T(8,128)S(1)}, f32[2,256,128]{2,1,0:T(8,128)S(1)}, u32[]{:S(2)}, u32[]{:S(2)}) collective-permute-start(f32[2,256,128]{2,1,0:T(8,128)S(1)} %get-tuple-element.45), channel_id=1, source_target_pairs={{0,16},{1,17},{2,18},{3,19},{4,20},{5,21},{6,22},{7,23},{8,24},{9,... | collective-permute-start | bytes 786440 | tf_op jit(solution)/shard_map/ppermute | solution.py:338
  27.6 8.4 %collective-permute-start.8 = (f32[2,256,128]{2,1,0:T(8,128)S(1)}, f32[2,256,128]{2,1,0:T(8,128)S(1)}, u32[]{:S(2)}, u32[]{:S(2)}) collective-permute-start(f32[2,256,128]{2,1,0:T(8,128)S(1)} %get-tuple-element.50), channel_id=1, source_target_pairs={{0,8},{1,9},{2,10},{3,11},{4,12},{5,13},{6,14},{7,15},{8,0},{9,1},... | collective-permute-start | bytes 786440 | tf_op jit(solution)/shard_map/ppermute | solution.py:338
  29.1 9.2 %collective-permute-start.10 = (f32[2,256,128]{2,1,0:T(8,128)S(1)}, f32[2,256,128]{2,1,0:T(8,128)S(1)}, u32[]{:S(2)}, u32[]{:S(2)}) collective-permute-start(f32[2,256,128]{2,1,0:T(8,128)S(1)} %get-tuple-element.52), channel_id=1, source_target_pairs={{0,16},{1,17},{2,18},{3,19},{4,20},{5,21},{6,22},{7,23},{8,24},{9,... | collective-permute-start | bytes 786440 | tf_op jit(solution)/shard_map/ppermute | solution.py:338
  30.7 9.3 %collective-permute-start.3 = (f32[1,256,128]{2,1,0:T(8,128)S(1)}, f32[1,256,128]{2,1,0:T(8,128)S(1)}, u32[]{:S(2)}, u32[]{:S(2)}) collective-permute-start(f32[1,256,128]{2,1,0:T(8,128)S(1)} %get-tuple-element.64), channel_id=1, source_target_pairs={{0,16},{1,17},{2,18},{3,19},{4,20},{5,21},{6,22},{7,23},{8,24},{9,... | collective-permute-start | bytes 393224 | tf_op jit(solution)/shard_map/ppermute | solution.py:338
  31.3 8.7 %collective-permute-start.5 = (f32[1,256,128]{2,1,0:T(8,128)S(1)}, f32[1,256,128]{2,1,0:T(8,128)S(1)}, u32[]{:S(2)}, u32[]{:S(2)}) collective-permute-start(f32[1,256,128]{2,1,0:T(8,128)S(1)} %get-tuple-element.61), channel_id=1, source_target_pairs={{0,8},{1,9},{2,10},{3,11},{4,12},{5,13},{6,14},{7,15},{8,0},{9,1},... | collective-permute-start | bytes 393224 | tf_op jit(solution)/shard_map/ppermute | solution.py:338
  36.0 5.4 %collective-permute-start.9 = (f32[1,256,128]{2,1,0:T(8,128)S(1)}, f32[1,256,128]{2,1,0:T(8,128)S(1)}, u32[]{:S(2)}, u32[]{:S(2)}) collective-permute-start(f32[1,256,128]{2,1,0:T(8,128)S(1)} %get-tuple-element.58), channel_id=1, source_target_pairs={{0,16},{1,17},{2,18},{3,19},{4,20},{5,21},{6,22},{7,23},{8,24},{9,... | collective-permute-start | bytes 393224 | tf_op jit(solution)/shard_map/ppermute | solution.py:338
  38.4 5.0 %collective-permute-start.11 = (f32[1,256,128]{2,1,0:T(8,128)S(1)}, f32[1,256,128]{2,1,0:T(8,128)S(1)}, u32[]{:S(2)}, u32[]{:S(2)}) collective-permute-start(f32[1,256,128]{2,1,0:T(8,128)S(1)} %get-tuple-element.55), channel_id=1, source_target_pairs={{0,8},{1,9},{2,10},{3,11},{4,12},{5,13},{6,14},{7,15},{8,0},{9,1},... | collective-permute-start | bytes 393224 | tf_op jit(solution)/shard_map/ppermute | solution.py:338
  44.0 1.3 %collective-permute-start.12 = (f32[72,128]{1,0:T(8,128)S(1)}, f32[72,128]{1,0:T(8,128)S(1)}, u32[]{:S(2)}, u32[]{:S(2)}) collective-permute-start(f32[72,128]{1,0:T(8,128)S(1)} %get-tuple-element.53), channel_id=1, source_target_pairs={{0,1},{1,0},{2,3},{3,2},{4,5},{5,4},{6,7},{7,6},{8,9},{9,8},{10,11... | collective-permute-start | bytes 110600 | tf_op jit(solution)/shard_map/ppermute | solution.py:338
  45.3 4.9 %collective-permute-start.15 = (f32[72,128]{1,0:T(8,128)S(1)}, f32[72,128]{1,0:T(8,128)S(1)}, u32[]{:S(2)}, u32[]{:S(2)}) collective-permute-start(f32[72,128]{1,0:T(8,128)S(1)} %add.31), channel_id=1, source_target_pairs={{0,24},{1,25},{2,26},{3,27},{4,28},{5,29},{6,30},{7,31},{8,16},{9,... | collective-permute-start | bytes 110600 | tf_op jit(solution)/shard_map/ppermute | solution.py:338
  46.7 4.0 %collective-permute-start.14 = (f32[72,128]{1,0:T(8,128)S(1)}, f32[72,128]{1,0:T(8,128)S(1)}, u32[]{:S(2)}, u32[]{:S(2)}) collective-permute-start(f32[72,128]{1,0:T(8,128)S(1)} %add.31), channel_id=1, source_target_pairs={{0,16},{1,17},{2,18},{3,19},{4,20},{5,21},{6,22},{7,23},{8,24},{9,... | collective-permute-start | bytes 110600 | tf_op jit(solution)/shard_map/ppermute | solution.py:338
  48.0 4.0 %collective-permute-start.13 = (f32[72,128]{1,0:T(8,128)S(1)}, f32[72,128]{1,0:T(8,128)S(1)}, u32[]{:S(2)}, u32[]{:S(2)}) collective-permute-start(f32[72,128]{1,0:T(8,128)S(1)} %add.31), channel_id=1, source_target_pairs={{0,8},{1,9},{2,10},{3,11},{4,12},{5,13},{6,14},{7,15},{8,0},{9,1},... | collective-permute-start | bytes 110600 | tf_op jit(solution)/shard_map/ppermute | solution.py:338
  51.9 4.0 %collective-permute-start.16 = (f32[72,128]{1,0:T(8,128)S(1)}, f32[72,128]{1,0:T(8,128)S(1)}, u32[]{:S(2)}, u32[]{:S(2)}) collective-permute-start(f32[72,128]{1,0:T(8,128)S(1)} %add_add_fusion), channel_id=1, source_target_pairs={{0,2},{1,3},{2,0},{3,1},{4,6},{5,7},{6,4},{7,5},{8,10},{9,11},{10,... | collective-permute-start | bytes 110600 | tf_op jit(solution)/shard_map/ppermute | solution.py:338
  56.0 4.9 %collective-permute-start.17 = (f32[72,128]{1,0:T(8,128)S(1)}, f32[72,128]{1,0:T(8,128)S(1)}, u32[]{:S(2)}, u32[]{:S(2)}) collective-permute-start(f32[72,128]{1,0:T(8,128)S(1)} %add.35.refs_0_), channel_id=1, source_target_pairs={{0,4},{1,5},{2,6},{3,7},{4,0},{5,1},{6,2},{7,3},{8,12},{9,13},{10,... | collective-permute-start | bytes 110600 | tf_op jit(solution)/shard_map/ppermute | solution.py:338

commit v5 on v4

--- a/solution.py
+++ b/solution.py
@@ -58,7 +58,7 @@
     out_ref[s] = pack_side(side_ref, s, 0)
 
 
-def first_kernel(weight, inv_hbm, field_hbm, rows_hbm, pass_ref, side_ref, off_ref, inv_high_ref, inv_low_ref,
+def first_kernel(inv_hbm, field_hbm, rows_hbm, pass_ref, side_ref, off_ref, inv_high_ref, inv_low_ref,
                  inv_buf, field_buf, rows, inv_sems, field_sems, rows_sem):
     count = field_buf.shape[0]
     rows_copy = pltpu.make_async_copy(rows_hbm, rows, rows_sem)
@@ -79,21 +79,22 @@
     def one_sub(s, carry):
         for copy in copies(s):
             copy.wait()
+        parts = split(inv_buf[s])
+        result = split_dot(parts, field_buf[s])
         gather_side(jnp.maximum(s - 1, 0), parity, pass_ref, rows, side_ref, off_ref)
-        inv_high_ref[s], inv_low_ref[s] = parts = split(inv_buf[s])
-        pass_ref[s] = weight[0] * split_dot(parts, field_buf[s])
+        inv_high_ref[s], inv_low_ref[s] = parts
+        pass_ref[s] = result
         return carry
 
     lax.fori_loop(0, count, one_sub, 0)
     gather_side(count - 1, parity, pass_ref, rows, side_ref, off_ref)
 
 
-def columns_kernel(rows_hbm, inv_high_ref, inv_low_ref, rows_ref, coup_ref, near_ref, pass_ref, off_side_ref,
-                   high_cols_ref, low_cols_ref, pass0_ref, pass1_ref, off_ref, on0_ref, on1_ref, table_ref,
+def columns_kernel(rows_hbm, weight_ref, inv_high_ref, inv_low_ref, rows_ref, coup_ref, near_ref, pass_ref, off_side_ref,
+                   high_cols_ref, low_cols_ref, off_ref, on0_ref, on1_ref, table_ref, wide_ref,
                    on_side_ref, rows, rows_sem):
     count, block_len = inv_high_ref.shape[:2]
     iface_len = rows_ref.shape[2]
-    quarter = block_len // 4
 
     rows_copy = pltpu.make_async_copy(rows_hbm, rows, rows_sem)
     rows_copy.start()
@@ -102,32 +103,31 @@
         near = lax.rem(near_ref[pl.ds(side, 1), :], count)
         for s in range(count):
             table_ref[spot, s] = jnp.broadcast_to(near[:, s : s + 1], table_ref.shape[2:])
+    weight = weight_ref[0]
+    wide_ref[...] = jnp.full(wide_ref.shape, weight, f32)
     place = lax.broadcasted_iota(jnp.int32, (block_len, 2 * iface_len), 0)
     rows_copy.wait()
 
     def one_sub(s, carry):
-        gather_side(s, 1 - parity, pass_ref, rows, on_side_ref, on0_ref)
-        on1_ref[s] = pack_side(on_side_ref, s, 1)
-        off_ref[s] = pack_side(off_side_ref, s, 1)
-        for half, out_ref in enumerate((pass0_ref, pass1_ref)):
-            for way in range(2):
-                at = 2 * way * quarter
-                out_ref[s, way] = pack(
-                    pass_ref[s, at : at + quarter, :], pass_ref[s, at + quarter : at + 2 * quarter, :], half
-                )
         at, coup = (
             jnp.concatenate([ref[s, pl.ds(side, 1), :] for side in (parity, 1 - parity)], axis=1)
             for ref in (rows_ref, coup_ref)
         )
         pick = (at == place).astype(f32).astype(bf16)
-        high_cols_ref[s], low_cols_ref[s] = split((mm(inv_high_ref[s], pick) + mm(inv_low_ref[s], pick)) * coup)
+        high, low = split((mm(inv_high_ref[s], pick) + mm(inv_low_ref[s], pick)) * (coup * weight))
+        gather_side(s, 1 - parity, pass_ref, rows, on_side_ref, on0_ref)
+        on1_ref[s] = pack_side(on_side_ref, s, 1)
+        off_ref[s] = pack_side(off_side_ref, s, 1)
+        high_cols_ref[s] = high
+        low_cols_ref[s] = low
         return carry
 
     lax.fori_loop(0, count, one_sub, 0)
 
 
-def second_kernel(poles, sent, table_ref, high_ref, low_ref, pass_ref, off_ref, on_ref, *out_refs):
-    count, ways, quarter, _ = pass_ref.shape
+def second_kernel(poles, half, sent, table_ref, wide_ref, high_ref, low_ref, pass_ref, off_ref, on_ref, *out_refs):
+    count, block_len, _ = pass_ref.shape
+    ways, quarter = 2, block_len // 4
     per_owner = count // poles
     steps = poles.bit_length() - 1
     me, parity = lax.axis_index("pole"), sub_parity()
@@ -161,9 +161,11 @@
                 for spot, way in enumerate(own_ways):
                     at = 2 * spot * quarter
                     top, bottom = out[at : at + quarter], out[at + quarter : at + 2 * quarter]
+                    at = 2 * way * quarter
+                    own = pack(pass_ref[sub, at : at + quarter, :], pass_ref[sub, at + quarter : at + 2 * quarter, :], half)
                     to = (c * len(own_ways) + spot) * quarter
                     out_refs[way if split_ways else 0][r // 2, to : to + quarter, :] = (
-                        jnp.where(left_lanes(top), top, bottom) + pass_ref[sub, way]
+                        jnp.where(left_lanes(top), top, bottom) + own * wide_ref[0:1, :]
                     )
 
 
@@ -346,7 +348,6 @@
     poles, groups = lax.axis_size("pole"), lax.axis_size("sub")
     fields = start_block.reshape(sub_count, block_len, vecs)
     shape = jax.ShapeDtypeStruct
-    smem = pl.BlockSpec(memory_space=pltpu.SMEM)
     hbm = pl.BlockSpec(memory_space=pltpu.HBM)
     vmem = pl.BlockSpec(memory_space=pltpu.VMEM)
     block_bytes = sub_count * block_len * block_len * 4
@@ -361,7 +362,7 @@
         (shape(fields.shape, f32), sides, packed, halves, halves),
         flops=8 * sub_count * block_len * block_len * vecs,
         moved=block_bytes + 3 * field_bytes,
-        in_specs=[smem] + [hbm] * 3,
+        in_specs=[hbm] * 3,
         out_specs=[vmem] * 5,
         scratch_shapes=[
             pltpu.VMEM(blocks.shape, f32),
@@ -372,46 +373,45 @@
             pltpu.SemaphoreType.DMA,
         ],
         name="first_pass",
-    )(pole_weights, *[in_hbm(v) for v in (blocks, fields, iface_rows)])
+    )(*[in_hbm(v) for v in (blocks, fields, iface_rows)])
     first, off_side, inv_high, inv_low = (in_vmem(v) for v in (first, off_side, inv_high, inv_low))
     across = [(s, (s + (1 if s % 2 else -1)) % groups) for s in range(groups)]
     inside = [(s, s ^ 1) for s in range(groups)]
     off_in0 = lax.ppermute(off0, "sub", across)
     cols = shape((sub_count, block_len, 2 * iface_len), bf16)
-    pass_half = shape((sub_count, 2, block_len // 4, vecs), f32)
-    cols_high, cols_low, pass0, pass1, off1, on0, on1, table = call(
+    cols_high, cols_low, off1, on0, on1, table, wide = call(
         columns_kernel,
-        (cols, cols, pass_half, pass_half, packed, packed, packed, shape((2, sub_count, 8, vecs), jnp.int32)),
+        (cols, cols, packed, packed, packed, shape((2, sub_count, 8, vecs), jnp.int32), shape((8, vecs), f32)),
         flops=8 * sub_count * block_len * block_len * iface_len,
         moved=2 * block_bytes,
-        in_specs=[hbm] + [vmem] * 7,
-        out_specs=[vmem] * 8,
+        in_specs=[hbm, pl.BlockSpec(memory_space=pltpu.SMEM)] + [vmem] * 7,
+        out_specs=[vmem] * 7,
         scratch_shapes=[
             pltpu.VMEM(sides.shape, f32),
             pltpu.SMEM(iface_rows.shape, jnp.int32),
             pltpu.SemaphoreType.DMA,
         ],
         name="interface_columns",
-    )(in_hbm(iface_rows), inv_high, inv_low, iface_rows, couplings, neighbors.T, first, off_side)
+    )(in_hbm(iface_rows), pole_weights, inv_high, inv_low, iface_rows, couplings, neighbors.T, first, off_side)
     on_in0 = lax.ppermute(on0, "sub", inside)
     on1, off_in0 = lax.optimization_barrier((on1, off_in0))
     halves = [(off_in0, on_in0), (lax.ppermute(off1, "sub", across), lax.ppermute(on1, "sub", inside))]
-    cols_high, cols_low, pass0, pass1 = (in_vmem(v) for v in (cols_high, cols_low, pass0, pass1))
+    cols_high, cols_low = in_vmem(cols_high), in_vmem(cols_low)
 
     per_owner = sub_count // poles
     steps = poles.bit_length() - 1
     pending = []
-    for arrays, own_pass, (off_in, on_in) in zip((2, 2), (pass0, pass1), halves):
+    for half, (arrays, (off_in, on_in)) in enumerate(zip((2, 2), halves)):
         send, keep = (
             call(
-                functools.partial(second_kernel, poles, sent),
+                functools.partial(second_kernel, poles, half, sent),
                 (shape((poles // 2, per_owner * block_len // (2 * arrays), vecs), f32),) * arrays,
                 flops=4 * sub_count * block_len * 2 * iface_len * vecs,
                 moved=2 * sub_count * block_len * vecs * 4,
-                in_specs=[vmem] * 6,
+                in_specs=[vmem] * 7,
                 out_specs=[vmem] * arrays,
                 name="second_pass",
-            )(table, cols_high, cols_low, own_pass, off_in, on_in)
+            )(table, wide, cols_high, cols_low, first, off_in, on_in)
             for sent in (1, 0)
         )
         pending.append([(a, [b]) for a, b in zip(send, keep)])
@@ -442,7 +442,11 @@
     )(*[v for arrays in summands for kept in arrays for v in kept])
 
     stages = [[(0, 1)], [(r, 0) for r in range(1, poles)]]
-    stages += [[(0, 1 << bit)] for bit in range(1, groups.bit_length() - 1)]
+    base = 2
+    while base < groups:
+        radix = min(4, groups // base)
+        stages.append([(0, base * r) for r in range(1, radix)])
+        base *= radix
     grams = [gram]
     for masks in stages:
         total = functools.reduce(jnp.add, grams)

time: 66 us -> 63.5 us (0.962)
  waiting for transfers between devices: 24.4 us -> 17.7 us
  starting transfers between devices: 19.2 us -> 23.5 us
    ppermute x14 -> x15, waiting for transfers between devices: 20.8 us -> 13.9 us  [swap(): return lax.ppermute(value, ('pole', 'sub'), pairs)]
    ppermute x14 -> x15, starting transfers between devices: 13.8 us -> 18.2 us  [swap(): return lax.ppermute(value, ('pole', 'sub'), pairs)]
  transfers between devices with their start and end apart: 18 -> 19, of which waited for: 13 -> 13; matrix products, arithmetic and copies ran while one was open for 0% -> 0% of each run, Pallas kernels for 15% -> 15%
where the time goes in v5:
time: 63.5 us; the launch traced here: 63.2 us
  starting transfers between devices  23.5 us (37%)
  Pallas kernels  21 us (33%)
  waiting for transfers between devices  17.7 us (28%)
  between operations  0.77 us (1%)
    ppermute x15, starting transfers between devices, swap(): return lax.ppermute(value, ('pole', 'sub'), pairs)  18.2 us
    ppermute x15, waiting for transfers between devices, swap(): return lax.ppermute(value, ('pole', 'sub'), pairs)  13.9 us
    pallas_call x1, Pallas kernels, per_device(): call(first_kernel, (shape(fields.shape, f32), sides, packed, halves, halv...  5.98 us
    pallas_call x1, Pallas kernels, per_device(): call(columns_kernel, (cols, cols, packed, packed, packed, shape((2, sub_c...  5.66 us
    pallas_call x1, Pallas kernels, per_device(): call(functools.partial(ortho_kernel, math.sqrt(total_rows)), shape((own_r...  4.9 us
    ppermute x1, starting transfers between devices, per_device(): off_in0 = lax.ppermute(off0, 'sub', across)  4.57 us
    pallas_call x4, Pallas kernels, per_device(): call(functools.partial(second_kernel, poles, half, sent), (shape((poles /...  3.93 us
    ppermute x1, waiting for transfers between devices, per_device(): lax.ppermute(off1, 'sub', across)  2.91 us
  transfers between devices with their start and end apart: 19, of which 13 were waited for; matrix products, arithmetic and copies ran while one was open for 0% of the time, Pallas kernels for 15%

profile of v5, /device:TPU:0, one launch (start us, length us, event | category | flops | bytes accessed | tf_op | source)
XLA Modules:
  0.0 63.2 jit_solution(13213136696784147888)
XLA Ops:
  0.0 6.0 %first_pass.1 = (f32[8,512,128]{2,1,0:T(8,128)S(1)}, f32[8,128,128]{2,1,0:T(8,128)S(1)}, f32[8,64,128]{2,1,0:T(8,128)S(1)}, bf16[8,512,512]{2,1,0:T(8,128)(2,1)S(1)}, bf16[8,512,512]{2,1,0:T(8,128)(2,1)S(1)}) custom-call(f32[8,512,512]{2,1,0:T(8,128)} %bitcast.4, f32[8,512,128]{2,1,0:T(8,128)} %bitcast.5, s32[8,2,128]{2,1,0:T(2,128)} %rows_ref.1), custom_call_target="tpu_custom_call" | custom-call | flops 2147483648 | bytes 14680064 | tf_op jit(solution)/shard_map/first_pass/pallas_call | solution.py:360
  6.0 4.6 %collective-permute-start = (f32[8,64,128]{2,1,0:T(8,128)S(1)}, f32[8,64,128]{2,1,0:T(8,128)S(1)}, u32[]{:S(2)}, u32[]{:S(2)}) collective-permute-start(f32[8,64,128]{2,1,0:T(8,128)S(1)} %get-tuple-element.38), channel_id=1, source_target_pairs={{0,7},{1,2},{2,1},{3,4},{4,3},{5,6},{6,5},{7,0},{8,15},{9,10},{10,... | collective-permute-start | bytes 786440 | tf_op jit(solution)/shard_map/ppermute | solution.py:380
  11.2 5.7 %interface_columns.1 = (bf16[8,512,256]{2,1,0:T(8,128)(2,1)S(1)}, bf16[8,512,256]{2,1,0:T(8,128)(2,1)S(1)}, f32[8,64,128]{2,1,0:T(8,128)S(1)}, f32[8,64,128]{2,1...) custom-call(s32[8,2,128]{2,1,0:T(2,128)} %rows_ref.1, ...), custom_call_target="tpu_custom_call" | custom-call | flops 2147483648 | bytes 16777216 | tf_op jit(solution)/shard_map/interface_columns/pallas_call | solution.py:382
  18.5 1.0 %second_pass.5 = (f32[2,256,128]{2,1,0:T(8,128)S(1)}, f32[2,256,128]{2,1,0:T(8,128)S(1)}) custom-call(s32[2,8,8,128]{3,2,1,0:T(8,128)S(1)} %get-tuple-element.33.table_ref, f32[8,128]{1,0:T(8,128)S(1)} %get-tuple-element.34.wide_ref, bf16[8,512,256]{2,1,0:T(8,128)(2,1)S(1)} %get-tuple-element.35.high_ref, ...), custom_call_target="tpu_custom_call" | custom-call | flops 536870912 | bytes 4194304 | tf_op jit(solution)/shard_map/second_pass/pallas_call | solution.py:406
  19.5 1.6 %collective-permute-start.2 = (f32[2,256,128]{2,1,0:T(8,128)S(1)}, f32[2,256,128]{2,1,0:T(8,128)S(1)}, u32[]{:S(2)}, u32[]{:S(2)}) collective-permute-start(f32[2,256,128]{2,1,0:T(8,128)S(1)} %get-tuple-element.42), channel_id=1, source_target_pairs={{0,8},{1,9},{2,10},{3,11},{4,12},{5,13},{6,14},{7,15},{8,0},{9,1},... | collective-permute-start | bytes 786440 | tf_op jit(solution)/shard_map/ppermute | solution.py:340
  21.1 1.5 %collective-permute-start.4 = (f32[2,256,128]{2,1,0:T(8,128)S(1)}, f32[2,256,128]{2,1,0:T(8,128)S(1)}, u32[]{:S(2)}, u32[]{:S(2)}) collective-permute-start(f32[2,256,128]{2,1,0:T(8,128)S(1)} %get-tuple-element.44), channel_id=1, source_target_pairs={{0,16},{1,17},{2,18},{3,19},{4,20},{5,21},{6,22},{7,23},{8,24},{9,... | collective-permute-start | bytes 786440 | tf_op jit(solution)/shard_map/ppermute | solution.py:340
  22.6 1.0 %second_pass.4 = (f32[2,256,128]{2,1,0:T(8,128)S(1)}, f32[2,256,128]{2,1,0:T(8,128)S(1)}) custom-call(s32[2,8,8,128]{3,2,1,0:T(8,128)S(1)} %get-tuple-element.33.table_ref, f32[8,128]{1,0:T(8,128)S(1)} %get-tuple-element.34.wide_ref, bf16[8,512,256]{2,1,0:T(8,128)(2,1)S(1)} %get-tuple-element.35.high_ref, ...), custom_call_target="tpu_custom_call" | custom-call | flops 536870912 | bytes 4194304 | tf_op jit(solution)/shard_map/second_pass/pallas_call | solution.py:406
  23.6 2.9 %collective-permute-done.6.off_ref = f32[8,64,128]{2,1,0:T(8,128)S(1)} collective-permute-done((f32[8,64,128]{2,1,0:T(8,128)S(1)}, f32[8,64,128]{2,1,0:T(8,128)S(1)}, u32[]{:S(2)}, u32[]{:S(2)}) %collective-permute-start.6) | collective-permute-done | bytes 262176 | tf_op jit(solution)/shard_map/ppermute | solution.py:398
  26.5 1.0 %second_pass.7 = (f32[2,256,128]{2,1,0:T(8,128)S(1)}, f32[2,256,128]{2,1,0:T(8,128)S(1)}) custom-call(s32[2,8,8,128]{3,2,1,0:T(8,128)S(1)} %get-tuple-element.33.table_ref, f32[8,128]{1,0:T(8,128)S(1)} %get-tuple-element.34.wide_ref, bf16[8,512,256]{2,1,0:T(8,128)(2,1)S(1)} %get-tuple-element.35.high_ref, ...), custom_call_target="tpu_custom_call" | custom-call | flops 536870912 | bytes 4194304 | tf_op jit(solution)/shard_map/second_pass/pallas_call | solution.py:406
  27.5 1.6 %collective-permute-start.8 = (f32[2,256,128]{2,1,0:T(8,128)S(1)}, f32[2,256,128]{2,1,0:T(8,128)S(1)}, u32[]{:S(2)}, u32[]{:S(2)}) collective-permute-start(f32[2,256,128]{2,1,0:T(8,128)S(1)} %get-tuple-element.48), channel_id=1, source_target_pairs={{0,8},{1,9},{2,10},{3,11},{4,12},{5,13},{6,14},{7,15},{8,0},{9,1},... | collective-permute-start | bytes 786440 | tf_op jit(solution)/shard_map/ppermute | solution.py:340
  29.1 1.5 %collective-permute-start.10 = (f32[2,256,128]{2,1,0:T(8,128)S(1)}, f32[2,256,128]{2,1,0:T(8,128)S(1)}, u32[]{:S(2)}, u32[]{:S(2)}) collective-permute-start(f32[2,256,128]{2,1,0:T(8,128)S(1)} %get-tuple-element.50), channel_id=1, source_target_pairs={{0,16},{1,17},{2,18},{3,19},{4,20},{5,21},{6,22},{7,23},{8,24},{9,... | collective-permute-start | bytes 786440 | tf_op jit(solution)/shard_map/ppermute | solution.py:340
  32.8 3.1 %collective-permute-done.8 = f32[2,256,128]{2,1,0:T(8,128)S(1)} collective-permute-done((f32[2,256,128]{2,1,0:T(8,128)S(1)}, f32[2,256,128]{2,1,0:T(8,128)S(1)}, u32[]{:S(2)}, u32[]{:S(2)}) %collective-permute-start.8) | collective-permute-done | bytes 262176 | tf_op jit(solution)/shard_map/ppermute | solution.py:340
  35.9 1.6 %collective-permute-start.9 = (f32[1,256,128]{2,1,0:T(8,128)S(1)}, f32[1,256,128]{2,1,0:T(8,128)S(1)}, u32[]{:S(2)}, u32[]{:S(2)}) collective-permute-start(f32[1,256,128]{2,1,0:T(8,128)S(1)} %get-tuple-element.56), channel_id=1, source_target_pairs={{0,16},{1,17},{2,18},{3,19},{4,20},{5,21},{6,22},{7,23},{8,24},{9,... | collective-permute-start | bytes 393224 | tf_op jit(solution)/shard_map/ppermute | solution.py:340
  38.3 1.3 %collective-permute-start.11 = (f32[1,256,128]{2,1,0:T(8,128)S(1)}, f32[1,256,128]{2,1,0:T(8,128)S(1)}, u32[]{:S(2)}, u32[]{:S(2)}) collective-permute-start(f32[1,256,128]{2,1,0:T(8,128)S(1)} %get-tuple-element.53), channel_id=1, source_target_pairs={{0,8},{1,9},{2,10},{3,11},{4,12},{5,13},{6,14},{7,15},{8,0},{9,1},... | collective-permute-start | bytes 393224 | tf_op jit(solution)/shard_map/ppermute | solution.py:340
  39.9 1.4 %collective-permute-done.9.refs_8_ = f32[1,256,128]{2,1,0:T(8,128)S(1)} collective-permute-done((f32[1,256,128]{2,1,0:T(8,128)S(1)}, f32[1,256,128]{2,1,0:T(8,128)S(1)}, u32[]{:S(2)}, u32[]{:S(2)}) %collective-permute-start.9) | collective-permute-done | bytes 131104 | tf_op jit(solution)/shard_map/ppermute | solution.py:340
  41.3 2.1 %collective-permute-done.11.refs_11_ = f32[1,256,128]{2,1,0:T(8,128)S(1)} collective-permute-done((f32[1,256,128]{2,1,0:T(8,128)S(1)}, f32[1,256,128]{2,1,0:T(8,128)S(1)}, u32[]{:S(2)}, u32[]{:S(2)}) %collective-permute-start.11) | collective-permute-done | bytes 131104 | tf_op jit(solution)/shard_map/ppermute | solution.py:340
  44.0 1.2 %collective-permute-done.12 = f32[72,128]{1,0:T(8,128)S(1)} collective-permute-done((f32[72,128]{1,0:T(8,128)S(1)}, f32[72,128]{1,0:T(8,128)S(1)}, u32[]{:S(2)}, u32[]{:S(2)}) %collective-permute-start.12) | collective-permute-done | bytes 36896 | tf_op jit(solution)/shard_map/ppermute | solution.py:340
  45.2 1.4 %collective-permute-start.15 = (f32[72,128]{1,0:T(8,128)S(1)}, f32[72,128]{1,0:T(8,128)S(1)}, u32[]{:S(2)}, u32[]{:S(2)}) collective-permute-start(f32[72,128]{1,0:T(8,128)S(1)} %add.28), channel_id=1, source_target_pairs={{0,24},{1,25},{2,26},{3,27},{4,28},{5,29},{6,30},{7,31},{8,16},{9,... | collective-permute-start | bytes 110600 | tf_op jit(solution)/shard_map/ppermute | solution.py:340
  46.6 1.3 %collective-permute-start.14 = (f32[72,128]{1,0:T(8,128)S(1)}, f32[72,128]{1,0:T(8,128)S(1)}, u32[]{:S(2)}, u32[]{:S(2)}) collective-permute-start(f32[72,128]{1,0:T(8,128)S(1)} %add.28), channel_id=1, source_target_pairs={{0,16},{1,17},{2,18},{3,19},{4,20},{5,21},{6,22},{7,23},{8,24},{9,... | collective-permute-start | bytes 110600 | tf_op jit(solution)/shard_map/ppermute | solution.py:340
  48.7 1.4 %collective-permute-done.15 = f32[72,128]{1,0:T(8,128)S(1)} collective-permute-done((f32[72,128]{1,0:T(8,128)S(1)}, f32[72,128]{1,0:T(8,128)S(1)}, u32[]{:S(2)}, u32[]{:S(2)}) %collective-permute-start.15) | collective-permute-done | bytes 36896 | tf_op jit(solution)/shard_map/ppermute | solution.py:340
  50.6 1.3 %collective-permute-done.13 = f32[72,128]{1,0:T(8,128)S(1)} collective-permute-done((f32[72,128]{1,0:T(8,128)S(1)}, f32[72,128]{1,0:T(8,128)S(1)}, u32[]{:S(2)}, u32[]{:S(2)}) %collective-permute-start.13) | collective-permute-done | bytes 36896 | tf_op jit(solution)/shard_map/ppermute | solution.py:340
  52.5 3.9 %collective-permute-start.16 = (f32[72,128]{1,0:T(8,128)S(1)}, f32[72,128]{1,0:T(8,128)S(1)}, u32[]{:S(2)}, u32[]{:S(2)}) collective-permute-start(f32[72,128]{1,0:T(8,128)S(1)} %add_add_fusion.refs_0_), channel_id=1, source_target_pairs={{0,2},{1,3},{2,0},{3,1},{4,6},{5,7},{6,4},{7,5},{8,10},{9,11},{10,... | collective-permute-start | bytes 110600 | tf_op jit(solution)/shard_map/ppermute | solution.py:340
  56.4 1.4 %collective-permute-done.18.refs_3_ = f32[72,128]{1,0:T(8,128)S(1)} collective-permute-done((f32[72,128]{1,0:T(8,128)S(1)}, f32[72,128]{1,0:T(8,128)S(1)}, u32[]{:S(2)}, u32[]{:S(2)}) %collective-permute-start.18) | collective-permute-done | bytes 36896 | tf_op jit(solution)/shard_map/ppermute | solution.py:340
  58.3 4.9 %ortho.1 = f32[1024,128]{1,0:T(8,128)} custom-call(f32[72,128]{1,0:T(8,128)S(1)} %add_add_fusion.refs_0_, f32[72,128]{1,0:T(8,128)S(1)} %collective-permute-done.16.refs_1_, f32[72,128]{1,0:T(8,128)S(1)} %collective-permute-done.17.refs_2_, f32[72,128]{1,0:T(8,128)S(1)} %collective-permute-done.18.refs_3_, bf16[1024,256]{1,0:T(8,128)(2,1)S(1)} %get-tuple-element.52.refs_4_), custom_call_target="tpu_custom_call" | custom-call | flops 100663296 | bytes 1048576 | tf_op jit(solution)/shard_map/ortho/pallas_call | solution.py:456
  (32 shorter events, 8.0 us)
Async XLA Ops:
  0.0 11.2 %copy-start = (f32[8,2,128]{2,1,0:T(2,128)S(1)}, f32[8,2,128]{2,1,0:T(2,128)}, u32[]{:S(2)}) copy-start(f32[8,2,128]{2,1,0:T(2,128)} %coup_ref.1) | copy-start | bytes 24580
  0.0 11.2 %copy-start.1 = (s32[8,2]{0,1:T(2,128)S(1)}, s32[8,2]{0,1:T(2,128)}, u32[]{:S(2)}) copy-start(s32[8,2]{0,1:T(2,128)} %param.9) | copy-start | bytes 196
  6.0 11.6 %collective-permute-start = (f32[8,64,128]{2,1,0:T(8,128)S(1)}, f32[8,64,128]{2,1,0:T(8,128)S(1)}, u32[]{:S(2)}, u32[]{:S(2)}) collective-permute-start(f32[8,64,128]{2,1,0:T(8,128)S(1)} %get-tuple-element.38), channel_id=1, source_target_pairs={{0,7},{1,2},{2,1},{3,4},{4,3},{5,6},{6,5},{7,0},{8,15},{9,10},{10,... | collective-permute-start | bytes 786440 | tf_op jit(solution)/shard_map/ppermute | solution.py:380
  16.9 1.6 %collective-permute-start.1 = (f32[8,64,128]{2,1,0:T(8,128)S(1)}, f32[8,64,128]{2,1,0:T(8,128)S(1)}, u32[]{:S(2)}, u32[]{:S(2)}) collective-permute-start(f32[8,64,128]{2,1,0:T(8,128)S(1)} %get-tuple-element.40), channel_id=1, source_target_pairs={{0,1},{1,0},{2,3},{3,2},{4,5},{5,4},{6,7},{7,6},{8,9},{9,8},{10,11... | collective-permute-start | bytes 786440 | tf_op jit(solution)/shard_map/ppermute | solution.py:396
  17.0 9.5 %collective-permute-start.6 = (f32[8,64,128]{2,1,0:T(8,128)S(1)}, f32[8,64,128]{2,1,0:T(8,128)S(1)}, u32[]{:S(2)}, u32[]{:S(2)}) collective-permute-start(f32[8,64,128]{2,1,0:T(8,128)S(1)} %get-tuple-element.45), channel_id=1, source_target_pairs={{0,7},{1,2},{2,1},{3,4},{4,3},{5,6},{6,5},{7,0},{8,15},{9,10},{10,... | collective-permute-start | bytes 786440 | tf_op jit(solution)/shard_map/ppermute | solution.py:398
  17.6 8.9 %collective-permute-start.7 = (f32[8,64,128]{2,1,0:T(8,128)S(1)}, f32[8,64,128]{2,1,0:T(8,128)S(1)}, u32[]{:S(2)}, u32[]{:S(2)}) collective-permute-start(f32[8,64,128]{2,1,0:T(8,128)S(1)} %get-tuple-element.46), channel_id=1, source_target_pairs={{0,1},{1,0},{2,3},{3,2},{4,5},{5,4},{6,7},{7,6},{8,9},{9,8},{10,11... | collective-permute-start | bytes 786440 | tf_op jit(solution)/shard_map/ppermute | solution.py:398
  19.5 11.1 %collective-permute-start.2 = (f32[2,256,128]{2,1,0:T(8,128)S(1)}, f32[2,256,128]{2,1,0:T(8,128)S(1)}, u32[]{:S(2)}, u32[]{:S(2)}) collective-permute-start(f32[2,256,128]{2,1,0:T(8,128)S(1)} %get-tuple-element.42), channel_id=1, source_target_pairs={{0,8},{1,9},{2,10},{3,11},{4,12},{5,13},{6,14},{7,15},{8,0},{9,1},... | collective-permute-start | bytes 786440 | tf_op jit(solution)/shard_map/ppermute | solution.py:340
  21.1 10.1 %collective-permute-start.4 = (f32[2,256,128]{2,1,0:T(8,128)S(1)}, f32[2,256,128]{2,1,0:T(8,128)S(1)}, u32[]{:S(2)}, u32[]{:S(2)}) collective-permute-start(f32[2,256,128]{2,1,0:T(8,128)S(1)} %get-tuple-element.44), channel_id=1, source_target_pairs={{0,16},{1,17},{2,18},{3,19},{4,20},{5,21},{6,22},{7,23},{8,24},{9,... | collective-permute-start | bytes 786440 | tf_op jit(solution)/shard_map/ppermute | solution.py:340
  27.5 8.4 %collective-permute-start.8 = (f32[2,256,128]{2,1,0:T(8,128)S(1)}, f32[2,256,128]{2,1,0:T(8,128)S(1)}, u32[]{:S(2)}, u32[]{:S(2)}) collective-permute-start(f32[2,256,128]{2,1,0:T(8,128)S(1)} %get-tuple-element.48), channel_id=1, source_target_pairs={{0,8},{1,9},{2,10},{3,11},{4,12},{5,13},{6,14},{7,15},{8,0},{9,1},... | collective-permute-start | bytes 786440 | tf_op jit(solution)/shard_map/ppermute | solution.py:340
  29.1 9.2 %collective-permute-start.10 = (f32[2,256,128]{2,1,0:T(8,128)S(1)}, f32[2,256,128]{2,1,0:T(8,128)S(1)}, u32[]{:S(2)}, u32[]{:S(2)}) collective-permute-start(f32[2,256,128]{2,1,0:T(8,128)S(1)} %get-tuple-element.50), channel_id=1, source_target_pairs={{0,16},{1,17},{2,18},{3,19},{4,20},{5,21},{6,22},{7,23},{8,24},{9,... | collective-permute-start | bytes 786440 | tf_op jit(solution)/shard_map/ppermute | solution.py:340
  30.6 9.3 %collective-permute-start.3 = (f32[1,256,128]{2,1,0:T(8,128)S(1)}, f32[1,256,128]{2,1,0:T(8,128)S(1)}, u32[]{:S(2)}, u32[]{:S(2)}) collective-permute-start(f32[1,256,128]{2,1,0:T(8,128)S(1)} %get-tuple-element.62), channel_id=1, source_target_pairs={{0,16},{1,17},{2,18},{3,19},{4,20},{5,21},{6,22},{7,23},{8,24},{9,... | collective-permute-start | bytes 393224 | tf_op jit(solution)/shard_map/ppermute | solution.py:340
  31.2 8.7 %collective-permute-start.5 = (f32[1,256,128]{2,1,0:T(8,128)S(1)}, f32[1,256,128]{2,1,0:T(8,128)S(1)}, u32[]{:S(2)}, u32[]{:S(2)}) collective-permute-start(f32[1,256,128]{2,1,0:T(8,128)S(1)} %get-tuple-element.59), channel_id=1, source_target_pairs={{0,8},{1,9},{2,10},{3,11},{4,12},{5,13},{6,14},{7,15},{8,0},{9,1},... | collective-permute-start | bytes 393224 | tf_op jit(solution)/shard_map/ppermute | solution.py:340
  35.9 5.4 %collective-permute-start.9 = (f32[1,256,128]{2,1,0:T(8,128)S(1)}, f32[1,256,128]{2,1,0:T(8,128)S(1)}, u32[]{:S(2)}, u32[]{:S(2)}) collective-permute-start(f32[1,256,128]{2,1,0:T(8,128)S(1)} %get-tuple-element.56), channel_id=1, source_target_pairs={{0,16},{1,17},{2,18},{3,19},{4,20},{5,21},{6,22},{7,23},{8,24},{9,... | collective-permute-start | bytes 393224 | tf_op jit(solution)/shard_map/ppermute | solution.py:340
  38.3 5.0 %collective-permute-start.11 = (f32[1,256,128]{2,1,0:T(8,128)S(1)}, f32[1,256,128]{2,1,0:T(8,128)S(1)}, u32[]{:S(2)}, u32[]{:S(2)}) collective-permute-start(f32[1,256,128]{2,1,0:T(8,128)S(1)} %get-tuple-element.53), channel_id=1, source_target_pairs={{0,8},{1,9},{2,10},{3,11},{4,12},{5,13},{6,14},{7,15},{8,0},{9,1},... | collective-permute-start | bytes 393224 | tf_op jit(solution)/shard_map/ppermute | solution.py:340
  44.0 1.3 %collective-permute-start.12 = (f32[72,128]{1,0:T(8,128)S(1)}, f32[72,128]{1,0:T(8,128)S(1)}, u32[]{:S(2)}, u32[]{:S(2)}) collective-permute-start(f32[72,128]{1,0:T(8,128)S(1)} %get-tuple-element.51), channel_id=1, source_target_pairs={{0,1},{1,0},{2,3},{3,2},{4,5},{5,4},{6,7},{7,6},{8,9},{9,8},{10,11... | collective-permute-start | bytes 110600 | tf_op jit(solution)/shard_map/ppermute | solution.py:340
  45.2 4.9 %collective-permute-start.15 = (f32[72,128]{1,0:T(8,128)S(1)}, f32[72,128]{1,0:T(8,128)S(1)}, u32[]{:S(2)}, u32[]{:S(2)}) collective-permute-start(f32[72,128]{1,0:T(8,128)S(1)} %add.28), channel_id=1, source_target_pairs={{0,24},{1,25},{2,26},{3,27},{4,28},{5,29},{6,30},{7,31},{8,16},{9,... | collective-permute-start | bytes 110600 | tf_op jit(solution)/shard_map/ppermute | solution.py:340
  46.6 4.0 %collective-permute-start.14 = (f32[72,128]{1,0:T(8,128)S(1)}, f32[72,128]{1,0:T(8,128)S(1)}, u32[]{:S(2)}, u32[]{:S(2)}) collective-permute-start(f32[72,128]{1,0:T(8,128)S(1)} %add.28), channel_id=1, source_target_pairs={{0,16},{1,17},{2,18},{3,19},{4,20},{5,21},{6,22},{7,23},{8,24},{9,... | collective-permute-start | bytes 110600 | tf_op jit(solution)/shard_map/ppermute | solution.py:340
  47.9 4.0 %collective-permute-start.13 = (f32[72,128]{1,0:T(8,128)S(1)}, f32[72,128]{1,0:T(8,128)S(1)}, u32[]{:S(2)}, u32[]{:S(2)}) collective-permute-start(f32[72,128]{1,0:T(8,128)S(1)} %add.28), channel_id=1, source_target_pairs={{0,8},{1,9},{2,10},{3,11},{4,12},{5,13},{6,14},{7,15},{8,0},{9,1},... | collective-permute-start | bytes 110600 | tf_op jit(solution)/shard_map/ppermute | solution.py:340
  51.9 5.8 %collective-permute-start.18 = (f32[72,128]{1,0:T(8,128)S(1)}, f32[72,128]{1,0:T(8,128)S(1)}, u32[]{:S(2)}, u32[]{:S(2)}) collective-permute-start(f32[72,128]{1,0:T(8,128)S(1)} %add_add_fusion.refs_0_), channel_id=1, source_target_pairs={{0,6},{1,7},{2,4},{3,5},{4,2},{5,3},{6,0},{7,1},{8,14},{9,15},{10,... | collective-permute-start | bytes 110600 | tf_op jit(solution)/shard_map/ppermute | solution.py:340
  52.0 5.7 %collective-permute-start.17 = (f32[72,128]{1,0:T(8,128)S(1)}, f32[72,128]{1,0:T(8,128)S(1)}, u32[]{:S(2)}, u32[]{:S(2)}) collective-permute-start(f32[72,128]{1,0:T(8,128)S(1)} %add_add_fusion.refs_0_), channel_id=1, source_target_pairs={{0,4},{1,5},{2,6},{3,7},{4,0},{5,1},{6,2},{7,3},{8,12},{9,13},{10,... | collective-permute-start | bytes 110600 | tf_op jit(solution)/shard_map/ppermute | solution.py:340
  52.5 5.8 %collective-permute-start.16 = (f32[72,128]{1,0:T(8,128)S(1)}, f32[72,128]{1,0:T(8,128)S(1)}, u32[]{:S(2)}, u32[]{:S(2)}) collective-permute-start(f32[72,128]{1,0:T(8,128)S(1)} %add_add_fusion.refs_0_), channel_id=1, source_target_pairs={{0,2},{1,3},{2,0},{3,1},{4,6},{5,7},{6,4},{7,5},{8,10},{9,11},{10,... | collective-permute-start | bytes 110600 | tf_op jit(solution)/shard_map/ppermute | solution.py:340

commit v6 on v5

--- a/solution.py
+++ b/solution.py
@@ -90,8 +90,8 @@
     gather_side(count - 1, parity, pass_ref, rows, side_ref, off_ref)
 
 
-def columns_kernel(rows_hbm, weight_ref, inv_high_ref, inv_low_ref, rows_ref, coup_ref, near_ref, pass_ref, off_side_ref,
-                   high_cols_ref, low_cols_ref, off_ref, on0_ref, on1_ref, table_ref, wide_ref,
+def columns_kernel(rows_hbm, inv_high_ref, inv_low_ref, rows_ref, coup_ref, near_ref, pass_ref, off_side_ref,
+                   high_cols_ref, low_cols_ref, off_ref, on0_ref, on1_ref, table_ref,
                    on_side_ref, rows, rows_sem):
     count, block_len = inv_high_ref.shape[:2]
     iface_len = rows_ref.shape[2]
@@ -103,8 +103,6 @@
         near = lax.rem(near_ref[pl.ds(side, 1), :], count)
         for s in range(count):
             table_ref[spot, s] = jnp.broadcast_to(near[:, s : s + 1], table_ref.shape[2:])
-    weight = weight_ref[0]
-    wide_ref[...] = jnp.full(wide_ref.shape, weight, f32)
     place = lax.broadcasted_iota(jnp.int32, (block_len, 2 * iface_len), 0)
     rows_copy.wait()
 
@@ -114,7 +112,7 @@
             for ref in (rows_ref, coup_ref)
         )
         pick = (at == place).astype(f32).astype(bf16)
-        high, low = split((mm(inv_high_ref[s], pick) + mm(inv_low_ref[s], pick)) * (coup * weight))
+        high, low = split((mm(inv_high_ref[s], pick) + mm(inv_low_ref[s], pick)) * coup)
         gather_side(s, 1 - parity, pass_ref, rows, on_side_ref, on0_ref)
         on1_ref[s] = pack_side(on_side_ref, s, 1)
         off_ref[s] = pack_side(off_side_ref, s, 1)
@@ -125,7 +123,7 @@
     lax.fori_loop(0, count, one_sub, 0)
 
 
-def second_kernel(poles, half, sent, table_ref, wide_ref, high_ref, low_ref, pass_ref, off_ref, on_ref, *out_refs):
+def second_kernel(poles, half, sent, weight_ref, table_ref, high_ref, low_ref, pass_ref, off_ref, on_ref, *out_refs):
     count, block_len, _ = pass_ref.shape
     ways, quarter = 2, block_len // 4
     per_owner = count // poles
@@ -164,8 +162,8 @@
                     at = 2 * way * quarter
                     own = pack(pass_ref[sub, at : at + quarter, :], pass_ref[sub, at + quarter : at + 2 * quarter, :], half)
                     to = (c * len(own_ways) + spot) * quarter
-                    out_refs[way if split_ways else 0][r // 2, to : to + quarter, :] = (
-                        jnp.where(left_lanes(top), top, bottom) + own * wide_ref[0:1, :]
+                    out_refs[way if split_ways else 0][r // 2, to : to + quarter, :] = weight_ref[0] * (
+                        jnp.where(left_lanes(top), top, bottom) + own
                     )
 
 
@@ -379,20 +377,20 @@
     inside = [(s, s ^ 1) for s in range(groups)]
     off_in0 = lax.ppermute(off0, "sub", across)
     cols = shape((sub_count, block_len, 2 * iface_len), bf16)
-    cols_high, cols_low, off1, on0, on1, table, wide = call(
+    cols_high, cols_low, off1, on0, on1, table = call(
         columns_kernel,
-        (cols, cols, packed, packed, packed, shape((2, sub_count, 8, vecs), jnp.int32), shape((8, vecs), f32)),
+        (cols, cols, packed, packed, packed, shape((2, sub_count, 8, vecs), jnp.int32)),
         flops=8 * sub_count * block_len * block_len * iface_len,
         moved=2 * block_bytes,
-        in_specs=[hbm, pl.BlockSpec(memory_space=pltpu.SMEM)] + [vmem] * 7,
-        out_specs=[vmem] * 7,
+        in_specs=[hbm] + [vmem] * 7,
+        out_specs=[vmem] * 6,
         scratch_shapes=[
             pltpu.VMEM(sides.shape, f32),
             pltpu.SMEM(iface_rows.shape, jnp.int32),
             pltpu.SemaphoreType.DMA,
         ],
         name="interface_columns",
-    )(in_hbm(iface_rows), pole_weights, inv_high, inv_low, iface_rows, couplings, neighbors.T, first, off_side)
+    )(in_hbm(iface_rows), inv_high, inv_low, iface_rows, couplings, neighbors.T, first, off_side)
     on_in0 = lax.ppermute(on0, "sub", inside)
     on1, off_in0 = lax.optimization_barrier((on1, off_in0))
     halves = [(off_in0, on_in0), (lax.ppermute(off1, "sub", across), lax.ppermute(on1, "sub", inside))]
@@ -408,10 +406,10 @@
                 (shape((poles // 2, per_owner * block_len // (2 * arrays), vecs), f32),) * arrays,
                 flops=4 * sub_count * block_len * 2 * iface_len * vecs,
                 moved=2 * sub_count * block_len * vecs * 4,
-                in_specs=[vmem] * 7,
+                in_specs=[pl.BlockSpec(memory_space=pltpu.SMEM)] + [vmem] * 6,
                 out_specs=[vmem] * arrays,
                 name="second_pass",
-            )(table, wide, cols_high, cols_low, first, off_in, on_in)
+            )(pole_weights, table, cols_high, cols_low, first, off_in, on_in)
             for sent in (1, 0)
         )
         pending.append([(a, [b]) for a, b in zip(send, keep)])

time: 63.5 us -> 63.6 us (level)
    ppermute x15, waiting for transfers between devices: 13.9 us -> 14.8 us  [swap(): return lax.ppermute(value, ('pole', 'sub'), pairs)]
    ppermute x1, waiting for transfers between devices: 0.87 us -> 0.1 us  [per_device(): on_in0 = lax.ppermute(on0, 'sub', inside)]
where the time goes in v6:
time: 63.6 us; the launch traced here: 63.3 us
  starting transfers between devices  23.5 us (37%)
  Pallas kernels  21 us (33%)
  waiting for transfers between devices  17.8 us (28%)
  between operations  0.78 us (1%)
    ppermute x15, starting transfers between devices, swap(): return lax.ppermute(value, ('pole', 'sub'), pairs)  18.1 us
    ppermute x15, waiting for transfers between devices, swap(): return lax.ppermute(value, ('pole', 'sub'), pairs)  14.8 us
    pallas_call x1, Pallas kernels, per_device(): call(first_kernel, (shape(fields.shape, f32), sides, packed, halves, halv...  5.97 us
    pallas_call x1, Pallas kernels, per_device(): call(columns_kernel, (cols, cols, packed, packed, packed, shape((2, sub_c...  5.66 us
    pallas_call x1, Pallas kernels, per_device(): call(functools.partial(ortho_kernel, math.sqrt(total_rows)), shape((own_r...  4.91 us
    ppermute x1, starting transfers between devices, per_device(): off_in0 = lax.ppermute(off0, 'sub', across)  4.57 us
    pallas_call x4, Pallas kernels, per_device(): call(functools.partial(second_kernel, poles, half, sent), (shape((poles /...  3.88 us
    ppermute x1, waiting for transfers between devices, per_device(): lax.ppermute(off1, 'sub', across)  2.98 us
  transfers between devices with their start and end apart: 19, of which 13 were waited for; matrix products, arithmetic and copies ran while one was open for 0% of the time, Pallas kernels for 15%

profile of v6, /device:TPU:0, one launch (start us, length us, event | category | flops | bytes accessed | tf_op | source)
XLA Modules:
  0.0 63.3 jit_solution(2807970640533954961)
XLA Ops:
  0.0 6.0 %first_pass.1 = (f32[8,512,128]{2,1,0:T(8,128)S(1)}, f32[8,128,128]{2,1,0:T(8,128)S(1)}, f32[8,64,128]{2,1,0:T(8,128)S(1)}, bf16[8,512,512]{2,1,0:T(8,128)(2,1)S(1)}, bf16[8,512,512]{2,1,0:T(8,128)(2,1)S(1)}) custom-call(f32[8,512,512]{2,1,0:T(8,128)} %bitcast.4, f32[8,512,128]{2,1,0:T(8,128)} %bitcast.5, s32[8,2,128]{2,1,0:T(2,128)} %rows_ref.1), custom_call_target="tpu_custom_call" | custom-call | flops 2147483648 | bytes 14680064 | tf_op jit(solution)/shard_map/first_pass/pallas_call | solution.py:358
  6.0 4.6 %collective-permute-start = (f32[8,64,128]{2,1,0:T(8,128)S(1)}, f32[8,64,128]{2,1,0:T(8,128)S(1)}, u32[]{:S(2)}, u32[]{:S(2)}) collective-permute-start(f32[8,64,128]{2,1,0:T(8,128)S(1)} %get-tuple-element.36), channel_id=1, source_target_pairs={{0,7},{1,2},{2,1},{3,4},{4,3},{5,6},{6,5},{7,0},{8,15},{9,10},{10,... | collective-permute-start | bytes 786440 | tf_op jit(solution)/shard_map/ppermute | solution.py:378
  10.6 5.7 %interface_columns.1 = (bf16[8,512,256]{2,1,0:T(8,128)(2,1)S(1)}, bf16[8,512,256]{2,1,0:T(8,128)(2,1)S(1)}, f32[8,64,128]{2,1,0:T(8,128)S(1)}, f32[8,64,128]{2,1...) custom-call(s32[8,2,128]{2,1,0:T(2,128)} %rows_ref.1, ...), custom_call_target="tpu_custom_call" | custom-call | flops 2147483648 | bytes 16777216 | tf_op jit(solution)/shard_map/interface_columns/pallas_call | solution.py:380
  17.8 1.0 %second_pass.5 = (f32[2,256,128]{2,1,0:T(8,128)S(1)}, f32[2,256,128]{2,1,0:T(8,128)S(1)}) custom-call(f32[1]{0:T(128)S(6)} %copy.7.weight_ref, s32[2,8,8,128]{3,2,1,0:T(8,128)S(1)} %get-tuple-element.32.table_ref, bf16[8,512,256]{2,1,0:T(8,128)(2,1)S(1)} %get-tuple-element.33.high_ref, bf16[8,512,256]{2,1,0:T(8,128)(2,1)S(1)} %get-tuple-element.34.low_ref, ...), custom_call_target="tpu_custom_call" | custom-call | flops 536870912 | bytes 4194304 | tf_op jit(solution)/shard_map/second_pass/pallas_call | solution.py:404
  18.8 1.6 %collective-permute-start.4 = (f32[2,256,128]{2,1,0:T(8,128)S(1)}, f32[2,256,128]{2,1,0:T(8,128)S(1)}, u32[]{:S(2)}, u32[]{:S(2)}) collective-permute-start(f32[2,256,128]{2,1,0:T(8,128)S(1)} %get-tuple-element.42), channel_id=1, source_target_pairs={{0,16},{1,17},{2,18},{3,19},{4,20},{5,21},{6,22},{7,23},{8,24},{9,... | collective-permute-start | bytes 786440 | tf_op jit(solution)/shard_map/ppermute | solution.py:338
  20.4 1.5 %collective-permute-start.2 = (f32[2,256,128]{2,1,0:T(8,128)S(1)}, f32[2,256,128]{2,1,0:T(8,128)S(1)}, u32[]{:S(2)}, u32[]{:S(2)}) collective-permute-start(f32[2,256,128]{2,1,0:T(8,128)S(1)} %get-tuple-element.40), channel_id=1, source_target_pairs={{0,8},{1,9},{2,10},{3,11},{4,12},{5,13},{6,14},{7,15},{8,0},{9,1},... | collective-permute-start | bytes 786440 | tf_op jit(solution)/shard_map/ppermute | solution.py:338
  22.8 3.0 %collective-permute-done.6.off_ref = f32[8,64,128]{2,1,0:T(8,128)S(1)} collective-permute-done((f32[8,64,128]{2,1,0:T(8,128)S(1)}, f32[8,64,128]{2,1,0:T(8,128)S(1)}, u32[]{:S(2)}, u32[]{:S(2)}) %collective-permute-start.6) | collective-permute-done | bytes 262176 | tf_op jit(solution)/shard_map/ppermute | solution.py:396
  25.8 1.0 %second_pass.7 = (f32[2,256,128]{2,1,0:T(8,128)S(1)}, f32[2,256,128]{2,1,0:T(8,128)S(1)}) custom-call(f32[1]{0:T(128)S(6)} %copy.7.weight_ref, s32[2,8,8,128]{3,2,1,0:T(8,128)S(1)} %get-tuple-element.32.table_ref, bf16[8,512,256]{2,1,0:T(8,128)(2,1)S(1)} %get-tuple-element.33.high_ref, bf16[8,512,256]{2,1,0:T(8,128)(2,1)S(1)} %get-tuple-element.34.low_ref, ...), custom_call_target="tpu_custom_call" | custom-call | flops 536870912 | bytes 4194304 | tf_op jit(solution)/shard_map/second_pass/pallas_call | solution.py:404
  26.8 1.6 %collective-permute-start.10 = (f32[2,256,128]{2,1,0:T(8,128)S(1)}, f32[2,256,128]{2,1,0:T(8,128)S(1)}, u32[]{:S(2)}, u32[]{:S(2)}) collective-permute-start(f32[2,256,128]{2,1,0:T(8,128)S(1)} %get-tuple-element.48), channel_id=1, source_target_pairs={{0,16},{1,17},{2,18},{3,19},{4,20},{5,21},{6,22},{7,23},{8,24},{9,... | collective-permute-start | bytes 786440 | tf_op jit(solution)/shard_map/ppermute | solution.py:338
  28.4 1.5 %collective-permute-start.8 = (f32[2,256,128]{2,1,0:T(8,128)S(1)}, f32[2,256,128]{2,1,0:T(8,128)S(1)}, u32[]{:S(2)}, u32[]{:S(2)}) collective-permute-start(f32[2,256,128]{2,1,0:T(8,128)S(1)} %get-tuple-element.46), channel_id=1, source_target_pairs={{0,8},{1,9},{2,10},{3,11},{4,12},{5,13},{6,14},{7,15},{8,0},{9,1},... | collective-permute-start | bytes 786440 | tf_op jit(solution)/shard_map/ppermute | solution.py:338
  32.1 3.1 %collective-permute-done.10 = f32[2,256,128]{2,1,0:T(8,128)S(1)} collective-permute-done((f32[2,256,128]{2,1,0:T(8,128)S(1)}, f32[2,256,128]{2,1,0:T(8,128)S(1)}, u32[]{:S(2)}, u32[]{:S(2)}) %collective-permute-start.10) | collective-permute-done | bytes 262176 | tf_op jit(solution)/shard_map/ppermute | solution.py:338
  35.3 1.5 %collective-permute-start.11 = (f32[1,256,128]{2,1,0:T(8,128)S(1)}, f32[1,256,128]{2,1,0:T(8,128)S(1)}, u32[]{:S(2)}, u32[]{:S(2)}) collective-permute-start(f32[1,256,128]{2,1,0:T(8,128)S(1)} %get-tuple-element.51), channel_id=1, source_target_pairs={{0,8},{1,9},{2,10},{3,11},{4,12},{5,13},{6,14},{7,15},{8,0},{9,1},... | collective-permute-start | bytes 393224 | tf_op jit(solution)/shard_map/ppermute | solution.py:338
  37.7 1.2 %collective-permute-start.9 = (f32[1,256,128]{2,1,0:T(8,128)S(1)}, f32[1,256,128]{2,1,0:T(8,128)S(1)}, u32[]{:S(2)}, u32[]{:S(2)}) collective-permute-start(f32[1,256,128]{2,1,0:T(8,128)S(1)} %get-tuple-element.54), channel_id=1, source_target_pairs={{0,16},{1,17},{2,18},{3,19},{4,20},{5,21},{6,22},{7,23},{8,24},{9,... | collective-permute-start | bytes 393224 | tf_op jit(solution)/shard_map/ppermute | solution.py:338
  39.3 1.4 %collective-permute-done.11.refs_11_ = f32[1,256,128]{2,1,0:T(8,128)S(1)} collective-permute-done((f32[1,256,128]{2,1,0:T(8,128)S(1)}, f32[1,256,128]{2,1,0:T(8,128)S(1)}, u32[]{:S(2)}, u32[]{:S(2)}) %collective-permute-start.11) | collective-permute-done | bytes 131104 | tf_op jit(solution)/shard_map/ppermute | solution.py:338
  40.7 2.1 %collective-permute-done.9.refs_8_ = f32[1,256,128]{2,1,0:T(8,128)S(1)} collective-permute-done((f32[1,256,128]{2,1,0:T(8,128)S(1)}, f32[1,256,128]{2,1,0:T(8,128)S(1)}, u32[]{:S(2)}, u32[]{:S(2)}) %collective-permute-start.9) | collective-permute-done | bytes 131104 | tf_op jit(solution)/shard_map/ppermute | solution.py:338
  43.4 1.2 %collective-permute-done.12 = f32[72,128]{1,0:T(8,128)S(1)} collective-permute-done((f32[72,128]{1,0:T(8,128)S(1)}, f32[72,128]{1,0:T(8,128)S(1)}, u32[]{:S(2)}, u32[]{:S(2)}) %collective-permute-start.12) | collective-permute-done | bytes 36896 | tf_op jit(solution)/shard_map/ppermute | solution.py:338
  44.6 1.5 %collective-permute-start.13 = (f32[72,128]{1,0:T(8,128)S(1)}, f32[72,128]{1,0:T(8,128)S(1)}, u32[]{:S(2)}, u32[]{:S(2)}) collective-permute-start(f32[72,128]{1,0:T(8,128)S(1)} %add.28), channel_id=1, source_target_pairs={{0,8},{1,9},{2,10},{3,11},{4,12},{5,13},{6,14},{7,15},{8,0},{9,1},... | collective-permute-start | bytes 110600 | tf_op jit(solution)/shard_map/ppermute | solution.py:338
  46.5 1.6 %collective-permute-start.15 = (f32[72,128]{1,0:T(8,128)S(1)}, f32[72,128]{1,0:T(8,128)S(1)}, u32[]{:S(2)}, u32[]{:S(2)}) collective-permute-start(f32[72,128]{1,0:T(8,128)S(1)} %add.28), channel_id=1, source_target_pairs={{0,24},{1,25},{2,26},{3,27},{4,28},{5,29},{6,30},{7,31},{8,16},{9,... | collective-permute-start | bytes 110600 | tf_op jit(solution)/shard_map/ppermute | solution.py:338
  48.6 1.8 %collective-permute-done.14 = f32[72,128]{1,0:T(8,128)S(1)} collective-permute-done((f32[72,128]{1,0:T(8,128)S(1)}, f32[72,128]{1,0:T(8,128)S(1)}, u32[]{:S(2)}, u32[]{:S(2)}) %collective-permute-start.14) | collective-permute-done | bytes 36896 | tf_op jit(solution)/shard_map/ppermute | solution.py:338
  50.4 1.0 %collective-permute-done.15 = f32[72,128]{1,0:T(8,128)S(1)} collective-permute-done((f32[72,128]{1,0:T(8,128)S(1)}, f32[72,128]{1,0:T(8,128)S(1)}, u32[]{:S(2)}, u32[]{:S(2)}) %collective-permute-start.15) | collective-permute-done | bytes 36896 | tf_op jit(solution)/shard_map/ppermute | solution.py:338
  51.5 1.1 %collective-permute-start.17 = (f32[72,128]{1,0:T(8,128)S(1)}, f32[72,128]{1,0:T(8,128)S(1)}, u32[]{:S(2)}, u32[]{:S(2)}) collective-permute-start(f32[72,128]{1,0:T(8,128)S(1)} %add_add_fusion.refs_0_), channel_id=1, source_target_pairs={{0,4},{1,5},{2,6},{3,7},{4,0},{5,1},{6,2},{7,3},{8,12},{9,13},{10,... | collective-permute-start | bytes 110600 | tf_op jit(solution)/shard_map/ppermute | solution.py:338
  52.6 3.2 %collective-permute-start.18 = (f32[72,128]{1,0:T(8,128)S(1)}, f32[72,128]{1,0:T(8,128)S(1)}, u32[]{:S(2)}, u32[]{:S(2)}) collective-permute-start(f32[72,128]{1,0:T(8,128)S(1)} %add_add_fusion.refs_0_), channel_id=1, source_target_pairs={{0,6},{1,7},{2,4},{3,5},{4,2},{5,3},{6,0},{7,1},{8,14},{9,15},{10,... | collective-permute-start | bytes 110600 | tf_op jit(solution)/shard_map/ppermute | solution.py:338
  56.4 2.0 %collective-permute-done.18.refs_3_ = f32[72,128]{1,0:T(8,128)S(1)} collective-permute-done((f32[72,128]{1,0:T(8,128)S(1)}, f32[72,128]{1,0:T(8,128)S(1)}, u32[]{:S(2)}, u32[]{:S(2)}) %collective-permute-start.18) | collective-permute-done | bytes 36896 | tf_op jit(solution)/shard_map/ppermute | solution.py:338
  58.4 4.9 %ortho.1 = f32[1024,128]{1,0:T(8,128)} custom-call(f32[72,128]{1,0:T(8,128)S(1)} %add_add_fusion.refs_0_, f32[72,128]{1,0:T(8,128)S(1)} %collective-permute-done.16.refs_1_, f32[72,128]{1,0:T(8,128)S(1)} %collective-permute-done.17.refs_2_, f32[72,128]{1,0:T(8,128)S(1)} %collective-permute-done.18.refs_3_, bf16[1024,256]{1,0:T(8,128)(2,1)S(1)} %get-tuple-element.50.refs_4_), custom_call_target="tpu_custom_call" | custom-call | flops 100663296 | bytes 1048576 | tf_op jit(solution)/shard_map/ortho/pallas_call | solution.py:454
  (32 shorter events, 7.4 us)
Async XLA Ops:
  0.0 10.6 %copy-start = (f32[8,2,128]{2,1,0:T(2,128)S(1)}, f32[8,2,128]{2,1,0:T(2,128)}, u32[]{:S(2)}) copy-start(f32[8,2,128]{2,1,0:T(2,128)} %coup_ref.1) | copy-start | bytes 24580
  0.0 10.6 %copy-start.1 = (s32[8,2]{0,1:T(2,128)S(1)}, s32[8,2]{0,1:T(2,128)}, u32[]{:S(2)}) copy-start(s32[8,2]{0,1:T(2,128)} %param.9) | copy-start | bytes 196
  6.0 11.7 %collective-permute-start = (f32[8,64,128]{2,1,0:T(8,128)S(1)}, f32[8,64,128]{2,1,0:T(8,128)S(1)}, u32[]{:S(2)}, u32[]{:S(2)}) collective-permute-start(f32[8,64,128]{2,1,0:T(8,128)S(1)} %get-tuple-element.36), channel_id=1, source_target_pairs={{0,7},{1,2},{2,1},{3,4},{4,3},{5,6},{6,5},{7,0},{8,15},{9,10},{10,... | collective-permute-start | bytes 786440 | tf_op jit(solution)/shard_map/ppermute | solution.py:378
  16.2 1.6 %collective-permute-start.1 = (f32[8,64,128]{2,1,0:T(8,128)S(1)}, f32[8,64,128]{2,1,0:T(8,128)S(1)}, u32[]{:S(2)}, u32[]{:S(2)}) collective-permute-start(f32[8,64,128]{2,1,0:T(8,128)S(1)} %get-tuple-element.38), channel_id=1, source_target_pairs={{0,1},{1,0},{2,3},{3,2},{4,5},{5,4},{6,7},{7,6},{8,9},{9,8},{10,11... | collective-permute-start | bytes 786440 | tf_op jit(solution)/shard_map/ppermute | solution.py:394
  16.3 9.5 %collective-permute-start.6 = (f32[8,64,128]{2,1,0:T(8,128)S(1)}, f32[8,64,128]{2,1,0:T(8,128)S(1)}, u32[]{:S(2)}, u32[]{:S(2)}) collective-permute-start(f32[8,64,128]{2,1,0:T(8,128)S(1)} %get-tuple-element.43), channel_id=1, source_target_pairs={{0,7},{1,2},{2,1},{3,4},{4,3},{5,6},{6,5},{7,0},{8,15},{9,10},{10,... | collective-permute-start | bytes 786440 | tf_op jit(solution)/shard_map/ppermute | solution.py:396
  17.7 8.2 %collective-permute-start.7 = (f32[8,64,128]{2,1,0:T(8,128)S(1)}, f32[8,64,128]{2,1,0:T(8,128)S(1)}, u32[]{:S(2)}, u32[]{:S(2)}) collective-permute-start(f32[8,64,128]{2,1,0:T(8,128)S(1)} %get-tuple-element.44), channel_id=1, source_target_pairs={{0,1},{1,0},{2,3},{3,2},{4,5},{5,4},{6,7},{7,6},{8,9},{9,8},{10,11... | collective-permute-start | bytes 786440 | tf_op jit(solution)/shard_map/ppermute | solution.py:396
  18.8 11.1 %collective-permute-start.4 = (f32[2,256,128]{2,1,0:T(8,128)S(1)}, f32[2,256,128]{2,1,0:T(8,128)S(1)}, u32[]{:S(2)}, u32[]{:S(2)}) collective-permute-start(f32[2,256,128]{2,1,0:T(8,128)S(1)} %get-tuple-element.42), channel_id=1, source_target_pairs={{0,16},{1,17},{2,18},{3,19},{4,20},{5,21},{6,22},{7,23},{8,24},{9,... | collective-permute-start | bytes 786440 | tf_op jit(solution)/shard_map/ppermute | solution.py:338
  20.4 10.2 %collective-permute-start.2 = (f32[2,256,128]{2,1,0:T(8,128)S(1)}, f32[2,256,128]{2,1,0:T(8,128)S(1)}, u32[]{:S(2)}, u32[]{:S(2)}) collective-permute-start(f32[2,256,128]{2,1,0:T(8,128)S(1)} %get-tuple-element.40), channel_id=1, source_target_pairs={{0,8},{1,9},{2,10},{3,11},{4,12},{5,13},{6,14},{7,15},{8,0},{9,1},... | collective-permute-start | bytes 786440 | tf_op jit(solution)/shard_map/ppermute | solution.py:338
  26.8 8.4 %collective-permute-start.10 = (f32[2,256,128]{2,1,0:T(8,128)S(1)}, f32[2,256,128]{2,1,0:T(8,128)S(1)}, u32[]{:S(2)}, u32[]{:S(2)}) collective-permute-start(f32[2,256,128]{2,1,0:T(8,128)S(1)} %get-tuple-element.48), channel_id=1, source_target_pairs={{0,16},{1,17},{2,18},{3,19},{4,20},{5,21},{6,22},{7,23},{8,24},{9,... | collective-permute-start | bytes 786440 | tf_op jit(solution)/shard_map/ppermute | solution.py:338
  28.4 9.2 %collective-permute-start.8 = (f32[2,256,128]{2,1,0:T(8,128)S(1)}, f32[2,256,128]{2,1,0:T(8,128)S(1)}, u32[]{:S(2)}, u32[]{:S(2)}) collective-permute-start(f32[2,256,128]{2,1,0:T(8,128)S(1)} %get-tuple-element.46), channel_id=1, source_target_pairs={{0,8},{1,9},{2,10},{3,11},{4,12},{5,13},{6,14},{7,15},{8,0},{9,1},... | collective-permute-start | bytes 786440 | tf_op jit(solution)/shard_map/ppermute | solution.py:338
  30.0 9.3 %collective-permute-start.5 = (f32[1,256,128]{2,1,0:T(8,128)S(1)}, f32[1,256,128]{2,1,0:T(8,128)S(1)}, u32[]{:S(2)}, u32[]{:S(2)}) collective-permute-start(f32[1,256,128]{2,1,0:T(8,128)S(1)} %get-tuple-element.57), channel_id=1, source_target_pairs={{0,8},{1,9},{2,10},{3,11},{4,12},{5,13},{6,14},{7,15},{8,0},{9,1},... | collective-permute-start | bytes 393224 | tf_op jit(solution)/shard_map/ppermute | solution.py:338
  30.6 8.6 %collective-permute-start.3 = (f32[1,256,128]{2,1,0:T(8,128)S(1)}, f32[1,256,128]{2,1,0:T(8,128)S(1)}, u32[]{:S(2)}, u32[]{:S(2)}) collective-permute-start(f32[1,256,128]{2,1,0:T(8,128)S(1)} %get-tuple-element.60), channel_id=1, source_target_pairs={{0,16},{1,17},{2,18},{3,19},{4,20},{5,21},{6,22},{7,23},{8,24},{9,... | collective-permute-start | bytes 393224 | tf_op jit(solution)/shard_map/ppermute | solution.py:338
  35.3 5.4 %collective-permute-start.11 = (f32[1,256,128]{2,1,0:T(8,128)S(1)}, f32[1,256,128]{2,1,0:T(8,128)S(1)}, u32[]{:S(2)}, u32[]{:S(2)}) collective-permute-start(f32[1,256,128]{2,1,0:T(8,128)S(1)} %get-tuple-element.51), channel_id=1, source_target_pairs={{0,8},{1,9},{2,10},{3,11},{4,12},{5,13},{6,14},{7,15},{8,0},{9,1},... | collective-permute-start | bytes 393224 | tf_op jit(solution)/shard_map/ppermute | solution.py:338
  37.7 5.0 %collective-permute-start.9 = (f32[1,256,128]{2,1,0:T(8,128)S(1)}, f32[1,256,128]{2,1,0:T(8,128)S(1)}, u32[]{:S(2)}, u32[]{:S(2)}) collective-permute-start(f32[1,256,128]{2,1,0:T(8,128)S(1)} %get-tuple-element.54), channel_id=1, source_target_pairs={{0,16},{1,17},{2,18},{3,19},{4,20},{5,21},{6,22},{7,23},{8,24},{9,... | collective-permute-start | bytes 393224 | tf_op jit(solution)/shard_map/ppermute | solution.py:338
  43.3 1.3 %collective-permute-start.12 = (f32[72,128]{1,0:T(8,128)S(1)}, f32[72,128]{1,0:T(8,128)S(1)}, u32[]{:S(2)}, u32[]{:S(2)}) collective-permute-start(f32[72,128]{1,0:T(8,128)S(1)} %get-tuple-element.49), channel_id=1, source_target_pairs={{0,1},{1,0},{2,3},{3,2},{4,5},{5,4},{6,7},{7,6},{8,9},{9,8},{10,11... | collective-permute-start | bytes 110600 | tf_op jit(solution)/shard_map/ppermute | solution.py:338
  44.6 4.0 %collective-permute-start.13 = (f32[72,128]{1,0:T(8,128)S(1)}, f32[72,128]{1,0:T(8,128)S(1)}, u32[]{:S(2)}, u32[]{:S(2)}) collective-permute-start(f32[72,128]{1,0:T(8,128)S(1)} %add.28), channel_id=1, source_target_pairs={{0,8},{1,9},{2,10},{3,11},{4,12},{5,13},{6,14},{7,15},{8,0},{9,1},... | collective-permute-start | bytes 110600 | tf_op jit(solution)/shard_map/ppermute | solution.py:338
  46.1 4.3 %collective-permute-start.14 = (f32[72,128]{1,0:T(8,128)S(1)}, f32[72,128]{1,0:T(8,128)S(1)}, u32[]{:S(2)}, u32[]{:S(2)}) collective-permute-start(f32[72,128]{1,0:T(8,128)S(1)} %add.28), channel_id=1, source_target_pairs={{0,16},{1,17},{2,18},{3,19},{4,20},{5,21},{6,22},{7,23},{8,24},{9,... | collective-permute-start | bytes 110600 | tf_op jit(solution)/shard_map/ppermute | solution.py:338
  46.5 4.9 %collective-permute-start.15 = (f32[72,128]{1,0:T(8,128)S(1)}, f32[72,128]{1,0:T(8,128)S(1)}, u32[]{:S(2)}, u32[]{:S(2)}) collective-permute-start(f32[72,128]{1,0:T(8,128)S(1)} %add.28), channel_id=1, source_target_pairs={{0,24},{1,25},{2,26},{3,27},{4,28},{5,29},{6,30},{7,31},{8,16},{9,... | collective-permute-start | bytes 110600 | tf_op jit(solution)/shard_map/ppermute | solution.py:338
  51.4 4.5 %collective-permute-start.16 = (f32[72,128]{1,0:T(8,128)S(1)}, f32[72,128]{1,0:T(8,128)S(1)}, u32[]{:S(2)}, u32[]{:S(2)}) collective-permute-start(f32[72,128]{1,0:T(8,128)S(1)} %add_add_fusion.refs_0_), channel_id=1, source_target_pairs={{0,2},{1,3},{2,0},{3,1},{4,6},{5,7},{6,4},{7,5},{8,10},{9,11},{10,... | collective-permute-start | bytes 110600 | tf_op jit(solution)/shard_map/ppermute | solution.py:338
  51.5 4.9 %collective-permute-start.17 = (f32[72,128]{1,0:T(8,128)S(1)}, f32[72,128]{1,0:T(8,128)S(1)}, u32[]{:S(2)}, u32[]{:S(2)}) collective-permute-start(f32[72,128]{1,0:T(8,128)S(1)} %add_add_fusion.refs_0_), channel_id=1, source_target_pairs={{0,4},{1,5},{2,6},{3,7},{4,0},{5,1},{6,2},{7,3},{8,12},{9,13},{10,... | collective-permute-start | bytes 110600 | tf_op jit(solution)/shard_map/ppermute | solution.py:338
  52.6 5.8 %collective-permute-start.18 = (f32[72,128]{1,0:T(8,128)S(1)}, f32[72,128]{1,0:T(8,128)S(1)}, u32[]{:S(2)}, u32[]{:S(2)}) collective-permute-start(f32[72,128]{1,0:T(8,128)S(1)} %add_add_fusion.refs_0_), channel_id=1, source_target_pairs={{0,6},{1,7},{2,4},{3,5},{4,2},{5,3},{6,0},{7,1},{8,14},{9,15},{10,... | collective-permute-start | bytes 110600 | tf_op jit(solution)/shard_map/ppermute | solution.py:338
